TPU v7x, 32 devices: a whole 2x2x4 slice. The times are simulated.
32 devices in a mesh: rows: 8 (over z, y), head: 4 (over x, core).
Axes of the slice: x: 2, y: 2, z: 4, core: 2. Of those that a mesh axis runs over, the one named last changes fastest.
Arguments:
- tokens: bfloat16 [2, 4096, 512], P(None, 'rows'), may hold values from -6 to 6
- cotangent: bfloat16 [2, 4096, 512], P(None, 'rows'), may hold values from -6 to 6
- dataset_ids: int32 [2, 4096], P(None, 'rows'), may hold values from 0 to 15, never falling along the last dimension, each value on 1 to 2048 neighbouring positions
- prompt_map: int32 [2, 16], replicated, may hold values from 0 to 7
- attn_in: bfloat16 [3, 512, 512], P(None, None, 'head'), may hold values from -0.25 to 0.25
- attn_out: bfloat16 [512, 512], P('head'), may hold values from -6 to 6
- up_weight: bfloat16 [512, 1024], P(None, 'head'), may hold values from -0.25 to 0.25
- up_bias: float32 [1024], P('head'), may hold values from -4 to 4
- down_weight: bfloat16 [1024, 512], P('head'), may hold values from -0.1875 to 0.1875
- down_bias: float32 [512], replicated, may hold values from -4 to 4
- norm_gains: float32 [2, 512], replicated, may hold values from 0.5 to 1.5
- norm_shifts: float32 [2, 512], replicated, may hold values from -4 to 4
- prompts: float32 [8000, 512], P('rows'), may hold values from -6 to 6
- moment_one: float32 [8000, 512], P('rows'), may hold values from -0.0008544922 to 0.0008544922
- moment_two: float32 [8000, 512], P('rows'), may hold values from 1.2207031e-10 to 1.953125e-09
- step_count: int32 [], replicated, may hold values from 1 to 20
Outputs:
- layer_out: float32 [2, 4096, 512], P(None, 'rows')
- input_grad: float32 [2, 4096, 512], P(None, 'rows')
- clipped_grad: float32 [8000, 512], P('rows')
- grad_norm: float32 [], replicated
- new_moment_one: float32 [8000, 512], P('rows')
- new_moment_two: float32 [8000, 512], P('rows')
- new_prompts: float32 [8000, 512], P('rows')
Inputs may be any that keep to these rules, and one draw needn't show every extreme that they name: `dataset_ids`: within a micro-batch dataset numbers never fall along the tokens; each dataset holds 1 to 2048 tokens, one exactly 2048.
All inputs are finite; a program needn't handle non-finite values.
Results may differ from a plain program's by a relative error of at most 0.023.
Values may be sent and summed in bfloat16 or wider, within the bound.
No kernel may reach another device: no remote copies, remote signals or barrier semaphores. Data moves between devices by JAX's collectives and lax.ppermute only.
A program may use at most 320 MiB of HBM per device.

v0:
```python
import functools

import jax
import jax.numpy as jnp
from jax import lax
from jax.experimental import pallas as pl
from jax.experimental.pallas import tpu as pltpu
from jax.sharding import PartitionSpec as P

PLEN = 1000
NEGATIVE = -1e30
BETA_ONE = 0.9
BETA_TWO = 0.999
LEARNING_RATE = 0.5
DECAY_RATE = 0.01
EPSILON = 1e-08
CLIP_NORM = 1.0
LOG2E = 1.4426950408889634
PACK = 16
STATS = 32
VMEM_LIMIT = 60 * 1024 * 1024
BF = jnp.bfloat16
F32 = jnp.float32
BOTH = ("rows", "head")


def params(operand_bytes):
    return pltpu.CompilerParams(vmem_limit_bytes=min(VMEM_LIMIT, operand_bytes + (20 << 20)))


def cost(flops, bytes_accessed, transcendentals=0):
    return pl.CostEstimate(
        flops=int(flops), bytes_accessed=int(bytes_accessed), transcendentals=int(transcendentals)
    )


def mm(a, b):
    return lax.dot_general(a, b, (((1,), (0,)), ((), ())), preferred_element_type=F32)


def mm_nt(a, b):
    return lax.dot_general(a, b, (((1,), (1,)), ((), ())), preferred_element_type=F32)


def split3(value):
    high = value.astype(BF)
    rest = value - high.astype(F32)
    mid = rest.astype(BF)
    low = (rest - mid.astype(F32)).astype(BF)
    return high, mid, low


def bit_orders(row_count):
    bits = row_count.bit_length() - 1
    return ([0] + list(range(bits - 1, 0, -1)), list(range(bits - 1, 0, -1)) + [0])


def slot_of(offset, parity, row_count):
    order_even, order_odd = bit_orders(row_count)

    def mapped(order):
        total = 0
        for place, bit in enumerate(order):
            total = total + (((offset >> bit) & 1) << place)
        return total

    return jnp.where(parity == 0, mapped(order_even), mapped(order_odd))


def gather_rows(block, row_count, head_count):
    order_even, order_odd = bit_orders(row_count)
    held = block[None]
    for place, (even_bit, odd_bit) in enumerate(zip(order_even, order_odd)):
        pairs = []
        for row in range(row_count):
            for head in range(head_count):
                bit = even_bit if head % 2 == 0 else odd_bit
                pairs.append((row * head_count + head, (row ^ (1 << bit)) * head_count + head))
        other = lax.ppermute(held, BOTH, pairs)
        if place < len(order_even) - 1:
            held = jnp.concatenate([held, other], axis=0)
    return held, other


def swap_head(value, mask, head_count):
    return lax.ppermute(value, "head", [(i, i ^ mask) for i in range(head_count)])


def smem():
    return pl.BlockSpec(memory_space=pltpu.SMEM)


def vmem():
    return pl.BlockSpec(memory_space=pltpu.VMEM)


def anywhere():
    return pl.BlockSpec(memory_space=pl.ANY)


def join_weights(meta, own, other, target, first):
    dim = own.shape[2]
    for kind in range(first, own.shape[0]):
        for place in range(2):
            column = ((kind - first) * 2 + place) * dim
            target[:, column : column + dim] = jnp.where(meta[1] == place, own[kind], other[kind])


def wide(value, count):
    return jnp.concatenate([value] * count, axis=1)


def column_of(line):
    return jnp.transpose(jnp.broadcast_to(line, (128, line.shape[1])))


def project_query_kernel(meta, a, b, c, d, own, other, q_out):
    half = a.shape[1] - PACK
    dim = own.shape[2]
    weights = jnp.concatenate(
        [jnp.where(meta[1] == place, own[0], other[0]) for place in range(2)], axis=1
    )
    for high, pair in enumerate(((a, b), (c, d))):
        for place, ref in enumerate(pair):
            q_out[high, 0, place] = mm(ref[0, :half], weights).astype(BF)


def project_query(meta, mine, theirs, in_own, in_other):
    slots, rows, width = mine[0].shape
    half = rows - PACK
    dim = in_own.shape[2]
    block = pl.BlockSpec((1, rows, width), lambda g: (g, 0, 0))
    whole = pl.BlockSpec((1,) + in_own.shape[1:], lambda g: (0, 0, 0))
    out = pl.pallas_call(
        project_query_kernel,
        out_shape=jax.ShapeDtypeStruct((2, slots, 2, half, 2 * dim), BF),
        grid=(slots,),
        in_specs=[smem()] + [block] * 4 + [whole] * 2,
        out_specs=pl.BlockSpec((2, 1, 2, half, 2 * dim), lambda g: (0, g, 0, 0, 0)),
        compiler_params=params(8 << 20),
        cost_estimate=cost(8 * slots * half * width * 2 * dim, 8 * slots * half * width),
        name="project_query",
    )(meta, mine[0], theirs[0], mine[1], theirs[1], in_own, in_other)
    return out.reshape(4 * slots, half, 2 * dim)


def key_range(starts, low, high, data_count):
    first = jnp.int32(1 << 30)
    last = jnp.int32(0)
    for data in range(data_count):
        begin, end = starts[data], starts[data + 1]
        hit = (begin < high) & (end > low) & (begin < end)
        first = jnp.where(hit, jnp.minimum(first, begin), first)
        last = jnp.where(hit, jnp.maximum(last, end), last)
    return first, last


def load_shard(meta, shard, gathered, x_ref, line_ref):
    mine_low, theirs_low, mine_high, theirs_high = gathered
    slots, half = mine_low.shape[0], mine_low.shape[1] - PACK
    parity = meta[2]
    for place, (low, high) in enumerate(((mine_low, mine_high), (theirs_low, theirs_high))):
        slot = slot_of(shard ^ meta[0], parity ^ place, 2 * slots)
        for bank, ref in enumerate((low, high)):

            @pl.when((slot < slots) if bank == 0 else (slot >= slots))
            def _():
                x_ref[place * half : (place + 1) * half, :] = ref[slot - bank * slots, :half, :]
                if place == 0:
                    line_ref[...] = ref[slot - bank * slots, half : half + 1, :].astype(F32)

    line = line_ref[...]
    first, second = line[:, :half], line[:, half : 2 * half]
    return jnp.concatenate(
        [jnp.where(parity == 0, first, second), jnp.where(parity == 0, second, first)], axis=1
    )


def online(scores, factor, mask, m_ref, head, rows):
    old_max = m_ref[head, rows, :]
    size = old_max.shape[0]
    top = jnp.broadcast_to(jnp.max(scores, axis=1, keepdims=True) * factor, (size, 128))
    new_max = jnp.maximum(old_max, top)
    shift = new_max
    if mask is not None:
        new_max = jnp.where(mask, new_max, old_max)
        shift = jnp.where(mask, new_max, -NEGATIVE)
    m_ref[head, rows, :] = new_max
    probs = jnp.exp2(scores * factor - wide(shift, scores.shape[1] // 128))
    return probs.astype(BF), jnp.exp2(old_max - new_max)


def accumulate(acc_ref, head, rows, alpha, probs, value):
    with_ones = jnp.concatenate([value, jnp.ones((value.shape[0], 128), BF)], axis=1)
    acc_ref[head, rows, :] = acc_ref[head, rows, :] * wide(
        alpha, with_ones.shape[1] // 128
    ) + mm(probs, with_ones)


def token_forward_kernel(
    data_count,
    factor,
    meta,
    starts,
    tok_ref,
    ids_ref,
    mine_low,
    theirs_low,
    mine_high,
    theirs_high,
    in_own,
    in_other,
    q_ref,
    m_ref,
    acc_ref,
    w_ref,
    x_ref,
    line_ref,
    id_ref,
):
    size, dim = tok_ref.shape[1], in_own.shape[2]
    base = meta[0] * size
    first, last = key_range(starts, base, base + size, data_count)
    join_weights(meta, in_own, in_other, w_ref, 0)
    q_ref[...] = mm(tok_ref[meta[1]], w_ref[:, : 2 * dim]).astype(BF)
    m_ref[...] = jnp.full(m_ref.shape, NEGATIVE, F32)
    acc_ref[...] = jnp.zeros(acc_ref.shape, F32)
    id_ref[...] = column_of(ids_ref[...])
    rows = pl.ds(0, size)

    def step(shard, carry):
        line = load_shard(
            meta, shard, (mine_low, theirs_low, mine_high, theirs_high), x_ref, line_ref
        )
        kv = mm(x_ref[...], w_ref[:, 2 * dim :]).astype(BF)
        mask = wide(id_ref[...], size // 128) == line
        raw = [
            mm_nt(q_ref[:, h * dim : (h + 1) * dim], kv[:, h * dim : (h + 1) * dim])
            for h in range(2)
        ]
        parts = [
            online(jnp.where(mask, raw[h], NEGATIVE), factor, None, m_ref, h, rows)
            for h in range(2)
        ]
        for h in range(2):
            value = kv[:, (2 + h) * dim : (3 + h) * dim]
            accumulate(acc_ref, h, rows, parts[h][1], parts[h][0], value)
        return carry

    lax.fori_loop(first // size, (last + size - 1) // size, step, 0)


def token_forward(meta, starts, tokens, ids_row, mine, theirs, in_own, in_other, factor, data_count):
    size, width = tokens.shape[1:]
    dim = in_own.shape[2]
    return pl.pallas_call(
        functools.partial(token_forward_kernel, data_count, factor),
        out_shape=(
            jax.ShapeDtypeStruct((size, 2 * dim), BF),
            jax.ShapeDtypeStruct((2, size, 128), F32),
            jax.ShapeDtypeStruct((2, size, dim + 128), F32),
        ),
        in_specs=[smem(), smem()] + [vmem()] * 8,
        out_specs=[vmem()] * 3,
        scratch_shapes=[
            pltpu.VMEM((width, 6 * dim), BF),
            pltpu.VMEM((size, width), BF),
            pltpu.VMEM((1, width), F32),
            pltpu.VMEM((size, 128), F32),
        ],
        compiler_params=params(4 * mine[0].size * 2),
        cost_estimate=cost(4e9, 8e6, 2e6),
        name="token_forward",
    )(meta, starts, tokens, ids_row, mine[0], theirs[0], mine[1], theirs[1], in_own, in_other)


def fetch_prompts(data_count, starts, table, base, size, prompt_hbm, raw_ref, state, sem):
    pieces = raw_ref.shape[1]
    for number in range(raw_ref.shape[0]):
        used = jnp.int32(0)
        for data in range(data_count):
            begin, end = starts[data], starts[data + 1]
            hit = (begin < base + size) & (end > base) & (begin < end) & (table[data] == number)
            used = jnp.where(hit, 1, used)
        state[number] = used

        @pl.when(used == 1)
        def _():
            pltpu.make_async_copy(
                prompt_hbm.at[pl.ds(number * pieces, pieces)], raw_ref.at[number], sem.at[number]
            ).start()


def project_prompt(number, prompt_hbm, raw_ref, w_ref, kv_ref, state, sem):
    pieces, head_count, block, _ = raw_ref.shape[1:]

    @pl.when(state[number] == 1)
    def _():
        pltpu.make_async_copy(
            prompt_hbm.at[pl.ds(number * pieces, pieces)], raw_ref.at[number], sem.at[number]
        ).wait()
        for piece in range(pieces):
            rows = jnp.concatenate([raw_ref[number, piece, h] for h in range(head_count)], axis=1)
            kv_ref[number, pl.ds(piece * block, block), :] = mm(rows, w_ref[...]).astype(BF)
        kv_ref[number, PLEN:, :] = jnp.zeros((kv_ref.shape[1] - PLEN, kv_ref.shape[2]), BF)
        state[number] = 2


def prompt_mask(scores):
    lanes = lax.broadcasted_iota(jnp.int32, (scores.shape[0], 128), 1)
    edge = scores.shape[1] - 128
    tail = jnp.where(lanes < PLEN - edge, scores[:, edge:], NEGATIVE)
    return jnp.concatenate([scores[:, :edge], tail], axis=1)


def visit_prompts(data_count, starts, table, base, size, prepare, update):
    def visit(data, carry):
        begin, end = starts[data], starts[data + 1]

        @pl.when((begin < base + size) & (end > base) & (begin < end))
        def _():
            number = table[data]
            prepare(number)
            low = (jnp.maximum(begin, base) - base) // 128
            count = (jnp.minimum(end, base + size) - base + 127) // 128 - low
            for case in range(1, size // 128 + 1):

                @pl.when(count == case)
                def _():
                    update(pl.ds(pl.multiple_of(low * 128, 128), case * 128), data, number)

        return carry

    lax.fori_loop(0, data_count, visit, 0)


def prompt_forward_kernel(
    data_count,
    factor,
    meta,
    starts,
    table,
    q_ref,
    ids_ref,
    m_in,
    acc_in,
    prompt_hbm,
    in_own,
    in_other,
    o_ref,
    wide_ref,
    lse_ref,
    m_ref,
    acc_ref,
    raw_ref,
    w_ref,
    kv_ref,
    id_ref,
    state,
    sem,
):
    size, dim = q_ref.shape[0], q_ref.shape[1] // 2
    base = meta[0] * size
    fetch_prompts(data_count, starts, table, base, size, prompt_hbm, raw_ref, state, sem)
    join_weights(meta, in_own, in_other, w_ref, 1)
    m_ref[...] = m_in[...]
    acc_ref[...] = acc_in[...]
    id_ref[...] = column_of(ids_ref[...])

    def prepare(number):
        project_prompt(number, prompt_hbm, raw_ref, w_ref, kv_ref, state, sem)

    def update(rows, data, number):
        mask = id_ref[rows, :] == data.astype(F32)
        raw = [
            mm_nt(q_ref[rows, pl.ds(h * dim, dim)], kv_ref[number, :, pl.ds(h * dim, dim)])
            for h in range(2)
        ]
        parts = [online(prompt_mask(raw[h]), factor, mask, m_ref, h, rows) for h in range(2)]
        for h in range(2):
            value = kv_ref[number, :, pl.ds((2 + h) * dim, dim)]
            accumulate(acc_ref, h, rows, parts[h][1], parts[h][0], value)

    visit_prompts(data_count, starts, table, base, size, prepare, update)
    for head in range(2):
        cols = pl.ds(head * dim, dim)
        total = acc_ref[head, :, dim:]
        attended = acc_ref[head, :, :dim] / total
        wide_ref[:, cols] = attended
        o_ref[:, cols] = attended.astype(BF)
        lse_ref[head] = m_ref[head] + jnp.log2(total)


def prompt_scratch(prompt_all, width, dim):
    shards, head_count, block, column = prompt_all.shape
    pieces = PLEN // block
    count = shards // pieces
    return [
        pltpu.VMEM((count, pieces, head_count, block, column), BF),
        pltpu.VMEM((width, 4 * dim), BF),
        pltpu.VMEM((count, -(-PLEN // 128) * 128, 4 * dim), BF),
    ], [pltpu.SMEM((count,), jnp.int32), pltpu.SemaphoreType.DMA((count,))]


def prompt_forward(
    meta, starts, table, q_own, ids_row, state, prompt_all, in_own, in_other, factor, data_count
):
    size, dim = q_own.shape[0], q_own.shape[1] // 2
    buffers, flags = prompt_scratch(prompt_all, in_own.shape[1], dim)
    return pl.pallas_call(
        functools.partial(prompt_forward_kernel, data_count, factor),
        out_shape=(
            jax.ShapeDtypeStruct((size, 2 * dim), BF),
            jax.ShapeDtypeStruct((size, 2 * dim), F32),
            jax.ShapeDtypeStruct((2, size, 128), F32),
        ),
        in_specs=[smem()] * 3 + [vmem()] * 4 + [anywhere()] + [vmem()] * 2,
        out_specs=[vmem()] * 3,
        scratch_shapes=[
            pltpu.VMEM(state[0].shape, F32),
            pltpu.VMEM(state[1].shape, F32),
            *buffers,
            pltpu.VMEM((size, 128), F32),
            *flags,
        ],
        compiler_params=params(20 << 20),
        cost_estimate=cost(4e9, 8e6, 2e6),
        name="prompt_forward",
    )(meta, starts, table, q_own, ids_row, *state, prompt_all, in_own, in_other)


def norm_parts(value):
    center = value - jnp.mean(value, axis=-1, keepdims=True)
    scale = lax.rsqrt(jnp.mean(center * center, axis=-1, keepdims=True) + 1e-05)
    return center * scale, scale


def norm_back(grad, unit, scale, gain):
    part = grad * gain
    return scale * (
        part
        - jnp.mean(part, axis=-1, keepdims=True)
        - unit * jnp.mean(part * unit, axis=-1, keepdims=True)
    )


def feed_kernel(
    meta,
    mine,
    theirs,
    wide_ref,
    lse_ref,
    tok_ref,
    cot_ref,
    w_ref,
    down_bias,
    gains,
    shifts,
    out_ref,
    da_ref,
    pack_ref,
    delta_ref,
):
    size, width = tok_ref.shape[1:]
    dim = mine.shape[1] // 2
    heads = w_ref.shape[0]
    hid = (w_ref.shape[1] - PACK - dim) // 2
    batch, parity = meta[1], meta[2]
    even = parity == 0
    spot = [((q % 2) ^ parity) * 2 + ((q // 2) ^ batch) for q in range(heads)]
    place_out = slice(hid, hid + dim)
    place_up = slice(hid + dim, 2 * hid + dim)
    place_bias = 2 * hid + dim
    sub = min(256, size)
    rows_per = size // (2 * dim)
    pack_ref[pl.ds(size, STATS), :] = jnp.zeros((STATS, 2 * dim), BF)
    g0, g1 = gains[0:1, :], gains[1:2, :]
    for part in range(size // sub):
        rows = pl.ds(part * sub, sub)
        a, b = mine[rows, :], theirs[rows, :]
        first = jnp.where(even, a, b)
        second = jnp.where(even, b, a)
        attn = mm(first[:, :dim], w_ref[spot[0], place_out, :])
        attn += mm(second[:, :dim], w_ref[spot[1], place_out, :])
        attn += mm(first[:, dim:], w_ref[spot[2], place_out, :])
        attn += mm(second[:, dim:], w_ref[spot[3], place_out, :])
        unit_one, scale_one = norm_parts(tok_ref[batch, rows, :].astype(F32) + attn)
        normed = unit_one * g0 + shifts[0:1, :]
        normed_low = normed.astype(BF)
        branch = down_bias[...]
        slopes = []
        for q in range(heads):
            bias = (
                w_ref[spot[q], place_bias : place_bias + 1, :hid].astype(F32)
                + w_ref[spot[q], place_bias : place_bias + 1, hid : 2 * hid].astype(F32)
                + w_ref[spot[q], place_bias + 1 : place_bias + 2, :hid].astype(F32)
            )
            pre = mm_nt(normed_low, w_ref[spot[q], place_up, :]) + bias
            cdf = 0.5 * (1.0 + lax.erf(pre * 0.7071067811865476))
            slopes.append(cdf + pre * (jnp.exp(-0.5 * pre * pre) * 0.3989422804014327))
            branch = branch + mm((pre * cdf).astype(BF), w_ref[spot[q], :hid, :])
        unit_two, scale_two = norm_parts(normed + branch)
        out_ref[rows, :] = unit_two * g1 + shifts[1:2, :]
        grad_mixed = norm_back(cot_ref[batch, rows, :].astype(F32), unit_two, scale_two, g1)
        mixed_low = grad_mixed.astype(BF)
        grad_normed = grad_mixed
        for q in range(heads):
            grad_pre = mm_nt(mixed_low, w_ref[spot[q], :hid, :]) * slopes[q]
            grad_normed = grad_normed + mm(grad_pre.astype(BF), w_ref[spot[q], place_up, :])
        grad_sum = norm_back(grad_normed, unit_one, scale_one, g0)
        da_ref[rows, :] = grad_sum
        sum_low = grad_sum.astype(BF)
        for head in range(2):
            cols = pl.ds(head * dim, dim)
            grad_out = mm_nt(sum_low, w_ref[head ^ batch, place_out, :]).astype(BF)
            pack_ref[rows, cols] = grad_out
            delta = jnp.sum(grad_out.astype(F32) * wide_ref[rows, cols], axis=1, keepdims=True)
            delta_ref[head, rows, :] = jnp.broadcast_to(delta, (sub, 128))
    for head in range(2):
        for kind, ref in enumerate((lse_ref, delta_ref)):
            for place, term in enumerate(split3(jnp.transpose(ref[head])[0:1, :])):
                for i in range(rows_per):
                    row = size + ((head * 2 + kind) * 3 + place) * rows_per + i
                    pack_ref[row : row + 1, :] = term[:, i * 2 * dim : (i + 1) * 2 * dim]


def feed(meta, mine, theirs, wide_out, lse, tokens, cotangent, w, down_bias, gains, shifts):
    size, width = tokens.shape[1:]
    dim = mine.shape[1] // 2
    return pl.pallas_call(
        feed_kernel,
        out_shape=(
            jax.ShapeDtypeStruct((size, width), F32),
            jax.ShapeDtypeStruct((size, width), F32),
            jax.ShapeDtypeStruct((size + STATS, 2 * dim), BF),
            jax.ShapeDtypeStruct((2, size, 128), F32),
        ),
        in_specs=[smem()] + [vmem()] * 10,
        out_specs=[vmem()] * 4,
        compiler_params=params(10 << 20),
        cost_estimate=cost(3e9, 8e6, 1e6),
        name="feed",
    )(meta, mine, theirs, wide_out, lse, tokens, cotangent, w, down_bias, gains, shifts)


def query_grad_kernel(
    data_count,
    factor,
    meta,
    starts,
    table,
    q_ref,
    ids_ref,
    lse_ref,
    delta_ref,
    do_ref,
    mine_low,
    theirs_low,
    mine_high,
    theirs_high,
    in_own,
    in_other,
    prompt_hbm,
    dq_ref,
    acc_ref,
    x_ref,
    line_ref,
    raw_ref,
    w_ref,
    kv_ref,
    id_ref,
    state,
    sem,
):
    size, dim = q_ref.shape[0], q_ref.shape[1] // 2
    base = meta[0] * size
    fetch_prompts(data_count, starts, table, base, size, prompt_hbm, raw_ref, state, sem)
    join_weights(meta, in_own, in_other, w_ref, 1)
    first, last = key_range(starts, base, base + size, data_count)
    acc_ref[...] = jnp.zeros(acc_ref.shape, F32)
    id_ref[...] = column_of(ids_ref[...])

    def low_grads(h, rows, scores, shift, grads):
        count = scores.shape[1] // 128
        probs = jnp.exp2(scores * factor - wide(shift, count))
        return (probs * (grads - wide(delta_ref[h, rows, :], count))).astype(BF)

    def step(shard, carry):
        line = load_shard(
            meta, shard, (mine_low, theirs_low, mine_high, theirs_high), x_ref, line_ref
        )
        kv = mm(x_ref[...], w_ref[...]).astype(BF)
        mask = wide(id_ref[...], size // 128) == line
        rows = pl.ds(0, size)
        raw, grads, low = [], [], []
        for h in range(2):
            raw.append(mm_nt(q_ref[:, h * dim : (h + 1) * dim], kv[:, h * dim : (h + 1) * dim]))
            grads.append(
                mm_nt(
                    do_ref[pl.ds(0, size), h * dim : (h + 1) * dim],
                    kv[:, (2 + h) * dim : (3 + h) * dim],
                )
            )
        for h in range(2):
            low.append(
                low_grads(h, rows, jnp.where(mask, raw[h], NEGATIVE), lse_ref[h], grads[h])
            )
        for h in range(2):
            acc_ref[h] += mm(low[h], kv[:, h * dim : (h + 1) * dim])
        return carry

    lax.fori_loop(first // size, (last + size - 1) // size, step, 0)

    def prepare(number):
        project_prompt(number, prompt_hbm, raw_ref, w_ref, kv_ref, state, sem)

    def update(rows, data, number):
        mask = id_ref[rows, :] == data.astype(F32)
        raw, grads, low = [], [], []
        for h in range(2):
            cols = pl.ds(h * dim, dim)
            raw.append(mm_nt(q_ref[rows, cols], kv_ref[number, :, cols]))
            grads.append(mm_nt(do_ref[rows, cols], kv_ref[number, :, pl.ds((2 + h) * dim, dim)]))
        for h in range(2):
            shift = jnp.where(mask, lse_ref[h, rows, :], -NEGATIVE)
            low.append(low_grads(h, rows, prompt_mask(raw[h]), shift, grads[h]))
        for h in range(2):
            acc_ref[h, rows, :] += mm(low[h], kv_ref[number, :, pl.ds(h * dim, dim)])

    visit_prompts(data_count, starts, table, base, size, prepare, update)
    for head in range(2):
        dq_ref[:, pl.ds(head * dim, dim)] = (acc_ref[head] * dim ** (-0.5)).astype(BF)


def query_grad(
    meta,
    starts,
    table,
    q_own,
    ids_row,
    lse,
    delta,
    pack,
    mine,
    theirs,
    in_own,
    in_other,
    prompt_all,
    factor,
    data_count,
):
    size, dim = q_own.shape[0], q_own.shape[1] // 2
    width = in_own.shape[1]
    buffers, flags = prompt_scratch(prompt_all, width, dim)
    return pl.pallas_call(
        functools.partial(query_grad_kernel, data_count, factor),
        out_shape=jax.ShapeDtypeStruct((size, 2 * dim), BF),
        in_specs=[smem()] * 3 + [vmem()] * 11 + [anywhere()],
        out_specs=vmem(),
        scratch_shapes=[
            pltpu.VMEM((2, size, dim), F32),
            pltpu.VMEM((size, width), BF),
            pltpu.VMEM((1, width), F32),
            *buffers,
            pltpu.VMEM((size, 128), F32),
            *flags,
        ],
        compiler_params=params((16 << 20) + 4 * mine[0].size * 2),
        cost_estimate=cost(6e9, 16e6, 4e6),
        name="query_grad",
    )(
        meta,
        starts,
        table,
        q_own,
        ids_row,
        lse,
        delta,
        pack,
        mine[0],
        theirs[0],
        mine[1],
        theirs[1],
        in_own,
        in_other,
        prompt_all,
    )


def half_shard(meta, index, q_ref, ids_ref, low_ref, high_ref):
    slots, rows, double = low_ref.shape
    half = q_ref.shape[1]
    size = rows - STATS
    shard, part = index // 2, index % 2
    slot = slot_of(shard ^ meta[0], meta[2], 2 * slots)
    other = slot_of(shard ^ meta[0], 1 - meta[2], 2 * slots)
    query = q_ref[jnp.where(part == meta[2], slot * 2, other * 2 + 1)]
    in_low = slot < slots
    place_low, place_high = jnp.minimum(slot, slots - 1), jnp.maximum(slot - slots, 0)
    span = pl.ds(pl.multiple_of(part * half, half), half)
    grad = jnp.where(in_low, low_ref[place_low, span, :], high_ref[place_high, span, :])
    line = ids_ref[slot]
    line = jnp.where(part == 0, line[:, :half], line[:, half : 2 * half])
    tail = pl.ds(size, STATS)
    stats = jnp.where(in_low, low_ref[place_low, tail, :], high_ref[place_high, tail, :])
    stats = stats.astype(F32)
    rows_per = size // double

    def stat(head, kind):
        total = 0.0
        for place in range(3):
            row = ((head * 2 + kind) * 3 + place) * rows_per
            term = stats[row : row + 1, :]
            for i in range(1, rows_per):
                term = jnp.where(part == i, stats[row + i : row + i + 1, :], term)
            total = total + term
        return total

    return query, grad, line, stat


def key_update(query, grad, kv_ref, mask, rows_mask, stat, factor, dk_ref, dv_ref):
    dim = query.shape[1] // 2
    cols = [slice(h * dim, (h + 1) * dim) for h in range(2)]
    raw = [mm_nt(kv_ref[:, cols[h]], query[:, cols[h]]) for h in range(2)]
    grads = [mm_nt(kv_ref[:, pl.ds((2 + h) * dim, dim)], grad[:, cols[h]]) for h in range(2)]
    probs, low = [], []
    for h in range(2):
        shift = stat(h, 0)
        scores = raw[h]
        if rows_mask is None:
            shift = jnp.where(mask, shift, -NEGATIVE)
        else:
            scores = jnp.where(rows_mask, scores, NEGATIVE)
        p = jnp.exp2(scores * factor - shift)
        probs.append(p.astype(BF))
        low.append((p * (grads[h] - stat(h, 1))).astype(BF))
    for h in range(2):
        dv_ref[:, cols[h]] += mm(probs[h], grad[:, cols[h]])
        dk_ref[:, cols[h]] += mm(low[h], query[:, cols[h]])


def prompt_grad_kernel(
    data_count,
    factor,
    meta,
    starts,
    table,
    q_ref,
    ids_ref,
    low_ref,
    high_ref,
    own_ref,
    in_own,
    in_other,
    keep_ref,
    send_ref,
    dk_ref,
    dv_ref,
    w_ref,
    kv_ref,
):
    half = q_ref.shape[1]
    block, width = own_ref.shape
    dim = in_own.shape[2]
    number = meta[0] * block // PLEN
    dk_ref[...] = jnp.zeros(dk_ref.shape, F32)
    dv_ref[...] = jnp.zeros(dv_ref.shape, F32)
    join_weights(meta, in_own, in_other, w_ref, 1)
    kv_ref[...] = mm(own_ref[...], w_ref[...]).astype(BF)

    def visit(data, carry):
        begin, end = starts[data], starts[data + 1]

        @pl.when((table[data] == number) & (begin < end))
        def _():
            def step(index, inner):
                query, grad, line, stat = half_shard(meta, index, q_ref, ids_ref, low_ref, high_ref)
                key_update(
                    query, grad, kv_ref, line == data.astype(F32), None, stat, factor, dk_ref, dv_ref
                )
                return inner

            lax.fori_loop(begin // half, (end + half - 1) // half, step, 0)

        return carry

    lax.fori_loop(0, data_count, visit, 0)
    grads = jnp.concatenate(
        [(dk_ref[...] * dim ** (-0.5)).astype(BF), dv_ref[...].astype(BF)], axis=1
    )
    split = width // 2
    parity = meta[2]
    send = w_ref[pl.ds(pl.multiple_of((1 - parity) * split, split), split), :]
    keep = w_ref[pl.ds(pl.multiple_of(parity * split, split), split), :]
    send_ref[...] = mm_nt(grads, send).astype(BF)
    keep_ref[...] = mm_nt(grads, keep)


def prompt_grad(meta, starts, table, q_all, ids_all, packs, own, in_own, in_other, factor, data_count):
    block, width = own.shape
    dim = in_own.shape[2]
    return pl.pallas_call(
        functools.partial(prompt_grad_kernel, data_count, factor),
        out_shape=(
            jax.ShapeDtypeStruct((block, width // 2), F32),
            jax.ShapeDtypeStruct((block, width // 2), BF),
        ),
        in_specs=[smem()] * 3 + [vmem()] * 7,
        out_specs=[vmem(), vmem()],
        scratch_shapes=[
            pltpu.VMEM((block, 2 * dim), F32),
            pltpu.VMEM((block, 2 * dim), F32),
            pltpu.VMEM((width, 4 * dim), BF),
            pltpu.VMEM((block, 4 * dim), BF),
        ],
        compiler_params=params(q_all.size * 2 + packs[0].size * 4),
        cost_estimate=cost(6e9, 16e6, 4e6),
        name="prompt_grad",
    )(meta, starts, table, q_all, ids_all, *packs, own, in_own, in_other)


def token_grad_kernel(
    data_count,
    factor,
    meta,
    starts,
    q_ref,
    ids_ref,
    low_ref,
    high_ref,
    tok_ref,
    own_ids,
    dq_ref,
    in_own,
    in_other,
    out_ref,
    dk_ref,
    dv_ref,
    w_ref,
    kv_ref,
    id_ref,
):
    size = tok_ref.shape[1]
    half = q_ref.shape[1]
    dim = in_own.shape[2]
    base = meta[0] * size
    first, last = key_range(starts, base, base + size, data_count)
    dk_ref[...] = jnp.zeros(dk_ref.shape, F32)
    dv_ref[...] = jnp.zeros(dv_ref.shape, F32)
    join_weights(meta, in_own, in_other, w_ref, 0)
    kv_ref[...] = mm(tok_ref[meta[1]], w_ref[:, 2 * dim :]).astype(BF)
    id_ref[...] = column_of(own_ids[...])

    def step(index, carry):
        query, grad, line, stat = half_shard(meta, index, q_ref, ids_ref, low_ref, high_ref)
        mask = wide(id_ref[...], half // 128) == line
        key_update(query, grad, kv_ref, None, mask, stat, factor, dk_ref, dv_ref)
        return carry

    lax.fori_loop(first // half, (last + half - 1) // half, step, 0)
    grads = jnp.concatenate(
        [dq_ref[...], (dk_ref[...] * dim ** (-0.5)).astype(BF), dv_ref[...].astype(BF)], axis=1
    )
    out_ref[...] = mm_nt(grads, w_ref[...]).astype(BF)


def token_grad(
    meta, starts, q_all, ids_all, packs, tokens, ids_row, dq, in_own, in_other, factor, data_count
):
    size, width = tokens.shape[1:]
    dim = in_own.shape[2]
    return pl.pallas_call(
        functools.partial(token_grad_kernel, data_count, factor),
        out_shape=jax.ShapeDtypeStruct((size, width), BF),
        in_specs=[smem()] * 2 + [vmem()] * 9,
        out_specs=vmem(),
        scratch_shapes=[
            pltpu.VMEM((size, 2 * dim), F32),
            pltpu.VMEM((size, 2 * dim), F32),
            pltpu.VMEM((width, 6 * dim), BF),
            pltpu.VMEM((size, 4 * dim), BF),
            pltpu.VMEM((size, 128), F32),
        ],
        compiler_params=params(q_all.size * 2 + packs[0].size * 4),
        cost_estimate=cost(4e9, 16e6, 4e6),
        name="token_grad",
    )(meta, starts, q_all, ids_all, *packs, tokens, ids_row, dq, in_own, in_other)


def per_device(
    tokens,
    cotangent,
    dataset_ids,
    prompt_map,
    attn_in,
    attn_out,
    up_weight,
    up_bias,
    down_weight,
    down_bias,
    norm_gains,
    norm_shifts,
    prompts,
    moment_one,
    moment_two,
    step_count,
):
    size, width = tokens.shape[1:]
    dim = attn_in.shape[2]
    hid = up_weight.shape[1]
    data_count = prompt_map.shape[1]
    row_count = lax.axis_size("rows")
    head_count = lax.axis_size("head")
    factor = dim ** (-0.5) * LOG2E
    row = lax.axis_index("rows")
    head = lax.axis_index("head")
    batch, parity = head // 2, head % 2
    half = size // 2
    meta = jnp.stack([row, batch, parity]).astype(jnp.int32)

    ids = jnp.where(batch == 0, dataset_ids[0], dataset_ids[1])
    table = jnp.where(batch == 0, prompt_map[0], prompt_map[1])
    ids_row = ids.astype(F32).reshape(1, size)
    tok_half = lax.dynamic_slice(tokens, (batch, parity * half, 0), (1, half, width))[0]
    id_rows = jnp.broadcast_to(ids.astype(BF)[None, :], (PACK, size))
    shard = jnp.concatenate([tok_half, id_rows], axis=0)
    prompt_low = prompts.astype(BF)
    column = width // head_count
    prompt_own = lax.dynamic_slice_in_dim(prompt_low, head * column, column, 1)
    prompt_all = lax.all_gather(prompt_own, BOTH, axis=0, tiled=False)
    prompt_all = prompt_all.reshape(row_count, head_count, prompt_own.shape[0], column)
    mine = gather_rows(shard, row_count, head_count)
    theirs = [swap_head(part, 1, head_count) for part in mine]
    in_other = swap_head(attn_in, 2, head_count)

    bias_high = lax.reduce_precision(up_bias, 8, 7)
    bias_rest = up_bias - bias_high
    bias_mid = lax.reduce_precision(bias_rest, 8, 7)
    bias_low = bias_rest - bias_mid
    bias_rows = jnp.concatenate([bias_high, bias_mid, bias_low, bias_low]).astype(BF)
    bias_rows = jnp.pad(bias_rows.reshape(-1, width), ((0, PACK - 4 * hid // width), (0, 0)))
    w_own = jnp.concatenate([down_weight, attn_out, up_weight.T, bias_rows], axis=0)
    w_pair = jnp.stack([w_own, swap_head(w_own, 2, head_count)])
    layer_weights = jnp.concatenate([w_pair, swap_head(w_pair, 1, head_count)], axis=0)

    ids_all = jnp.concatenate([part[:, half, :size] for part in mine], axis=0).astype(F32)
    numbers = jnp.arange(data_count + 1, dtype=jnp.int32).astype(F32)
    starts = jnp.sum((ids_all.reshape(1, -1) < numbers[:, None]).astype(jnp.int32), axis=1)
    ids_all = ids_all.reshape(row_count, 1, size)
    q_own, *state = token_forward(
        meta, starts, tokens, ids_row, mine, theirs, attn_in, in_other, factor, data_count
    )
    q_all = project_query(meta, mine, theirs, attn_in, in_other)
    o_mine, wide_out, lse = prompt_forward(
        meta, starts, table, q_own, ids_row, state, prompt_all, attn_in, in_other, factor, data_count
    )
    o_theirs = swap_head(o_mine, 1, head_count)
    out, grad_sum, pack, delta = feed(
        meta,
        o_mine,
        o_theirs,
        wide_out,
        lse,
        tokens,
        cotangent,
        layer_weights,
        down_bias.reshape(1, width),
        norm_gains,
        norm_shifts,
    )
    out_other = swap_head(out, 2, head_count)
    layer_out = jnp.stack(
        [jnp.where(batch == 0, out, out_other), jnp.where(batch == 0, out_other, out)]
    )

    packs = gather_rows(pack, row_count, head_count)
    dq = query_grad(
        meta,
        starts,
        table,
        q_own,
        ids_row,
        lse,
        delta,
        pack,
        mine,
        theirs,
        attn_in,
        in_other,
        prompt_all,
        factor,
        data_count,
    )
    packs, layer_out, dq = lax.optimization_barrier((packs, layer_out, dq))
    keep, send = prompt_grad(
        meta, starts, table, q_all, ids_all, packs, prompt_low, attn_in, in_other, factor, data_count
    )

    pair = keep + swap_head(send, 1, head_count).astype(F32)
    pair_low = lax.reduce_precision(pair, 8, 7).astype(BF)
    dq, pair_low = lax.optimization_barrier((dq, pair_low))
    pair_other = swap_head(pair_low, 2, head_count)
    token_part = token_grad(
        meta, starts, q_all, ids_all, packs, tokens, ids_row, dq, attn_in, in_other, factor, data_count
    )
    full_low = pair_low.astype(F32) + pair_other.astype(F32)
    full_low = lax.reduce_precision(full_low, 8, 7).astype(BF)
    squares = jnp.sum(full_low.astype(F32) ** 2).reshape(1, 1)
    squares = jnp.broadcast_to(squares, (8, 128))
    squares = squares + swap_head(squares, 1, head_count)
    mask = 1
    while mask < row_count:
        squares = squares + lax.ppermute(
            squares, "rows", [(i, i ^ mask) for i in range(row_count)]
        )
        mask = mask * 2
    grad_norm = jnp.sqrt(squares[0, 0])
    full_other = swap_head(full_low, 1, head_count)
    prompt_grads = jnp.concatenate(
        [jnp.where(parity == 0, full_low, full_other), jnp.where(parity == 0, full_other, full_low)],
        axis=1,
    ).astype(F32)
    clipped = prompt_grads * jnp.minimum(1.0, CLIP_NORM / (grad_norm + 1e-06))
    step_value = step_count.astype(F32)
    new_one = BETA_ONE * moment_one + (1.0 - BETA_ONE) * clipped
    new_two = BETA_TWO * moment_two + (1.0 - BETA_TWO) * clipped * clipped
    first_hat = new_one / (1.0 - jnp.power(BETA_ONE, step_value))
    second_hat = new_two / (1.0 - jnp.power(BETA_TWO, step_value))
    new_prompts = prompts * (1.0 - LEARNING_RATE * DECAY_RATE) - LEARNING_RATE * first_hat / (
        jnp.sqrt(second_hat) + EPSILON
    )

    core_sum = token_part.astype(F32) + swap_head(token_part, 1, head_count).astype(F32)
    total = lax.reduce_precision(grad_sum + core_sum, 8, 7).astype(BF)
    mine_half = lax.dynamic_slice_in_dim(total, parity * half, half, 0)
    other_half = swap_head(mine_half, 2, head_count)
    other_rest = swap_head(other_half, 1, head_count)
    other = jnp.concatenate(
        [
            jnp.where(parity == 0, other_half, other_rest),
            jnp.where(parity == 0, other_rest, other_half),
        ],
        axis=0,
    )
    input_grad = jnp.stack(
        [jnp.where(batch == 0, total, other), jnp.where(batch == 0, other, total)]
    ).astype(F32)
    return (layer_out, input_grad, clipped, grad_norm, new_one, new_two, new_prompts)


def solution(mesh):
    in_specs = (
        P(None, "rows", None),
        P(None, "rows", None),
        P(None, "rows"),
        P(),
        P(None, None, "head"),
        P("head", None),
        P(None, "head"),
        P("head"),
        P("head", None),
        P(),
        P(),
        P(),
        P("rows", None),
        P("rows", None),
        P("rows", None),
        P(),
    )
    out_specs = (
        P(None, "rows", None),
        P(None, "rows", None),
        P("rows", None),
        P(),
        P("rows", None),
        P("rows", None),
        P("rows", None),
    )
    return jax.shard_map(
        per_device, mesh=mesh, in_specs=in_specs, out_specs=out_specs, check_vma=False
    )
```

profile of v0, /device:TPU:0, one launch (start us, length us, event | category | flops | bytes accessed | tf_op | source)
XLA Modules:
  0.0 247.0 jit_solution(16249202386902494573)
XLA Ops:
  7.2 1.7 convert_element_type.89.own_ref
  10.8 3.0 %collective-permute-start = (bf16[1,272,512]{2,1,0:T(8,128)(2,1)S(1)}, bf16[1,272,512]{2,1,0:T(8,128)(2,1)S(1)}, u32[]{:S(2)}, u32[]{:S(2)}) collective-permute-start(bf16[1,272,512]{2,1,0:T(8,128)(2,1)S(1)} %maximum_bitcast_fusion), channel_id=1, source_target_pairs={{0,4},{1,17},{2,6},{3,19},{4,0},{5,21},{6,2},{7,23},{8,12},{9,25},... | collective-permute-start | bytes 835592 | tf_op jit(solution)/shard_map/ppermute | solution.py:79
  13.8 4.5 %collective-permute-done = bf16[1,272,512]{2,1,0:T(8,128)(2,1)S(1)} collective-permute-done((bf16[1,272,512]{2,1,0:T(8,128)(2,1)S(1)}, bf16[1,272,512]{2,1,0:T(8,128)(2,1)S(1)}, u32[]{:S(2)}, u32[]{:S(2)}) %collective-permute-start) | collective-permute-done | bytes 278560 | tf_op jit(solution)/shard_map/ppermute | solution.py:79
  18.4 3.2 %collective-permute-start.1 = (bf16[2,272,512]{2,1,0:T(8,128)(2,1)S(1)}, bf16[2,272,512]{2,1,0:T(8,128)(2,1)S(1)}, u32[]{:S(2)}, u32[]{:S(2)}) collective-permute-start(bf16[2,272,512]{2,1,0:T(8,128)(2,1)S(1)} %pad_maximum_fusion.5), channel_id=1, source_target_pairs={{0,16},{1,9},{2,18},{3,11},{4,20},{5,13},{6,22},{7,15},{8,24},{9,1... | collective-permute-start | bytes 1671176 | tf_op jit(solution)/shard_map/ppermute | solution.py:79
  21.6 18.9 %collective-permute-done.1 = bf16[2,272,512]{2,1,0:T(8,128)(2,1)S(1)} collective-permute-done((bf16[2,272,512]{2,1,0:T(8,128)(2,1)S(1)}, bf16[2,272,512]{2,1,0:T(8,128)(2,1)S(1)}, u32[]{:S(2)}, u32[]{:S(2)}) %collective-permute-start.1) | collective-permute-done | bytes 557088 | tf_op jit(solution)/shard_map/ppermute | solution.py:79
  43.9 1.6 collective-permute-start.7
  45.6 21.5 %collective-permute-done.2.mine_high.c = bf16[4,272,512]{2,1,0:T(8,128)(2,1)S(1)} collective-permute-done((bf16[4,272,512]{2,1,0:T(8,128)(2,1)S(1)}, bf16[4,272,512]{2,1,0:T(8,128)(2,1)S(1)}, u32[]{:S(2)}, u32[]{:S(2)}) %collective-permute-start.2) | collective-permute-done | bytes 1114144 | tf_op jit(solution)/shard_map/ppermute | solution.py:79
  67.1 1.8 collective-permute-start.5
  72.0 12.8 %collective-permute-done.5.in_other.other = bf16[3,512,128]{2,1,0:T(8,128)(2,1)} collective-permute-done((bf16[3,512,128]{2,1,0:T(8,128)(2,1)}, bf16[3,512,128]{2,1,0:T(8,128)(2,1)}, u32[]{:S(2)}, u32[]{:S(2)}) %collective-permute-start.5) | collective-permute-done | bytes 393248 | tf_op jit(solution)/shard_map/ppermute | solution.py:86
  87.1 5.3 %token_forward.1 = (bf16[512,256]{1,0:T(8,128)(2,1)S(1)}, f32[2,512,128]{2,1,0:T(8,128)S(1)}, f32[2,512,256]{2,1,0:T(8,128)S(1)}) custom-call(s32[3]{0:T(128)S(1)} %pad_add_fusion.meta, s32[17]{0:T(128)S(1)} %convert_reduce_fusion.starts, bf16[2,512,512]{2,1,0:T(8,128)(2,1)S(1)} %copy-done.2, f32[1,512]{1,0:T(1,128)S(1)} %get-tuple-element.49.ids_ref.own_ids, ...), custom_call_target="tpu_custom_call" | custom-call | flops 4000000000 | bytes 8000000 | tf_op jit(solution)/shard_map/token_forward/pallas_call | solution.py:256
  94.1 13.1 %all-gather.3.cloned.1.call-done = bf16[32000,128]{1,0:T(8,128)(2,1)} async-done(((bf16[1000,128]{1,0:T(8,128)(2,1)}), bf16[32000,128]{1,0:T(8,128)(2,1)}) %all-gather.3.cloned.1.call-update) | async-done | bytes 8192016 | tf_op jit(solution)/shard_map/all_gather | solution.py:931
  108.2 3.3 %copy-done.4 = bf16[32000,128]{1,0:T(8,128)(2,1)S(1)} copy-done((bf16[32000,128]{1,0:T(8,128)(2,1)S(1)}, bf16[32000,128]{1,0:T(8,128)(2,1)}, u32[]{:S(2)}) %copy-start.4) | copy-done | bytes 8192024
  113.8 10.7 %prompt_forward.1 = (bf16[512,256]{1,0:T(8,128)(2,1)S(1)}, f32[512,256]{1,0:T(8,128)S(1)}, f32[2,512,128]{2,1,0:T(8,128)S(1)}) custom-call(s32[3]{0:T(128)S(1)} %pad_add_fusion.meta, s32[17]{0:T(128)S(1)} %convert_reduce_fusion.starts, s32[16]{0:T(128)S(1)} %fusion.4.table, bf16[512,256]{1,0:T(8,128)(2,1)S(1)} %get-tuple-element.25.q_ref, ...), custom_call_target="tpu_custom_call" | custom-call | flops 4000000000 | bytes 8000000 | tf_op jit(solution)/shard_map/prompt_forward/pallas_call | solution.py:410
  125.0 1.8 pad_maximum_fusion.w_ref
  126.8 6.4 %feed.1 = (f32[512,512]{1,0:T(8,128)S(1)}, f32[512,512]{1,0:T(8,128)S(1)}, bf16[544,256]{1,0:T(8,128)(2,1)S(1)}, f32[2,512,128]{2,1,0:T(8,128)S(1)}) custom-call(s32[3]{0:T(128)S(1)} %pad_add_fusion.meta, bf16[512,256]{1,0:T(8,128)(2,1)S(1)} %get-tuple-element.28.mine, bf16[512,256]{1,0:T(8,128)(2,1)S(1)} %collective-permute-done.6.theirs, ...), custom_call_target="tpu_custom_call" | custom-call | flops 3000000000 | bytes 8000000 | tf_op jit(solution)/shard_map/feed/pallas_call | solution.py:530
  133.4 6.5 %collective-permute-done.9 = bf16[1,544,256]{2,1,0:T(8,128)(2,1)S(1)} collective-permute-done((bf16[1,544,256]{2,1,0:T(8,128)(2,1)S(1)}, bf16[1,544,256]{2,1,0:T(8,128)(2,1)S(1)}, u32[]{:S(2)}, u32[]{:S(2)}) %collective-permute-start.9) | collective-permute-done | bytes 278560 | tf_op jit(solution)/shard_map/ppermute | solution.py:79
  140.0 1.8 collective-permute-start.12
  141.8 11.5 %collective-permute-done.10 = bf16[2,544,256]{2,1,0:T(8,128)(2,1)S(1)} collective-permute-done((bf16[2,544,256]{2,1,0:T(8,128)(2,1)S(1)}, bf16[2,544,256]{2,1,0:T(8,128)(2,1)S(1)}, u32[]{:S(2)}, u32[]{:S(2)}) %collective-permute-start.10) | collective-permute-done | bytes 557088 | tf_op jit(solution)/shard_map/ppermute | solution.py:79
  153.5 3.7 %project_query.1 = bf16[2,4,2,256,256]{4,3,2,1,0:T(8,128)(2,1)S(1)} custom-call(s32[3]{0:T(128)S(1)} %pad_add_fusion.meta, bf16[4,272,512]{2,1,0:T(8,128)(2,1)S(1)} %pad_maximum_fusion.3.mine_low.a, bf16[4,272,512]{2,1,0:T(8,128)(2,1)} %collective-permute-done.3.theirs_low.b, bf16[4,272,512]{2,1,0:T(8,128)(2,1)S(1)} %collective-permute-done.2.mine_high.c, ...), custom_call_target="tpu_custom_call" | custom-call | flops 1073741824 | bytes 4194304 | tf_op jit(solution)/shard_map/project_query/pallas_call | solution.py:134
  157.2 13.8 %query_grad.1.dq_ref = bf16[512,256]{1,0:T(8,128)(2,1)S(1)} custom-call(s32[3]{0:T(128)S(1)} %pad_add_fusion.meta, s32[17]{0:T(128)S(1)} %convert_reduce_fusion.starts, s32[16]{0:T(128)S(1)} %fusion.4.table, bf16[512,256]{1,0:T(8,128)(2,1)S(1)} %get-tuple-element.25.q_ref, f32[1,512]{1,0:T(1,128)S(1)} %get-tuple-element.49.ids_ref.own_ids, ...), custom_call_target="tpu_custom_call" | custom-call | flops 6000000000 | bytes 16000000 | tf_op jit(solution)/shard_map/query_grad/pallas_call | solution.py:655
  172.8 2.9 %prompt_grad.1 = (f32[1000,256]{1,0:T(8,128)S(1)}, bf16[1000,256]{1,0:T(8,128)(2,1)S(1)}) custom-call(s32[3]{0:T(128)S(1)} %pad_add_fusion.meta, s32[17]{0:T(128)S(1)} %convert_reduce_fusion.starts, s32[16]{0:T(128)S(1)} %fusion.4.table, bf16[16,256,256]{2,1,0:T(8,128)(2,1)S(1)} %bitcast.35, f32[8,1,512]{2,1,0:T(1,128)S(1)} %maximum_convert_fusion.1.ids_ref, ...), custom_call_target="tpu_custom_call" | custom-call | flops 6000000000 | bytes 16000000 | tf_op jit(solution)/shard_map/prompt_grad/pallas_call | solution.py:803
  175.7 2.2 collective-permute-start.13
  179.6 6.5 %collective-permute-start.17 = (bf16[1000,256]{1,0:T(8,128)(2,1)S(1)}, bf16[1000,256]{1,0:T(8,128)(2,1)S(1)}, u32[]{:S(2)}, u32[]{:S(2)}) collective-permute-start(bf16[1000,256]{1,0:T(8,128)(2,1)S(1)} %reduce-precision_convert_fusion.2), channel_id=1, source_target_pairs={{0,2},{1,3},{2,0},{3,1},{4,6},{5,7},{6,4},{7,5},{8,10},{9,11},{10,... | collective-permute-start | bytes 1536008 | tf_op jit(solution)/shard_map/ppermute | solution.py:86
  186.0 4.8 %token_grad.1 = bf16[512,512]{1,0:T(8,128)(2,1)S(1)} custom-call(s32[3]{0:T(128)S(1)} %pad_add_fusion.meta, s32[17]{0:T(128)S(1)} %convert_reduce_fusion.starts, bf16[16,256,256]{2,1,0:T(8,128)(2,1)S(1)} %bitcast.36, f32[8,1,512]{2,1,0:T(1,128)S(1)} %maximum_convert_fusion.1.ids_ref, bf16[4,544,256]{2,1,0:T(8,128)(2,1)S(1)} %pad_maximum_fusion.4.low_ref, ...), custom_call_target="tpu_custom_call" | custom-call | flops 4000000000 | bytes 16000000 | tf_op jit(solution)/shard_map/token_grad/pallas_call | solution.py:873
  191.0 7.2 %collective-permute-done.17 = bf16[1000,256]{1,0:T(8,128)(2,1)S(1)} collective-permute-done((bf16[1000,256]{1,0:T(8,128)(2,1)S(1)}, bf16[1000,256]{1,0:T(8,128)(2,1)S(1)}, u32[]{:S(2)}, u32[]{:S(2)}) %collective-permute-start.17) | collective-permute-done | bytes 512032 | tf_op jit(solution)/shard_map/ppermute | solution.py:86
  198.2 1.6 multiply_reduce_fusion
  202.1 1.8 collective-permute-start.15
  204.6 6.1 %collective-permute-start.20 = (f32[8,128]{1,0:T(8,128)S(1)}, f32[8,128]{1,0:T(8,128)S(1)}, u32[]{:S(2)}, u32[]{:S(2)}) collective-permute-start(f32[8,128]{1,0:T(8,128)S(1)} %broadcast_add_fusion), channel_id=1, source_target_pairs={{0,4},{4,0},{8,12},{12,8},{16,20},{20,16},{24,28},{28,24},{1,5},{5... | collective-permute-start | bytes 12296 | tf_op jit(solution)/shard_map/ppermute | solution.py:1014
  210.7 1.6 collective-permute-done.20
  212.9 9.5 %collective-permute-start.21 = (f32[8,128]{1,0:T(8,128)S(1)}, f32[8,128]{1,0:T(8,128)S(1)}, u32[]{:S(2)}, u32[]{:S(2)}) collective-permute-start(f32[8,128]{1,0:T(8,128)S(1)} %fusion.7), channel_id=1, source_target_pairs={{0,8},{4,12},{8,0},{12,4},{16,24},{20,28},{24,16},{28,20},{1,9},{5... | collective-permute-start | bytes 12296 | tf_op jit(solution)/shard_map/ppermute | solution.py:1014
  224.7 3.8 %collective-permute-done.22 = f32[8,128]{1,0:T(8,128)S(1)} collective-permute-done((f32[8,128]{1,0:T(8,128)S(1)}, f32[8,128]{1,0:T(8,128)S(1)}, u32[]{:S(2)}, u32[]{:S(2)}) %collective-permute-start.22) | collective-permute-done | bytes 4128 | tf_op jit(solution)/shard_map/ppermute | solution.py:1014
  231.6 5.7 %divide_subtract_fusion = (f32[1000,512]{1,0:T(8,128)}, f32[1000,512]{1,0:T(8,128)}, f32[1000,512]{1,0:T(8,128)}, f32[1000,512]{1,0:T(8,128)}) fusion(f32[1000,512]{1,0:T(8,128)S(1)} %copy-done.13, f32[]{:T(128)S(6)} %sub.23, f32[]{:T(128)S(6)} %sub.22, f32[1000,512]{1,0:T(8,128)S(1)} %copy-done.20, f32[1000,512]{1,0:T(8,128)} %param.29, f32[]{:T(128)S(6)} %min.3, ...), kind=kLoop, calls=%fused_computation.4 | loop fusion | flops 9728000 | bytes 15360012 | tf_op jit(solution)/shard_map/sub | solution.py:1030
  (119 shorter events, 29.1 us)
Async XLA Ops:
  7.2 2.6 %copy-start.21 = (s32[2,512]{1,0:T(2,128)S(1)}, s32[2,512]{1,0:T(2,128)}, u32[]{:S(2)}) copy-start(s32[2,512]{1,0:T(2,128)} %param.18) | copy-start | bytes 12292
  7.2 100.1 %all-gather.3.cloned.1.call-start = ((), (), s32[]{:S(2)}) async-start(), calls=%async_computation | async-start | bytes 8448000 | tf_op jit(solution)/shard_map/all_gather | solution.py:931
  10.8 30.9 %copy-start.22 = (f32[256]{0:T(256)S(1)}, f32[256]{0:T(256)}, u32[]{:S(2)}) copy-start(f32[256]{0:T(256)} %param.23) | copy-start | bytes 3076
  10.8 7.6 %collective-permute-start = (bf16[1,272,512]{2,1,0:T(8,128)(2,1)S(1)}, bf16[1,272,512]{2,1,0:T(8,128)(2,1)S(1)}, u32[]{:S(2)}, u32[]{:S(2)}) collective-permute-start(bf16[1,272,512]{2,1,0:T(8,128)(2,1)S(1)} %maximum_bitcast_fusion), channel_id=1, source_target_pairs={{0,4},{1,17},{2,6},{3,19},{4,0},{5,21},{6,2},{7,23},{8,12},{9,25},... | collective-permute-start | bytes 835592 | tf_op jit(solution)/shard_map/ppermute | solution.py:79
  18.4 22.1 %collective-permute-start.1 = (bf16[2,272,512]{2,1,0:T(8,128)(2,1)S(1)}, bf16[2,272,512]{2,1,0:T(8,128)(2,1)S(1)}, u32[]{:S(2)}, u32[]{:S(2)}) collective-permute-start(bf16[2,272,512]{2,1,0:T(8,128)(2,1)S(1)} %pad_maximum_fusion.5), channel_id=1, source_target_pairs={{0,16},{1,9},{2,18},{3,11},{4,20},{5,13},{6,22},{7,15},{8,24},{9,1... | collective-permute-start | bytes 1671176 | tf_op jit(solution)/shard_map/ppermute | solution.py:79
  40.6 26.5 %collective-permute-start.2 = (bf16[4,272,512]{2,1,0:T(8,128)(2,1)S(1)}, bf16[4,272,512]{2,1,0:T(8,128)(2,1)S(1)}, u32[]{:S(2)}, u32[]{:S(2)}) collective-permute-start(bf16[4,272,512]{2,1,0:T(8,128)(2,1)S(1)} %pad_maximum_fusion.3.mine_low.a), channel_id=1, source_target_pairs={{0,8},{1,5},{2,10},{3,7},{4,12},{5,1},{6,14},{7,3},{8,0},{9,13},{1... | collective-permute-start | bytes 3342344 | tf_op jit(solution)/shard_map/ppermute | solution.py:79
  43.9 27.7 %copy-start.23 = (s32[2,16]{1,0:T(2,128)S(1)}, s32[2,16]{1,0:T(2,128)}, u32[]{:S(2)}) copy-start(s32[2,16]{1,0:T(2,128)} %param.19) | copy-start | bytes 388
  43.9 26.1 %collective-permute-start.7 = (bf16[656,512]{1,0:T(8,128)(2,1)S(1)}, bf16[656,512]{1,0:T(8,128)(2,1)S(1)}, u32[]{:S(2)}, u32[]{:S(2)}) collective-permute-start(bf16[656,512]{1,0:T(8,128)(2,1)S(1)} %fusion.2), channel_id=1, source_target_pairs={{0,2},{1,3},{2,0},{3,1},{4,6},{5,7},{6,4},{7,5},{8,10},{9,11},{10,... | collective-permute-start | bytes 2015240 | tf_op jit(solution)/shard_map/ppermute | solution.py:86
  45.5 39.3 %collective-permute-start.3 = (bf16[4,272,512]{2,1,0:T(8,128)(2,1)S(1)}, bf16[4,272,512]{2,1,0:T(8,128)(2,1)}, u32[]{:S(2)}, u32[]{:S(2)}) collective-permute-start(bf16[4,272,512]{2,1,0:T(8,128)(2,1)S(1)} %pad_maximum_fusion.3.mine_low.a), channel_id=1, source_target_pairs={{0,1},{1,0},{2,3},{3,2},{4,5},{5,4},{6,7},{7,6},{8,9},{9,8},{10,11... | collective-permute-start | bytes 3342344 | tf_op jit(solution)/shard_map/ppermute | solution.py:86
  67.1 17.7 %collective-permute-start.4 = (bf16[4,272,512]{2,1,0:T(8,128)(2,1)S(1)}, bf16[4,272,512]{2,1,0:T(8,128)(2,1)}, u32[]{:S(2)}, u32[]{:S(2)}) collective-permute-start(bf16[4,272,512]{2,1,0:T(8,128)(2,1)S(1)} %collective-permute-done.2.mine_high.c), channel_id=1, source_target_pairs={{0,1},{1,0},{2,3},{3,2},{4,5},{5,4},{6,7},{7,6},{8,9},{9,8},{10,11... | collective-permute-start | bytes 3342344 | tf_op jit(solution)/shard_map/ppermute | solution.py:86
  67.1 17.7 %collective-permute-start.5 = (bf16[3,512,128]{2,1,0:T(8,128)(2,1)}, bf16[3,512,128]{2,1,0:T(8,128)(2,1)}, u32[]{:S(2)}, u32[]{:S(2)}) collective-permute-start(bf16[3,512,128]{2,1,0:T(8,128)(2,1)} %in_own.9), channel_id=1, source_target_pairs={{0,2},{1,3},{2,0},{3,1},{4,6},{5,7},{6,4},{7,5},{8,10},{9,11},{10,... | collective-permute-start | bytes 1179656 | tf_op jit(solution)/shard_map/ppermute | solution.py:86
  71.4 53.6 %collective-permute-start.8 = (bf16[2,656,512]{2,1,0:T(8,128)(2,1)}, bf16[2,656,512]{2,1,0:T(8,128)(2,1)}, u32[]{:S(2)}, u32[]{:S(2)}) collective-permute-start(bf16[2,656,512]{2,1,0:T(8,128)(2,1)} %pad_maximum_fusion.2), channel_id=1, source_target_pairs={{0,1},{1,0},{2,3},{3,2},{4,5},{5,4},{6,7},{7,6},{8,9},{9,8},{10,11... | collective-permute-start | bytes 4030472 | tf_op jit(solution)/shard_map/ppermute | solution.py:86
  108.2 3.3 %copy-start.4 = (bf16[32000,128]{1,0:T(8,128)(2,1)S(1)}, bf16[32000,128]{1,0:T(8,128)(2,1)}, u32[]{:S(2)}) copy-start(bf16[32000,128]{1,0:T(8,128)(2,1)} %all-gather.3.cloned.1.call-done) | copy-start | bytes 24576004
  113.8 11.1 %copy-start.15 = (bf16[1,656,512]{2,1,0:T(8,128)(2,1)S(1)}, bf16[1,656,512]{2,1,0:T(8,128)(2,1)}, u32[]{:S(2)}) copy-start(bf16[1,656,512]{2,1,0:T(8,128)(2,1)} %copy-done.14) | copy-start | bytes 2015236
  113.8 11.1 %copy-start.19 = (bf16[656,512]{1,0:T(8,128)(2,1)S(1)}, bf16[656,512]{1,0:T(8,128)(2,1)}, u32[]{:S(2)}) copy-start(bf16[656,512]{1,0:T(8,128)(2,1)} %copy-done.18) | copy-start | bytes 2015236
  124.7 2.1 collective-permute-start.6
  133.3 6.6 %collective-permute-start.9 = (bf16[1,544,256]{2,1,0:T(8,128)(2,1)S(1)}, bf16[1,544,256]{2,1,0:T(8,128)(2,1)S(1)}, u32[]{:S(2)}, u32[]{:S(2)}) collective-permute-start(bf16[1,544,256]{2,1,0:T(8,128)(2,1)S(1)} %bitcast.37), channel_id=1, source_target_pairs={{0,4},{1,17},{2,6},{3,19},{4,0},{5,21},{6,2},{7,23},{8,12},{9,25},... | collective-permute-start | bytes 835592 | tf_op jit(solution)/shard_map/ppermute | solution.py:79
  140.0 13.4 %collective-permute-start.10 = (bf16[2,544,256]{2,1,0:T(8,128)(2,1)S(1)}, bf16[2,544,256]{2,1,0:T(8,128)(2,1)S(1)}, u32[]{:S(2)}, u32[]{:S(2)}) collective-permute-start(bf16[2,544,256]{2,1,0:T(8,128)(2,1)S(1)} %pad_maximum_fusion.6), channel_id=1, source_target_pairs={{0,16},{1,9},{2,18},{3,11},{4,20},{5,13},{6,22},{7,15},{8,24},{9,1... | collective-permute-start | bytes 1671176 | tf_op jit(solution)/shard_map/ppermute | solution.py:79
  140.0 31.0 %collective-permute-start.12 = (f32[512,512]{1,0:T(8,128)S(1)}, f32[512,512]{1,0:T(8,128)S(1)}, u32[]{:S(2)}, u32[]{:S(2)}) collective-permute-start(f32[512,512]{1,0:T(8,128)S(1)} %get-tuple-element.32), channel_id=1, source_target_pairs={{0,2},{1,3},{2,0},{3,1},{4,6},{5,7},{6,4},{7,5},{8,10},{9,11},{10,... | collective-permute-start | bytes 3145736 | tf_op jit(solution)/shard_map/ppermute | solution.py:86
  153.5 19.3 %collective-permute-start.11 = (bf16[4,544,256]{2,1,0:T(8,128)(2,1)S(1)}, bf16[4,544,256]{2,1,0:T(8,128)(2,1)S(1)}, u32[]{:S(2)}, u32[]{:S(2)}) collective-permute-start(bf16[4,544,256]{2,1,0:T(8,128)(2,1)S(1)} %pad_maximum_fusion.4.low_ref), channel_id=1, source_target_pairs={{0,8},{1,5},{2,10},{3,7},{4,12},{5,1},{6,14},{7,3},{8,0},{9,13},{1... | collective-permute-start | bytes 3342344 | tf_op jit(solution)/shard_map/ppermute | solution.py:79
  175.7 3.7 %collective-permute-start.13 = (bf16[1000,256]{1,0:T(8,128)(2,1)S(1)}, bf16[1000,256]{1,0:T(8,128)(2,1)S(1)}, u32[]{:S(2)}, u32[]{:S(2)}) collective-permute-start(bf16[1000,256]{1,0:T(8,128)(2,1)S(1)} %get-tuple-element.40), channel_id=1, source_target_pairs={{0,1},{1,0},{2,3},{3,2},{4,5},{5,4},{6,7},{7,6},{8,9},{9,8},{10,11... | collective-permute-start | bytes 1536008 | tf_op jit(solution)/shard_map/ppermute | solution.py:86
  179.6 18.6 %collective-permute-start.17 = (bf16[1000,256]{1,0:T(8,128)(2,1)S(1)}, bf16[1000,256]{1,0:T(8,128)(2,1)S(1)}, u32[]{:S(2)}, u32[]{:S(2)}) collective-permute-start(bf16[1000,256]{1,0:T(8,128)(2,1)S(1)} %reduce-precision_convert_fusion.2), channel_id=1, source_target_pairs={{0,2},{1,3},{2,0},{3,1},{4,6},{5,7},{6,4},{7,5},{8,10},{9,11},{10,... | collective-permute-start | bytes 1536008 | tf_op jit(solution)/shard_map/ppermute | solution.py:86
  190.8 10.2 %collective-permute-start.14 = (bf16[512,512]{1,0:T(8,128)(2,1)S(1)}, bf16[512,512]{1,0:T(8,128)(2,1)S(1)}, u32[]{:S(2)}, u32[]{:S(2)}) collective-permute-start(bf16[512,512]{1,0:T(8,128)(2,1)S(1)} %token_grad.1), channel_id=1, source_target_pairs={{0,1},{1,0},{2,3},{3,2},{4,5},{5,4},{6,7},{7,6},{8,9},{9,8},{10,11... | collective-permute-start | bytes 1572872 | tf_op jit(solution)/shard_map/ppermute | solution.py:86
  199.8 30.0 %collective-permute-start.18 = (bf16[1000,256]{1,0:T(8,128)(2,1)}, bf16[1000,256]{1,0:T(8,128)(2,1)}, u32[]{:S(2)}, u32[]{:S(2)}) collective-permute-start(bf16[1000,256]{1,0:T(8,128)(2,1)} %get-tuple-element.48), channel_id=1, source_target_pairs={{0,1},{1,0},{2,3},{3,2},{4,5},{5,4},{6,7},{7,6},{8,9},{9,8},{10,11... | collective-permute-start | bytes 1536008 | tf_op jit(solution)/shard_map/ppermute | solution.py:86
  200.5 3.4 %collective-permute-start.19 = (f32[8,128]{1,0:T(8,128)S(1)}, f32[8,128]{1,0:T(8,128)S(1)}, u32[]{:S(2)}, u32[]{:S(2)}) collective-permute-start(f32[8,128]{1,0:T(8,128)S(1)} %broadcast_in_dim.24), channel_id=1, source_target_pairs={{0,1},{1,0},{2,3},{3,2},{4,5},{5,4},{6,7},{7,6},{8,9},{9,8},{10,11... | collective-permute-start | bytes 12296 | tf_op jit(solution)/shard_map/ppermute | solution.py:86
  201.1 30.2 %copy-start.13 = (f32[1000,512]{1,0:T(8,128)S(1)}, f32[1000,512]{1,0:T(8,128)}, u32[]{:S(2)}) copy-start(f32[1000,512]{1,0:T(8,128)} %param.28) | copy-start | bytes 6144004
  202.1 27.6 %collective-permute-start.15 = (bf16[256,512]{1,0:T(8,128)(2,1)S(1)}, bf16[256,512]{1,0:T(8,128)(2,1)S(1)}, u32[]{:S(2)}, u32[]{:S(2)}) collective-permute-start(bf16[256,512]{1,0:T(8,128)(2,1)S(1)} %constant_dynamic-slice_fusion), channel_id=1, source_target_pairs={{0,2},{1,3},{2,0},{3,1},{4,6},{5,7},{6,4},{7,5},{8,10},{9,11},{10,... | collective-permute-start | bytes 786440 | tf_op jit(solution)/shard_map/ppermute | solution.py:86
  204.6 7.7 %collective-permute-start.20 = (f32[8,128]{1,0:T(8,128)S(1)}, f32[8,128]{1,0:T(8,128)S(1)}, u32[]{:S(2)}, u32[]{:S(2)}) collective-permute-start(f32[8,128]{1,0:T(8,128)S(1)} %broadcast_add_fusion), channel_id=1, source_target_pairs={{0,4},{4,0},{8,12},{12,8},{16,20},{20,16},{24,28},{28,24},{1,5},{5... | collective-permute-start | bytes 12296 | tf_op jit(solution)/shard_map/ppermute | solution.py:1014
  212.9 11.1 %collective-permute-start.21 = (f32[8,128]{1,0:T(8,128)S(1)}, f32[8,128]{1,0:T(8,128)S(1)}, u32[]{:S(2)}, u32[]{:S(2)}) collective-permute-start(f32[8,128]{1,0:T(8,128)S(1)} %fusion.7), channel_id=1, source_target_pairs={{0,8},{4,12},{8,0},{12,4},{16,24},{20,28},{24,16},{28,20},{1,9},{5... | collective-permute-start | bytes 12296 | tf_op jit(solution)/shard_map/ppermute | solution.py:1014
  224.0 4.5 %collective-permute-start.22 = (f32[8,128]{1,0:T(8,128)S(1)}, f32[8,128]{1,0:T(8,128)S(1)}, u32[]{:S(2)}, u32[]{:S(2)}) collective-permute-start(f32[8,128]{1,0:T(8,128)S(1)} %add.66), channel_id=1, source_target_pairs={{0,16},{4,20},{8,24},{12,28},{16,0},{20,4},{24,8},{28,12},{1,17},{... | collective-permute-start | bytes 12296 | tf_op jit(solution)/shard_map/ppermute | solution.py:1014
  229.7 7.6 %collective-permute-start.16 = (bf16[256,512]{1,0:T(8,128)(2,1)S(1)}, bf16[256,512]{1,0:T(8,128)(2,1)S(1)}, u32[]{:S(2)}, u32[]{:S(2)}) collective-permute-start(bf16[256,512]{1,0:T(8,128)(2,1)S(1)} %collective-permute-done.15), channel_id=1, source_target_pairs={{0,1},{1,0},{2,3},{3,2},{4,5},{5,4},{6,7},{7,6},{8,9},{9,8},{10,11... | collective-permute-start | bytes 786440 | tf_op jit(solution)/shard_map/ppermute | solution.py:86
  231.6 5.8 %copy-start.17 = (bf16[512,512]{1,0:T(8,128)(2,1)S(1)}, bf16[512,512]{1,0:T(8,128)(2,1)}, u32[]{:S(2)}) copy-start(bf16[512,512]{1,0:T(8,128)(2,1)} %copy-done.16) | copy-start | bytes 1572868
  (16 other events, 23.7 us)
Sparse Core Ops, SparseCore 0:
  11.5 95.6 all-gather.2
where the time goes:
time: 251 us; the launch traced here: 247 us
  waiting for transfers between devices  105 us (42%)
  Pallas kernels  47.6 us (19%)
  starting transfers between devices  40.1 us (16%)
  other arithmetic  21.5 us (9%)
  between operations  17.2 us (7%)
  local copies, waits for them, and re-layouts  15.8 us (6%)
    ppermute x6, waiting for transfers between devices, gather_rows(): other = lax.ppermute(held, BOTH, pairs)  63 us
    ppermute x14, waiting for transfers between devices, swap_head(): lax.ppermute(value, 'head', [(i, i ^ mask) for i in range(head_count)])  21.6 us
    ppermute x14, starting transfers between devices, swap_head(): lax.ppermute(value, 'head', [(i, i ^ mask) for i in range(head_count)])  17.1 us
    ppermute x3, starting transfers between devices, per_device(): lax.ppermute(squares, 'rows', [(i, i ^ mask) for i in range(row_count)])  15.6 us
    pallas_call x1, Pallas kernels, query_grad(): pl.pallas_call(functools.partial(query_grad_kernel, data_count, factor),...  13.8 us
    all_gather x1, waiting for transfers between devices, per_device(): prompt_all = lax.all_gather(prompt_own, BOTH, axis=0, tiled=False)  13.1 us
    unnamed x52, local copies, waits for them, and re-layouts  12.9 us
    pallas_call x1, Pallas kernels, prompt_forward(): pl.pallas_call(functools.partial(prompt_forward_kernel, data_count, facto...  10.7 us
  transfers between devices with their start and end apart: 24, of which 12 were waited for; matrix products, arithmetic and copies ran while one was open for 9% of the time, Pallas kernels for 16%

commit v1 on v0

v1 whole, which is shorter than its diff:
```python
import functools

import jax
import jax.numpy as jnp
from jax import lax
from jax.experimental import pallas as pl
from jax.experimental.pallas import tpu as pltpu
from jax.sharding import PartitionSpec as P

PLEN = 1000
NEGATIVE = -1e30
BETA_ONE = 0.9
BETA_TWO = 0.999
LEARNING_RATE = 0.5
DECAY_RATE = 0.01
EPSILON = 1e-08
CLIP_NORM = 1.0
LOG2E = 1.4426950408889634
PACK = 16
STATS = 32
VMEM_LIMIT = 60 * 1024 * 1024
BF = jnp.bfloat16
F32 = jnp.float32
BOTH = ("rows", "head")


def params(*operands, spare=20 << 20):
    held = sum(x.size * x.dtype.itemsize for x in operands)
    return pltpu.CompilerParams(vmem_limit_bytes=min(VMEM_LIMIT, held + spare))


def cost(flops, bytes_accessed, transcendentals=0):
    return pl.CostEstimate(
        flops=int(flops), bytes_accessed=int(bytes_accessed), transcendentals=int(transcendentals)
    )


def mm(a, b):
    return lax.dot_general(a, b, (((1,), (0,)), ((), ())), preferred_element_type=F32)


def mm_nt(a, b):
    return lax.dot_general(a, b, (((1,), (1,)), ((), ())), preferred_element_type=F32)


def split3(value):
    high = value.astype(BF)
    rest = value - high.astype(F32)
    mid = rest.astype(BF)
    low = (rest - mid.astype(F32)).astype(BF)
    return high, mid, low


def bit_orders(row_count):
    bits = row_count.bit_length() - 1
    return ([0] + list(range(bits - 1, 0, -1)), list(range(bits - 1, 0, -1)) + [0])


def prompt_orders(row_count):
    bits = row_count.bit_length() - 1
    if bits < 2:
        return bit_orders(row_count)
    high = list(range(bits - 1, 1, -1))
    return (high + [0, 1], [1] + high + [0])


def slot_of(offset, parity, orders):
    def mapped(order):
        total = 0
        for place, bit in enumerate(order):
            total = total + (((offset >> bit) & 1) << place)
        return total

    return jnp.where(parity == 0, mapped(orders[0]), mapped(orders[1]))


def gather_stage(held, place, orders, row_count, head_count):
    pairs = []
    for row in range(row_count):
        for head in range(head_count):
            bit = orders[head % 2][place]
            pairs.append((row * head_count + head, (row ^ (1 << bit)) * head_count + head))
    return lax.ppermute(held, BOTH, pairs)


def gather_rows(block, row_count, head_count, before_send):
    held = block[None]
    orders = bit_orders(row_count)
    stages = len(orders[0])
    for place in range(stages):
        held = before_send(stages - place, held)
        other = gather_stage(held, place, orders, row_count, head_count)
        if place < stages - 1:
            held = jnp.concatenate([held, other], axis=0)
    return held, other


def xor_sum(value, row_count, head_count, after):
    def moved(mask):
        count = row_count * head_count
        return lax.ppermute(value, BOTH, [(i, i ^ mask) for i in range(count)])

    masks = [1]
    bit = head_count
    while bit < row_count * head_count:
        masks.append(bit)
        bit = bit * 2
    done = 0
    while masks:
        if len(masks) == 1:
            value = value + moved(masks[0])
        else:
            first, second, both = (moved(m) for m in (masks[0], masks[1], masks[0] ^ masks[1]))
            value = (value + first) + (second + both)
        masks = masks[2:]
        done = done + 1
        value = after(done, value)
    return value


def swap_head(value, mask, head_count):
    return lax.ppermute(value, "head", [(i, i ^ mask) for i in range(head_count)])


def smem():
    return pl.BlockSpec(memory_space=pltpu.SMEM)


def vmem():
    return pl.BlockSpec(memory_space=pltpu.VMEM)


def hbm():
    return pl.BlockSpec(memory_space=pltpu.HBM)


def join_weights(meta, own, other, target, first):
    dim = own.shape[2]
    for kind in range(first, own.shape[0]):
        for place in range(2):
            column = ((kind - first) * 2 + place) * dim
            target[:, column : column + dim] = jnp.where(meta[1] == place, own[kind], other[kind])


def wide(value, count):
    return jnp.concatenate([value] * count, axis=1)


def column_of(line):
    return jnp.transpose(jnp.broadcast_to(line, (128, line.shape[1])))


def project_query_kernel(meta, a, b, c, d, own, other, q_out):
    half = a.shape[1] - PACK
    dim = own.shape[2]
    weights = jnp.concatenate(
        [jnp.where(meta[1] == place, own[0], other[0]) for place in range(2)], axis=1
    )
    for high, pair in enumerate(((a, b), (c, d))):
        for place, ref in enumerate(pair):
            q_out[high, 0, place] = mm(ref[0, :half], weights).astype(BF)


def project_query(meta, mine, theirs, in_own, in_other):
    slots, rows, width = mine[0].shape
    half = rows - PACK
    dim = in_own.shape[2]
    block = pl.BlockSpec((1, rows, width), lambda g: (g, 0, 0))
    whole = pl.BlockSpec((1,) + in_own.shape[1:], lambda g: (0, 0, 0))
    out = pl.pallas_call(
        project_query_kernel,
        out_shape=jax.ShapeDtypeStruct((2, slots, 2, half, 2 * dim), BF),
        grid=(slots,),
        in_specs=[smem()] + [block] * 4 + [whole] * 2,
        out_specs=pl.BlockSpec((2, 1, 2, half, 2 * dim), lambda g: (0, g, 0, 0, 0)),
        compiler_params=params(),
        cost_estimate=cost(8 * slots * half * width * 2 * dim, 8 * slots * half * width),
        name="project_query",
    )(meta, mine[0], theirs[0], mine[1], theirs[1], in_own, in_other)
    return out.reshape(4 * slots, half, 2 * dim)


def key_range(starts, low, high, data_count):
    first = jnp.int32(1 << 30)
    last = jnp.int32(0)
    for data in range(data_count):
        begin, end = starts[data], starts[data + 1]
        hit = (begin < high) & (end > low) & (begin < end)
        first = jnp.where(hit, jnp.minimum(first, begin), first)
        last = jnp.where(hit, jnp.maximum(last, end), last)
    return first, last


def shard_copies(meta, shard, gathered, x_ref, sem):
    slots = gathered[0].shape[0]
    copies = []
    for place in range(2):
        slot = slot_of(shard ^ meta[0], meta[2] ^ place, bit_orders(2 * slots))
        for bank in range(2):
            here = (slot < slots) if bank == 0 else (slot >= slots)
            source = gathered[place * 2 + bank]
            copy = pltpu.make_async_copy(
                source.at[jnp.where(here, slot - bank * slots, 0)],
                x_ref.at[shard, place],
                sem.at[shard, place],
            )
            copies.append((here, copy))
    return copies


def fetch_shards(meta, first, last, gathered, x_ref, sem):
    def start(shard, carry):
        for here, copy in shard_copies(meta, shard, gathered, x_ref, sem):

            @pl.when(here)
            def _():
                copy.start()

        return carry

    lax.fori_loop(first, last, start, 0)


def load_shard(meta, shard, gathered, x_ref, sem):
    half = x_ref.shape[2] - PACK
    parity = meta[2]
    for place in range(2):
        pltpu.make_async_copy(gathered[0].at[0], x_ref.at[shard, place], sem.at[shard, place]).wait()
    line = x_ref[shard, 0, half : half + 1, :].astype(F32)
    first, second = line[:, :half], line[:, half : 2 * half]
    line = jnp.concatenate(
        [jnp.where(parity == 0, first, second), jnp.where(parity == 0, second, first)], axis=1
    )
    return jnp.concatenate([x_ref[shard, 0, :half, :], x_ref[shard, 1, :half, :]], axis=0), line


def online(scores, factor, mask, m_ref, place):
    old_max = m_ref[place]
    size = old_max.shape[0]
    top = jnp.broadcast_to(jnp.max(scores, axis=1, keepdims=True) * factor, (size, 128))
    new_max = jnp.maximum(old_max, top)
    shift = new_max
    if mask is not None:
        new_max = jnp.where(mask, new_max, old_max)
        shift = jnp.where(mask, new_max, -NEGATIVE)
    m_ref[place] = new_max
    probs = jnp.exp2(scores * factor - wide(shift, scores.shape[1] // 128))
    return probs.astype(BF), jnp.exp2(old_max - new_max)


def accumulate(acc_ref, place, alpha, probs, value):
    with_ones = jnp.concatenate([value, jnp.ones((value.shape[0], 128), BF)], axis=1)
    acc_ref[place] = acc_ref[place] * wide(alpha, with_ones.shape[1] // 128) + mm(probs, with_ones)


def token_forward_kernel(
    data_count,
    factor,
    meta,
    starts,
    ids_ref,
    in_own,
    in_other,
    tok_hbm,
    mine_low,
    mine_high,
    theirs_low,
    theirs_high,
    q_ref,
    m_ref,
    acc_ref,
    w_ref,
    x_ref,
    id_ref,
    tok_ref,
    sem,
    tok_sem,
):
    size, dim = tok_ref.shape[1], in_own.shape[2]
    tok_copy = pltpu.make_async_copy(tok_hbm, tok_ref, tok_sem)
    tok_copy.start()
    base = meta[0] * size
    first, last = key_range(starts, base, base + size, data_count)
    first, last = first // size, (last + size - 1) // size
    gathered = (mine_low, mine_high, theirs_low, theirs_high)
    fetch_shards(meta, first, last, gathered, x_ref, sem)
    join_weights(meta, in_own, in_other, w_ref, 0)
    tok_copy.wait()
    for slot in range(2):
        q_ref[slot] = mm(tok_ref[meta[1] ^ slot], w_ref[:, : 2 * dim]).astype(BF)
    m_ref[...] = jnp.full(m_ref.shape, NEGATIVE, F32)
    acc_ref[...] = jnp.zeros(acc_ref.shape, F32)
    id_ref[...] = column_of(ids_ref[meta[1]])
    rows = pl.ds(0, size)

    def step(shard, carry):
        raw_rows, line = load_shard(meta, shard, gathered, x_ref, sem)
        kv = mm(raw_rows, w_ref[:, 2 * dim :]).astype(BF)
        mask = wide(id_ref[...], size // 128) == line
        raw = [
            mm_nt(q_ref[0, :, h * dim : (h + 1) * dim], kv[:, h * dim : (h + 1) * dim])
            for h in range(2)
        ]
        parts = [
            online(jnp.where(mask, raw[h], NEGATIVE), factor, None, m_ref, (h, rows))
            for h in range(2)
        ]
        for h in range(2):
            value = kv[:, (2 + h) * dim : (3 + h) * dim]
            accumulate(acc_ref, (h, rows), parts[h][1], parts[h][0], value)
        return carry

    lax.fori_loop(first, last, step, 0)


def shard_scratch(banks):
    slots, rows, width = banks[0].shape
    return pltpu.VMEM((2 * slots, 2, rows, width), BF)


def token_forward(meta, starts, tokens, ids_rows, mine, theirs, in_own, in_other, factor, data_count):
    size, width = tokens.shape[1:]
    dim = in_own.shape[2]
    return pl.pallas_call(
        functools.partial(token_forward_kernel, data_count, factor),
        out_shape=(
            jax.ShapeDtypeStruct((2, size, 2 * dim), BF),
            jax.ShapeDtypeStruct((2, size, 128), F32),
            jax.ShapeDtypeStruct((2, size, dim + 128), F32),
        ),
        in_specs=[smem(), smem()] + [vmem()] * 3 + [hbm()] * 5,
        out_specs=[vmem()] * 3,
        scratch_shapes=[
            pltpu.VMEM((width, 6 * dim), BF),
            shard_scratch(mine),
            pltpu.VMEM((size, 128), F32),
            pltpu.VMEM(tokens.shape, BF),
            pltpu.SemaphoreType.DMA((2 * mine[0].shape[0], 2)),
            pltpu.SemaphoreType.DMA,
        ],
        compiler_params=params(*mine, *theirs),
        cost_estimate=cost(8e9, 8e6, 2e6),
        name="token_forward",
    )(meta, starts, ids_rows, in_own, in_other, tokens, *mine, *theirs)


def half_rows(block):
    return -(-block // 32) * 16


def fetch_prompts(meta, local, table, sources, raws, state, sem):
    pieces = raws.shape[2]
    slots = sources[0].shape[0]
    for number in range(state.shape[0]):
        state[number] = 0
    for batch in range(2):
        for data in range(table.shape[1]):
            number = table[batch, data]
            used = local[batch, data + 1] > local[batch, data]
            state[number] = jnp.where(used, 1, state[number])

    def start(number, carry):
        @pl.when(state[number] == 1)
        def _():
            for piece in range(pieces):
                for place in range(2):
                    shard = number * pieces + piece
                    slot = slot_of(shard ^ meta[0], meta[2] ^ place, prompt_orders(2 * slots))
                    for bank in range(2):

                        @pl.when((slot < slots) if bank == 0 else (slot >= slots))
                        def _():
                            pltpu.make_async_copy(
                                sources[place * 2 + bank].at[slot - bank * slots],
                                raws.at[place, number, piece],
                                sem.at[place, number, piece],
                            ).start()

        return carry

    lax.fori_loop(0, state.shape[0], start, 0)


def project_prompt(meta, number, sources, raws, w_ref, kv_ref, state, sem):
    pieces, block = raws.shape[2:4]

    @pl.when(state[number] == 1)
    def _():
        even = meta[2] == 0
        for piece in range(pieces):
            for place in range(2):
                pltpu.make_async_copy(
                    sources[0].at[0], raws.at[place, number, piece], sem.at[place, number, piece]
                ).wait()
            a, b = raws[0, number, piece], raws[1, number, piece]
            rows = jnp.concatenate([jnp.where(even, a, b), jnp.where(even, b, a)], axis=1)
            kv_ref[number, pl.ds(piece * block, block), :] = mm(rows, w_ref[...]).astype(BF)
        full = pieces * block
        if full < kv_ref.shape[1]:
            kv_ref[number, full:, :] = jnp.zeros((kv_ref.shape[1] - full, kv_ref.shape[2]), BF)
        state[number] = 2


def prompt_mask(meta, scores, block):
    part = half_rows(block)
    pieces = PLEN // block
    doubled = 2 * part - block
    head = min(128, part) if pieces == 1 else scores.shape[1]
    lanes = lax.broadcasted_iota(jnp.int32, (scores.shape[0], head), 1)
    out = (lanes % part < doubled * meta[1]) | (lanes >= pieces * part)
    first = jnp.where(out, NEGATIVE, scores[:, :head])
    if head == scores.shape[1]:
        return first
    return jnp.concatenate([first, scores[:, head:]], axis=1)


def visit_prompts(meta, local, table, size, prepare, update):
    data_count = table.shape[1]

    def visit(index, carry):
        slot, data = index // data_count, index % data_count
        batch = meta[1] ^ slot
        begin, end = local[batch, data], local[batch, data + 1]

        @pl.when(begin < end)
        def _():
            number = table[batch, data]
            prepare(number)
            low = begin // 128
            count = (end + 127) // 128 - low
            for case in range(1, size // 128 + 1):

                @pl.when(count == case)
                def _():
                    rows = pl.ds(pl.multiple_of(low * 128, 128), case * 128)
                    update(slot, rows, data, number)

        return carry

    lax.fori_loop(0, 2 * data_count, visit, 0)


def store_line(ref, row, line):
    width = ref.shape[1]
    for term in split3(line):
        for low in range(0, line.shape[1], width):
            ref[row : row + 1, :] = term[:, low : low + width]
            row = row + 1
    return row


def load_line(ref, row, length):
    width = ref.shape[1]
    rows_per = length // width
    total = 0.0
    for place in range(3):
        first = row + place * rows_per
        pieces = [ref[first + i : first + i + 1, :].astype(F32) for i in range(rows_per)]
        total = total + jnp.concatenate(pieces, axis=1)
    return total


def prompt_forward_kernel(
    block,
    factor,
    meta,
    local,
    table,
    q_ref,
    ids_ref,
    m_in,
    acc_in,
    in_own,
    in_other,
    mine_low,
    mine_high,
    theirs_low,
    theirs_high,
    wide_ref,
    lse_ref,
    send_ref,
    m_ref,
    acc_ref,
    raws,
    w_ref,
    kv_ref,
    id_ref,
    state,
    sem,
):
    size, dim = q_ref.shape[1], q_ref.shape[2] // 2
    sources = (mine_low, mine_high, theirs_low, theirs_high)
    fetch_prompts(meta, local, table, sources, raws, state, sem)
    join_weights(meta, in_own, in_other, w_ref, 1)
    m_ref[0] = m_in[...]
    acc_ref[0] = acc_in[...]
    m_ref[1] = jnp.full(m_in.shape, NEGATIVE, F32)
    acc_ref[1] = jnp.zeros(acc_in.shape, F32)
    for slot in range(2):
        id_ref[slot] = column_of(ids_ref[meta[1] ^ slot])

    def prepare(number):
        project_prompt(meta, number, sources, raws, w_ref, kv_ref, state, sem)

    def update(slot, rows, data, number):
        mask = id_ref[slot, rows, :] == data.astype(F32)
        raw = [
            mm_nt(q_ref[slot, rows, pl.ds(h * dim, dim)], kv_ref[number, :, pl.ds(h * dim, dim)])
            for h in range(2)
        ]
        parts = [
            online(prompt_mask(meta, raw[h], block), factor, mask, m_ref, (slot, h, rows))
            for h in range(2)
        ]
        for h in range(2):
            value = kv_ref[number, :, pl.ds((2 + h) * dim, dim)]
            accumulate(acc_ref, (slot, h, rows), parts[h][1], parts[h][0], value)

    visit_prompts(meta, local, table, size, prepare, update)
    row = size
    send_ref[pl.ds(size, PACK), :] = jnp.zeros((PACK, 2 * dim), BF)
    for h in range(2):
        cols = pl.ds(h * dim, dim)
        total = acc_ref[0, h, :, dim:]
        wide_ref[:, cols] = acc_ref[0, h, :, :dim] / total
        lse_ref[h] = m_ref[0, h] + jnp.log2(total)
        total = acc_ref[1, h, :, dim:]
        send_ref[pl.ds(0, size), cols] = (acc_ref[1, h, :, :dim] / total).astype(BF)
        line = jnp.transpose(m_ref[1, h] + jnp.log2(total))[0:1, :]
        row = store_line(send_ref, row, line)


def prompt_scratch(prompt_banks, width, dim, block):
    slots, part, columns = prompt_banks[0].shape
    pieces = PLEN // block
    count = 2 * slots // pieces
    return [
        pltpu.VMEM((2, count, pieces, part, columns), BF),
        pltpu.VMEM((width, 4 * dim), BF),
        pltpu.VMEM((count, -(-pieces * part // 128) * 128, 4 * dim), BF),
    ], [pltpu.SMEM((count,), jnp.int32), pltpu.SemaphoreType.DMA((2, count, pieces))]


def prompt_forward(
    meta, local, table, q_own, ids_rows, state, prompt_mine, prompt_theirs, in_own, in_other, factor, block
):
    size, dim = q_own.shape[1], q_own.shape[2] // 2
    buffers, flags = prompt_scratch(prompt_mine, in_own.shape[1], dim, block)
    return pl.pallas_call(
        functools.partial(prompt_forward_kernel, block, factor),
        out_shape=(
            jax.ShapeDtypeStruct((size, 2 * dim), F32),
            jax.ShapeDtypeStruct((2, size, 128), F32),
            jax.ShapeDtypeStruct((size + PACK, 2 * dim), BF),
        ),
        in_specs=[smem()] * 3 + [vmem()] * 6 + [hbm()] * 4,
        out_specs=[vmem()] * 3,
        scratch_shapes=[
            pltpu.VMEM((2,) + state[0].shape, F32),
            pltpu.VMEM((2,) + state[1].shape, F32),
            *buffers,
            pltpu.VMEM((2, size, 128), F32),
            *flags,
        ],
        compiler_params=params(*prompt_mine, *prompt_mine, *prompt_mine, *prompt_mine),
        cost_estimate=cost(4e9, 8e6, 2e6),
        name="prompt_forward",
    )(meta, local, table, q_own, ids_rows, *state, in_own, in_other, *prompt_mine, *prompt_theirs)


def join_kernel(wide_in, lse_in, other_ref, o_ref, wide_ref, lse_ref):
    size, dim = wide_in.shape[0], wide_in.shape[1] // 2
    rows_per = size // (2 * dim)
    for h in range(2):
        cols = pl.ds(h * dim, dim)
        first = lse_in[h]
        second = column_of(load_line(other_ref, size + h * 3 * rows_per, size))
        top = jnp.maximum(first, second)
        first, second = jnp.exp2(first - top), jnp.exp2(second - top)
        total = first + second
        other = other_ref[pl.ds(0, size), cols].astype(F32)
        attended = (first * wide_in[:, cols] + second * other) / total
        wide_ref[:, cols] = attended
        o_ref[:, cols] = attended.astype(BF)
        lse_ref[h] = top + jnp.log2(total)


def join_halves(wide_half, lse_half, other):
    return pl.pallas_call(
        join_kernel,
        out_shape=(
            jax.ShapeDtypeStruct(wide_half.shape, BF),
            jax.ShapeDtypeStruct(wide_half.shape, F32),
            jax.ShapeDtypeStruct(lse_half.shape, F32),
        ),
        in_specs=[vmem()] * 3,
        out_specs=[vmem()] * 3,
        compiler_params=params(),
        cost_estimate=cost(4e6, 3e6, 1e6),
        name="join_halves",
    )(wide_half, lse_half, other)


def norm_parts(value):
    center = value - jnp.mean(value, axis=-1, keepdims=True)
    scale = lax.rsqrt(jnp.mean(center * center, axis=-1, keepdims=True) + 1e-05)
    return center * scale, scale


def norm_back(grad, unit, scale, gain):
    part = grad * gain
    return scale * (
        part
        - jnp.mean(part, axis=-1, keepdims=True)
        - unit * jnp.mean(part * unit, axis=-1, keepdims=True)
    )


def feed_kernel(
    meta,
    mine,
    theirs,
    wide_ref,
    lse_ref,
    tok_ref,
    cot_ref,
    down_bias,
    gains,
    shifts,
    w_own,
    w_along,
    w_core,
    w_far,
    out_ref,
    da_ref,
    pack_ref,
    delta_ref,
    w_ref,
    sem,
):
    size, width = tok_ref.shape[1:]
    dim = mine.shape[1] // 2
    heads = w_ref.shape[0]
    hid = (w_ref.shape[1] - PACK - dim) // 2
    batch, parity = meta[1], meta[2]
    even = parity == 0
    for q in range(heads):
        for place, ref in enumerate((w_own, w_along, w_core, w_far)):

            @pl.when((2 * batch + parity) == (q ^ (0, 2, 1, 3)[place]))
            def _():
                pltpu.make_async_copy(ref, w_ref.at[q], sem.at[q]).start()

    place_out = slice(hid, hid + dim)
    place_up = slice(hid + dim, 2 * hid + dim)
    place_bias = 2 * hid + dim
    sub = min(256, size)
    pack_ref[pl.ds(size, STATS), :] = jnp.zeros((STATS, 2 * dim), BF)
    g0, g1 = gains[0:1, :], gains[1:2, :]
    for q in range(heads):
        pltpu.make_async_copy(w_own, w_ref.at[q], sem.at[q]).wait()
    for part in range(size // sub):
        rows = pl.ds(part * sub, sub)
        a, b = mine[rows, :], theirs[rows, :]
        first = jnp.where(even, a, b)
        second = jnp.where(even, b, a)
        attn = mm(first[:, :dim], w_ref[0, place_out, :])
        attn += mm(second[:, :dim], w_ref[1, place_out, :])
        attn += mm(first[:, dim:], w_ref[2, place_out, :])
        attn += mm(second[:, dim:], w_ref[3, place_out, :])
        unit_one, scale_one = norm_parts(tok_ref[batch, rows, :].astype(F32) + attn)
        normed = unit_one * g0 + shifts[0:1, :]
        normed_low = normed.astype(BF)
        branch = down_bias[...]
        slopes = []
        for q in range(heads):
            bias = (
                w_ref[q, place_bias : place_bias + 1, :hid].astype(F32)
                + w_ref[q, place_bias : place_bias + 1, hid : 2 * hid].astype(F32)
                + w_ref[q, place_bias + 1 : place_bias + 2, :hid].astype(F32)
            )
            pre = mm_nt(normed_low, w_ref[q, place_up, :]) + bias
            cdf = 0.5 * (1.0 + lax.erf(pre * 0.7071067811865476))
            slopes.append(cdf + pre * (jnp.exp(-0.5 * pre * pre) * 0.3989422804014327))
            branch = branch + mm((pre * cdf).astype(BF), w_ref[q, :hid, :])
        unit_two, scale_two = norm_parts(normed + branch)
        out_ref[rows, :] = (unit_two * g1 + shifts[1:2, :]).astype(BF)
        grad_mixed = norm_back(cot_ref[batch, rows, :].astype(F32), unit_two, scale_two, g1)
        mixed_low = grad_mixed.astype(BF)
        grad_normed = grad_mixed
        for q in range(heads):
            grad_pre = mm_nt(mixed_low, w_ref[q, :hid, :]) * slopes[q]
            grad_normed = grad_normed + mm(grad_pre.astype(BF), w_ref[q, place_up, :])
        grad_sum = norm_back(grad_normed, unit_one, scale_one, g0)
        da_ref[rows, :] = grad_sum
        sum_low = grad_sum.astype(BF)
        for head in range(2):
            cols = pl.ds(head * dim, dim)
            grad_out = mm_nt(sum_low, w_ref[2 * head + parity, place_out, :]).astype(BF)
            pack_ref[rows, cols] = grad_out
            delta = jnp.sum(grad_out.astype(F32) * wide_ref[rows, cols], axis=1, keepdims=True)
            delta_ref[head, rows, :] = jnp.broadcast_to(delta, (sub, 128))
    row = size
    for head in range(2):
        for ref in (lse_ref, delta_ref):
            row = store_line(pack_ref, row, jnp.transpose(ref[head])[0:1, :])


def feed(meta, mine, theirs, wide_out, lse, tokens, cotangent, w, down_bias, gains, shifts):
    size, width = tokens.shape[1:]
    dim = mine.shape[1] // 2
    return pl.pallas_call(
        feed_kernel,
        out_shape=(
            jax.ShapeDtypeStruct((size, width), BF),
            jax.ShapeDtypeStruct((size, width), F32),
            jax.ShapeDtypeStruct((size + STATS, 2 * dim), BF),
            jax.ShapeDtypeStruct((2, size, 128), F32),
        ),
        in_specs=[smem()] + [vmem()] * 9 + [hbm()] * 4,
        out_specs=[vmem()] * 4,
        scratch_shapes=[pltpu.VMEM((4,) + w[0].shape, BF), pltpu.SemaphoreType.DMA((4,))],
        compiler_params=params(),
        cost_estimate=cost(3e9, 8e6, 1e6),
        name="feed",
    )(meta, mine, theirs, wide_out, lse, tokens, cotangent, down_bias, gains, shifts, *w)


def low_grads(scores, factor, shift, grads, delta):
    count = scores.shape[1] // 128
    probs = jnp.exp2(scores * factor - wide(shift, count))
    return (probs * (grads - wide(delta, count))).astype(BF)


def token_query_grad_kernel(
    data_count,
    factor,
    meta,
    starts,
    q_ref,
    ids_ref,
    lse_ref,
    delta_ref,
    do_ref,
    acc_in,
    in_own,
    in_other,
    mine_low,
    mine_high,
    theirs_low,
    theirs_high,
    dq_ref,
    acc_ref,
    x_ref,
    w_ref,
    id_ref,
    sem,
):
    size, dim = q_ref.shape[1], q_ref.shape[2] // 2
    base = meta[0] * size
    first, last = key_range(starts, base, base + size, data_count)
    first, last = first // size, (last + size - 1) // size
    gathered = (mine_low, mine_high, theirs_low, theirs_high)
    fetch_shards(meta, first, last, gathered, x_ref, sem)
    join_weights(meta, in_own, in_other, w_ref, 1)
    acc_ref[...] = acc_in[...]
    id_ref[...] = column_of(ids_ref[meta[1]])

    def step(shard, carry):
        raw_rows, line = load_shard(meta, shard, gathered, x_ref, sem)
        kv = mm(raw_rows, w_ref[...]).astype(BF)
        mask = wide(id_ref[...], size // 128) == line
        raw, grads, low = [], [], []
        for h in range(2):
            raw.append(mm_nt(q_ref[0, :, h * dim : (h + 1) * dim], kv[:, h * dim : (h + 1) * dim]))
            grads.append(
                mm_nt(
                    do_ref[pl.ds(0, size), h * dim : (h + 1) * dim],
                    kv[:, (2 + h) * dim : (3 + h) * dim],
                )
            )
        for h in range(2):
            scores = jnp.where(mask, raw[h], NEGATIVE)
            low.append(low_grads(scores, factor, lse_ref[h], grads[h], delta_ref[h]))
        for h in range(2):
            acc_ref[h] += mm(low[h], kv[:, h * dim : (h + 1) * dim])
        return carry

    lax.fori_loop(first, last, step, 0)
    for h in range(2):
        dq_ref[:, pl.ds(h * dim, dim)] = acc_ref[h] * dim ** (-0.5)


def token_query_grad(
    meta, starts, q_own, ids_rows, lse, delta, pack, acc, mine, theirs, in_own, in_other, factor, data_count
):
    size, dim = q_own.shape[1], q_own.shape[2] // 2
    width = in_own.shape[1]
    return pl.pallas_call(
        functools.partial(token_query_grad_kernel, data_count, factor),
        out_shape=jax.ShapeDtypeStruct((size, 2 * dim), F32),
        in_specs=[smem()] * 2 + [vmem()] * 8 + [hbm()] * 4,
        out_specs=vmem(),
        scratch_shapes=[
            pltpu.VMEM((2, size, dim), F32),
            shard_scratch(mine),
            pltpu.VMEM((width, 4 * dim), BF),
            pltpu.VMEM((size, 128), F32),
            pltpu.SemaphoreType.DMA((2 * mine[0].shape[0], 2)),
        ],
        compiler_params=params(*mine, *theirs),
        cost_estimate=cost(6e9, 16e6, 4e6),
        name="token_query_grad",
    )(
        meta,
        starts,
        q_own,
        ids_rows,
        lse,
        delta,
        pack,
        acc,
        in_own,
        in_other,
        *mine,
        *theirs,
    )


def prompt_query_grad_kernel(
    block,
    factor,
    meta,
    local,
    table,
    q_ref,
    ids_ref,
    lse_in,
    delta_in,
    pack_own,
    pack_other,
    in_own,
    in_other,
    mine_low,
    mine_high,
    theirs_low,
    theirs_high,
    dq_ref,
    send_ref,
    acc_ref,
    lse_ref,
    delta_ref,
    do_ref,
    raws,
    w_ref,
    kv_ref,
    id_ref,
    state,
    sem,
):
    size, dim = q_ref.shape[1], q_ref.shape[2] // 2
    rows_per = size // (2 * dim)
    sources = (mine_low, mine_high, theirs_low, theirs_high)
    fetch_prompts(meta, local, table, sources, raws, state, sem)
    join_weights(meta, in_own, in_other, w_ref, 1)
    acc_ref[...] = jnp.zeros(acc_ref.shape, F32)
    lse_ref[0] = lse_in[...]
    delta_ref[0] = delta_in[...]
    do_ref[0] = pack_own[pl.ds(0, size), :]
    do_ref[1] = pack_other[pl.ds(0, size), :]
    for h in range(2):
        for kind, ref in enumerate((lse_ref, delta_ref)):
            row = size + (h * 2 + kind) * 3 * rows_per
            ref[1, h] = column_of(load_line(pack_other, row, size))
    for slot in range(2):
        id_ref[slot] = column_of(ids_ref[meta[1] ^ slot])

    def prepare(number):
        project_prompt(meta, number, sources, raws, w_ref, kv_ref, state, sem)

    def update(slot, rows, data, number):
        mask = id_ref[slot, rows, :] == data.astype(F32)
        raw, grads, low = [], [], []
        for h in range(2):
            cols = pl.ds(h * dim, dim)
            raw.append(mm_nt(q_ref[slot, rows, cols], kv_ref[number, :, cols]))
            value = kv_ref[number, :, pl.ds((2 + h) * dim, dim)]
            grads.append(mm_nt(do_ref[slot, rows, cols], value))
        for h in range(2):
            shift = jnp.where(mask, lse_ref[slot, h, rows, :], -NEGATIVE)
            scores = prompt_mask(meta, raw[h], block)
            low.append(low_grads(scores, factor, shift, grads[h], delta_ref[slot, h, rows, :]))
        for h in range(2):
            acc_ref[slot, h, rows, :] += mm(low[h], kv_ref[number, :, pl.ds(h * dim, dim)])

    visit_prompts(meta, local, table, size, prepare, update)
    for h in range(2):
        cols = pl.ds(h * dim, dim)
        dq_ref[h] = acc_ref[0, h]
        send_ref[:, cols] = (acc_ref[1, h] * dim ** (-0.5)).astype(BF)


def prompt_query_grad(
    meta,
    local,
    table,
    q_own,
    ids_rows,
    lse,
    delta,
    pack,
    pack_other,
    prompt_mine,
    prompt_theirs,
    in_own,
    in_other,
    factor,
    block,
):
    size, dim = q_own.shape[1], q_own.shape[2] // 2
    buffers, flags = prompt_scratch(prompt_mine, in_own.shape[1], dim, block)
    return pl.pallas_call(
        functools.partial(prompt_query_grad_kernel, block, factor),
        out_shape=(
            jax.ShapeDtypeStruct((2, size, dim), F32),
            jax.ShapeDtypeStruct((size, 2 * dim), BF),
        ),
        in_specs=[smem()] * 3 + [vmem()] * 8 + [hbm()] * 4,
        out_specs=[vmem()] * 2,
        scratch_shapes=[
            pltpu.VMEM((2, 2, size, dim), F32),
            pltpu.VMEM((2, 2, size, 128), F32),
            pltpu.VMEM((2, 2, size, 128), F32),
            pltpu.VMEM((2, size, 2 * dim), BF),
            *buffers,
            pltpu.VMEM((2, size, 128), F32),
            *flags,
        ],
        compiler_params=params(*prompt_mine, *prompt_mine, *prompt_mine, *prompt_mine),
        cost_estimate=cost(6e9, 16e6, 4e6),
        name="prompt_query_grad",
    )(
        meta,
        local,
        table,
        q_own,
        ids_rows,
        lse,
        delta,
        pack,
        pack_other,
        in_own,
        in_other,
        *prompt_mine,
        *prompt_theirs,
    )


def half_shard(meta, index, q_ref, ids_ref, low_ref, high_ref):
    slots, rows, double = low_ref.shape
    half = q_ref.shape[1]
    size = rows - STATS
    shard, part = index // 2, index % 2
    slot = slot_of(shard ^ meta[0], meta[2], bit_orders(2 * slots))
    other = slot_of(shard ^ meta[0], 1 - meta[2], bit_orders(2 * slots))
    query = q_ref[jnp.where(part == meta[2], slot * 2, other * 2 + 1)]
    in_low = slot < slots
    place_low, place_high = jnp.minimum(slot, slots - 1), jnp.maximum(slot - slots, 0)
    span = pl.ds(pl.multiple_of(part * half, half), half)
    grad = jnp.where(in_low, low_ref[place_low, span, :], high_ref[place_high, span, :])
    line = ids_ref[slot]
    line = jnp.where(part == 0, line[:, :half], line[:, half : 2 * half])
    tail = pl.ds(size, STATS)
    stats = jnp.where(in_low, low_ref[place_low, tail, :], high_ref[place_high, tail, :])
    stats = stats.astype(F32)
    rows_per = size // double

    def stat(head, kind):
        total = 0.0
        for place in range(3):
            row = ((head * 2 + kind) * 3 + place) * rows_per
            term = stats[row : row + 1, :]
            for i in range(1, rows_per):
                term = jnp.where(part == i, stats[row + i : row + i + 1, :], term)
            total = total + term
        return total

    return query, grad, line, stat


def key_update(query, grad, kv_ref, mask, rows_mask, stat, factor, dk_ref, dv_ref):
    dim = query.shape[1] // 2
    cols = [slice(h * dim, (h + 1) * dim) for h in range(2)]
    raw = [mm_nt(kv_ref[:, cols[h]], query[:, cols[h]]) for h in range(2)]
    grads = [mm_nt(kv_ref[:, pl.ds((2 + h) * dim, dim)], grad[:, cols[h]]) for h in range(2)]
    probs, low = [], []
    for h in range(2):
        shift = stat(h, 0)
        scores = raw[h]
        if rows_mask is None:
            shift = jnp.where(mask, shift, -NEGATIVE)
        else:
            scores = jnp.where(rows_mask, scores, NEGATIVE)
        p = jnp.exp2(scores * factor - shift)
        probs.append(p.astype(BF))
        low.append((p * (grads[h] - stat(h, 1))).astype(BF))
    for h in range(2):
        dv_ref[:, cols[h]] += mm(probs[h], grad[:, cols[h]])
        dk_ref[:, cols[h]] += mm(low[h], query[:, cols[h]])


def prompt_grad_kernel(
    data_count,
    factor,
    meta,
    starts,
    table,
    q_ref,
    ids_ref,
    low_ref,
    high_ref,
    own_ref,
    in_own,
    in_other,
    keep_ref,
    send_ref,
    dk_ref,
    dv_ref,
    w_ref,
    kv_ref,
):
    half = q_ref.shape[1]
    block, width = own_ref.shape
    dim = in_own.shape[2]
    number = meta[0] * block // PLEN
    dk_ref[...] = jnp.zeros(dk_ref.shape, F32)
    dv_ref[...] = jnp.zeros(dv_ref.shape, F32)
    join_weights(meta, in_own, in_other, w_ref, 1)
    kv_ref[...] = mm(own_ref[...].astype(BF), w_ref[...]).astype(BF)

    def visit(data, carry):
        begin, end = starts[data], starts[data + 1]

        @pl.when((table[meta[1], data] == number) & (begin < end))
        def _():
            def step(index, inner):
                query, grad, line, stat = half_shard(meta, index, q_ref, ids_ref, low_ref, high_ref)
                key_update(
                    query, grad, kv_ref, line == data.astype(F32), None, stat, factor, dk_ref, dv_ref
                )
                return inner

            lax.fori_loop(begin // half, (end + half - 1) // half, step, 0)

        return carry

    lax.fori_loop(0, data_count, visit, 0)
    grads = jnp.concatenate(
        [(dk_ref[...] * dim ** (-0.5)).astype(BF), dv_ref[...].astype(BF)], axis=1
    )
    split = width // 2
    parity = meta[2]
    send = w_ref[pl.ds(pl.multiple_of((1 - parity) * split, split), split), :]
    keep = w_ref[pl.ds(pl.multiple_of(parity * split, split), split), :]
    send_ref[...] = mm_nt(grads, send).astype(BF)
    keep_ref[...] = mm_nt(grads, keep)


def prompt_grad(meta, starts, table, q_all, ids_all, packs, own, in_own, in_other, factor, data_count):
    block, width = own.shape
    dim = in_own.shape[2]
    return pl.pallas_call(
        functools.partial(prompt_grad_kernel, data_count, factor),
        out_shape=(
            jax.ShapeDtypeStruct((block, width // 2), F32),
            jax.ShapeDtypeStruct((block, width // 2), BF),
        ),
        in_specs=[smem()] * 3 + [vmem()] * 7,
        out_specs=[vmem(), vmem()],
        scratch_shapes=[
            pltpu.VMEM((block, 2 * dim), F32),
            pltpu.VMEM((block, 2 * dim), F32),
            pltpu.VMEM((width, 4 * dim), BF),
            pltpu.VMEM((block, 4 * dim), BF),
        ],
        compiler_params=params(q_all, *packs),
        cost_estimate=cost(6e9, 16e6, 4e6),
        name="prompt_grad",
    )(meta, starts, table, q_all, ids_all, *packs, own, in_own, in_other)


def token_grad_kernel(
    data_count,
    factor,
    meta,
    starts,
    q_ref,
    ids_ref,
    low_ref,
    high_ref,
    tok_ref,
    own_ids,
    dq_ref,
    dq_other,
    in_own,
    in_other,
    out_ref,
    dk_ref,
    dv_ref,
    w_ref,
    kv_ref,
    id_ref,
):
    size = tok_ref.shape[1]
    half = q_ref.shape[1]
    dim = in_own.shape[2]
    base = meta[0] * size
    first, last = key_range(starts, base, base + size, data_count)
    dk_ref[...] = jnp.zeros(dk_ref.shape, F32)
    dv_ref[...] = jnp.zeros(dv_ref.shape, F32)
    join_weights(meta, in_own, in_other, w_ref, 0)
    kv_ref[...] = mm(tok_ref[meta[1]], w_ref[:, 2 * dim :]).astype(BF)
    id_ref[...] = column_of(own_ids[meta[1]])

    def step(index, carry):
        query, grad, line, stat = half_shard(meta, index, q_ref, ids_ref, low_ref, high_ref)
        mask = wide(id_ref[...], half // 128) == line
        key_update(query, grad, kv_ref, None, mask, stat, factor, dk_ref, dv_ref)
        return carry

    lax.fori_loop(first // half, (last + half - 1) // half, step, 0)
    dq = (dq_ref[...] + dq_other[...].astype(F32)).astype(BF)
    grads = jnp.concatenate(
        [dq, (dk_ref[...] * dim ** (-0.5)).astype(BF), dv_ref[...].astype(BF)], axis=1
    )
    out_ref[...] = mm_nt(grads, w_ref[...]).astype(BF)


def token_grad(
    meta, starts, q_all, ids_all, packs, tokens, ids_rows, dq, in_own, in_other, factor, data_count
):
    size, width = tokens.shape[1:]
    dim = in_own.shape[2]
    return pl.pallas_call(
        functools.partial(token_grad_kernel, data_count, factor),
        out_shape=jax.ShapeDtypeStruct((size, width), BF),
        in_specs=[smem()] * 2 + [vmem()] * 10,
        out_specs=vmem(),
        scratch_shapes=[
            pltpu.VMEM((size, 2 * dim), F32),
            pltpu.VMEM((size, 2 * dim), F32),
            pltpu.VMEM((width, 6 * dim), BF),
            pltpu.VMEM((size, 4 * dim), BF),
            pltpu.VMEM((size, 128), F32),
        ],
        compiler_params=params(spare=VMEM_LIMIT),
        cost_estimate=cost(4e9, 16e6, 4e6),
        name="token_grad",
    )(meta, starts, q_all, ids_all, *packs, tokens, ids_rows, *dq, in_own, in_other)


def sum_prompt_kernel(a_ref, b_ref, sum_ref, square_ref):
    low = (a_ref[...].astype(F32) + b_ref[...].astype(F32)).astype(BF)
    sum_ref[...] = low
    value = low.astype(F32)
    square_ref[...] = jnp.broadcast_to(jnp.sum(value * value, keepdims=True), square_ref.shape)


def sum_prompt(a, b):
    return pl.pallas_call(
        sum_prompt_kernel,
        out_shape=(
            jax.ShapeDtypeStruct(a.shape, BF),
            jax.ShapeDtypeStruct((8, 128), F32),
        ),
        in_specs=[vmem(), vmem()],
        out_specs=[vmem(), vmem()],
        compiler_params=params(),
        cost_estimate=cost(4 * a.size, 6 * a.size),
        name="sum_prompt",
    )(a, b)


def optimizer_kernel(
    meta,
    biases,
    mine,
    theirs,
    squares,
    prompts,
    one_in,
    two_in,
    clip_out,
    one_out,
    two_out,
    new_out,
    held,
    sem,
):
    even = meta[2] == 0
    block = prompts.shape[0]
    tiles = sem.shape[1]
    tile = block // tiles
    norm = jnp.sqrt(squares[0:1, :])
    factor = jnp.minimum(1.0, CLIP_NORM / (norm + 1e-06))
    copies = []
    for index in range(tiles):
        rows = pl.ds(index * tile, tile)
        a, b = mine[rows, :].astype(F32), theirs[rows, :].astype(F32)
        grads = jnp.concatenate([jnp.where(even, a, b), jnp.where(even, b, a)], axis=1)
        clipped = grads * wide(factor, grads.shape[1] // 128)
        new_one = BETA_ONE * one_in[rows, :] + (1.0 - BETA_ONE) * clipped
        new_two = BETA_TWO * two_in[rows, :] + (1.0 - BETA_TWO) * clipped * clipped
        first_hat = new_one / biases[0]
        second_hat = new_two / biases[1]
        held[0, rows, :] = clipped
        held[1, rows, :] = new_one
        held[2, rows, :] = new_two
        held[3, rows, :] = prompts[rows, :] * (
            1.0 - LEARNING_RATE * DECAY_RATE
        ) - LEARNING_RATE * first_hat / (jnp.sqrt(second_hat) + EPSILON)
        for place, out in enumerate((clip_out, one_out, two_out, new_out)):
            copies.append(
                pltpu.make_async_copy(held.at[place, rows], out.at[rows], sem.at[place, index])
            )
            copies[-1].start()
    for copy in copies:
        copy.wait()


def optimizer(meta, biases, mine, theirs, squares, prompts, moment_one, moment_two):
    block, width = prompts.shape
    tiles = 5 if block % 40 == 0 else 1
    shape = jax.ShapeDtypeStruct((block, width), F32)
    return pl.pallas_call(
        optimizer_kernel,
        out_shape=(shape,) * 4,
        in_specs=[smem(), smem()] + [vmem()] * 6,
        out_specs=[hbm()] * 4,
        scratch_shapes=[
            pltpu.VMEM((4, block, width), F32),
            pltpu.SemaphoreType.DMA((4, tiles)),
        ],
        compiler_params=params(prompts, prompts),
        cost_estimate=cost(20 * block * width, 32 * block * width),
        name="optimizer",
    )(meta, biases, mine, theirs, squares, prompts, moment_one, moment_two)


def per_device(
    tokens,
    cotangent,
    dataset_ids,
    prompt_map,
    attn_in,
    attn_out,
    up_weight,
    up_bias,
    down_weight,
    down_bias,
    norm_gains,
    norm_shifts,
    prompts,
    moment_one,
    moment_two,
    step_count,
):
    size, width = tokens.shape[1:]
    dim = attn_in.shape[2]
    hid = up_weight.shape[1]
    data_count = prompt_map.shape[1]
    row_count = lax.axis_size("rows")
    head_count = lax.axis_size("head")
    factor = dim ** (-0.5) * LOG2E
    row = lax.axis_index("rows")
    head = lax.axis_index("head")
    batch, parity = head // 2, head % 2
    half = size // 2
    meta = jnp.stack([row, batch, parity]).astype(jnp.int32)

    block = prompts.shape[0]

    part = half_rows(block)
    prompt_own = lax.dynamic_slice(
        prompts, (batch * (block - part), parity * (width // 2)), (part, width // 2)
    ).astype(BF)
    in_other = swap_head(attn_in, 2, head_count)
    ids = jnp.where(batch == 0, dataset_ids[0], dataset_ids[1])
    tok_half = lax.dynamic_slice(tokens, (batch, parity * half, 0), (1, half, width))[0]
    id_rows = jnp.broadcast_to(ids.astype(BF)[None, :], (PACK, size))
    shard = jnp.concatenate([tok_half, id_rows], axis=0)

    bias_high = lax.reduce_precision(up_bias, 8, 7)
    bias_rest = up_bias - bias_high
    bias_mid = lax.reduce_precision(bias_rest, 8, 7)
    bias_low = bias_rest - bias_mid
    bias_rows = jnp.concatenate([bias_high, bias_mid, bias_low, bias_low]).astype(BF)
    bias_rows = jnp.pad(bias_rows.reshape(-1, width), ((0, PACK - 4 * hid // width), (0, 0)))
    w_own = jnp.concatenate([down_weight, attn_out, up_weight.T, bias_rows], axis=0)
    in_other, w_own = lax.optimization_barrier((in_other, w_own))
    w_along = swap_head(w_own, 2, head_count)
    step_value = step_count.astype(F32)
    biases = jnp.stack(
        [1.0 - jnp.power(BETA_ONE, step_value), 1.0 - jnp.power(BETA_TWO, step_value)]
    )
    numbers = jnp.arange(data_count + 1, dtype=jnp.int32)
    local = jnp.sum((dataset_ids[:, None, :] < numbers[None, :, None]).astype(jnp.int32), axis=2)
    ids_rows = dataset_ids.astype(F32).reshape(2, 1, size)
    tied = {}

    orders, later = bit_orders(row_count), prompt_orders(row_count)
    stages = len(orders[0])
    held, prompt_held = shard[None], prompt_own[None]

    def prompt_stage(place):
        other = gather_stage(prompt_held, place, later, row_count, head_count)
        return jnp.concatenate([prompt_held, other], axis=0)

    for place in range(stages):
        if place == stages - 1:
            held, in_other, w_along, meta, (biases, local, ids_rows) = lax.optimization_barrier(
                (held, in_other, w_along, meta, (biases, local, ids_rows))
            )
        if place != 1:
            held, prompt_held = lax.optimization_barrier((held, prompt_held))
        other = gather_stage(held, place, orders, row_count, head_count)
        if place != 1:
            prompt_held = prompt_stage(max(place - 1, 0))
        if place < stages - 1:
            held = jnp.concatenate([held, other], axis=0)
        if place == 0:
            held, prompt_held = lax.optimization_barrier((held, prompt_held))
    theirs_low = swap_head(held, 1, head_count)
    other, prompt_held = lax.optimization_barrier((other, prompt_held))
    mine = (held, other)
    prompt_high = gather_stage(prompt_held, stages - 1, later, row_count, head_count)
    theirs = (theirs_low, swap_head(other, 1, head_count))
    w_core = swap_head(w_own, 1, head_count)
    w_far = swap_head(w_along, 1, head_count)

    ids_all = jnp.concatenate([bank[:, half, :size] for bank in mine], axis=0).astype(F32)
    starts = jnp.sum(
        (ids_all.reshape(1, -1) < numbers.astype(F32)[:, None]).astype(jnp.int32), axis=1
    )
    ids_all = ids_all.reshape(row_count, 1, size)
    q_own, *state = token_forward(
        meta, starts, tokens, ids_rows, mine, theirs, attn_in, in_other, factor, data_count
    )
    prompt_theirs_low = swap_head(prompt_held, 1, head_count)
    prompt_high, state, prompt_theirs_low, w_core, w_far = lax.optimization_barrier(
        (prompt_high, state, prompt_theirs_low, w_core, w_far)
    )
    prompt_mine = (prompt_held, prompt_high)
    prompt_theirs = (prompt_theirs_low, swap_head(prompt_high, 1, head_count))
    wide_half, lse_half, send_half = prompt_forward(
        meta,
        local,
        prompt_map,
        q_own,
        ids_rows,
        state,
        prompt_mine,
        prompt_theirs,
        attn_in,
        in_other,
        factor,
        block,
    )
    o_mine, wide_out, lse = join_halves(wide_half, lse_half, swap_head(send_half, 2, head_count))
    o_theirs = swap_head(o_mine, 1, head_count)
    out, grad_sum, pack, delta = feed(
        meta,
        o_mine,
        o_theirs,
        wide_out,
        lse,
        tokens,
        cotangent,
        (w_own, w_along, w_core, w_far),
        down_bias.reshape(1, width),
        norm_gains,
        norm_shifts,
    )
    pack_other = swap_head(pack, 2, head_count)

    def tie_query_grads(stages_left, held):
        if stages_left == 3:
            held, here = lax.optimization_barrier((held, in_other))
            tied["q"] = project_query(meta, mine, theirs, attn_in, here)
        if stages_left == 2:
            held, other, tied["q"] = lax.optimization_barrier((held, pack_other, tied["q"]))
            tied["dq"] = prompt_query_grad(
                meta,
                local,
                prompt_map,
                q_own,
                ids_rows,
                lse,
                delta,
                pack,
                other,
                prompt_mine,
                prompt_theirs,
                attn_in,
                in_other,
                factor,
                block,
            )
        if stages_left == 1:
            held, (acc, dq_send) = lax.optimization_barrier((held, tied["dq"]))
            tied["dq_other"] = swap_head(dq_send, 2, head_count)
            tied["dq"] = token_query_grad(
                meta,
                starts,
                q_own,
                ids_rows,
                lse,
                delta,
                pack,
                acc,
                mine,
                theirs,
                attn_in,
                in_other,
                factor,
                data_count,
            )
        return held

    out_half = lax.dynamic_slice_in_dim(out, parity * half, half, 0)
    out_half = swap_head(out_half, 2, head_count)
    packs = gather_rows(pack, row_count, head_count, tie_query_grads)
    q_all = tied["q"]
    packs, dq, dq_other, out_half = lax.optimization_barrier(
        (packs, tied["dq"], tied["dq_other"], out_half)
    )
    keep, send = prompt_grad(
        meta, starts, prompt_map, q_all, ids_all, packs, prompts, attn_in, in_other, factor, data_count
    )

    pair = keep + swap_head(send, 1, head_count).astype(F32)
    pair_low = lax.reduce_precision(pair, 8, 7).astype(BF)
    dq, pair_low = lax.optimization_barrier((dq, pair_low))
    pair_other = swap_head(pair_low, 2, head_count)
    out_rest = swap_head(out_half, 1, head_count)
    token_part = token_grad(
        meta,
        starts,
        q_all,
        ids_all,
        packs,
        tokens,
        ids_rows,
        (dq, dq_other),
        attn_in,
        in_other,
        factor,
        data_count,
    )
    token_part, pair_other = lax.optimization_barrier((token_part, pair_other))
    full_low, squares = sum_prompt(pair_low, pair_other)
    full_other = swap_head(full_low, 1, head_count)

    def both_batches(own, here, rest):
        other = jnp.concatenate(
            [jnp.where(parity == 0, here, rest), jnp.where(parity == 0, rest, here)], axis=0
        )
        first = jnp.where(batch == 0, own, other)
        return jnp.stack([first, jnp.where(batch == 0, other, own)]).astype(F32)

    core_sum = token_part.astype(F32) + swap_head(token_part, 1, head_count).astype(F32)
    total = lax.reduce_precision(grad_sum + core_sum, 8, 7).astype(BF)
    mine_half = lax.dynamic_slice_in_dim(total, parity * half, half, 0)
    other_half = swap_head(mine_half, 2, head_count)
    layer_out = both_batches(out, out_half, out_rest)

    def tie_sum(stages_done, value):
        if stages_done == 1:
            value, _ = lax.optimization_barrier((value, total))
        if stages_done == 2:
            value, tied["half"], tied["out"] = lax.optimization_barrier(
                (value, other_half, layer_out)
            )
        return value

    squares = xor_sum(squares, row_count, head_count, tie_sum)
    other_half, layer_out = tied["half"], tied["out"]
    input_grad = both_batches(total, other_half, swap_head(other_half, 1, head_count))
    clipped, new_one, new_two, new_prompts = optimizer(
        meta, biases, full_low, full_other, squares, prompts, moment_one, moment_two
    )
    return (layer_out, input_grad, clipped, jnp.sqrt(squares[0, 0]), new_one, new_two, new_prompts)


def solution(mesh):
    in_specs = (
        P(None, "rows", None),
        P(None, "rows", None),
        P(None, "rows"),
        P(),
        P(None, None, "head"),
        P("head", None),
        P(None, "head"),
        P("head"),
        P("head", None),
        P(),
        P(),
        P(),
        P("rows", None),
        P("rows", None),
        P("rows", None),
        P(),
    )
    out_specs = (
        P(None, "rows", None),
        P(None, "rows", None),
        P("rows", None),
        P(),
        P("rows", None),
        P("rows", None),
        P("rows", None),
    )
    return jax.shard_map(
        per_device, mesh=mesh, in_specs=in_specs, out_specs=out_specs, check_vma=False
    )
```

time: 251 us -> 219 us (0.87)
  waiting for transfers between devices: 105 us -> 83.8 us
  other arithmetic: 21.5 us -> 8.23 us
  between operations: 17.2 us -> 4.19 us
  starting transfers between devices: 40.1 us -> 48.5 us
  Pallas kernels: 47.6 us -> 53.9 us
    ppermute x9 -> x15, waiting for transfers between devices: 70 us -> 54.3 us  [the longest x9 48.1 us: gather_stage(): return lax.ppermute(held, BOTH, pairs)]
    all_gather x1 -> x0, waiting for transfers between devices: 13.1 us -> none  [per_device(): prompt_all = lax.all_gather(prompt_own, BOTH, axis=0, tiled=False)]
    ppermute x9 -> x15, starting transfers between devices: 23 us -> 32.8 us  [the longest x9 17.1 us: gather_stage(): return lax.ppermute(held, BOTH, pairs)]
    ppermute x14 -> x20, waiting for transfers between devices: 21.6 us -> 29.5 us  [swap_head(): lax.ppermute(value, 'head', [(i, i ^ mask) for i in range(head_count)])]
    sub x1 -> x0, other arithmetic: 5.69 us -> none  [per_device(): prompts * (1.0 - LEARNING_RATE * DECAY_RATE)]
    another operation x6 -> x4, other arithmetic: 4.27 us -> 0.96 us  [the longest x1 0.56 us: per_device(): jnp.stack([1.0 - jnp.power(BETA_ONE, step_value), 1.0 - jnp.power(BETA_TW...]
    pallas_call x2 -> x6, Pallas kernels: 24.6 us -> 26.5 us  [the longest x1 7.89 us: prompt_forward(): pl.pallas_call(functools.partial(prompt_forward_kernel, block, factor), o...]
    ppermute x14 -> x20, starting transfers between devices: 17.1 us -> 15.7 us  [swap_head(): lax.ppermute(value, 'head', [(i, i ^ mask) for i in range(head_count)])]
  transfers between devices with their start and end apart: 24 -> 35, of which waited for: 12 -> 22; matrix products, arithmetic and copies ran while one was open for 9% -> 3% of each run, Pallas kernels for 16% -> 15%
where the time goes in v1:
time: 219 us; the launch traced here: 216 us
  waiting for transfers between devices  83.8 us (38%)
  Pallas kernels  53.9 us (25%)
  starting transfers between devices  48.5 us (22%)
  local copies, waits for them, and re-layouts  17.6 us (8%)
  other arithmetic  8.23 us (4%)
  between operations  4.19 us (2%)
    ppermute x9, waiting for transfers between devices, gather_stage(): return lax.ppermute(held, BOTH, pairs)  48.1 us
    ppermute x20, waiting for transfers between devices, swap_head(): lax.ppermute(value, 'head', [(i, i ^ mask) for i in range(head_count)])  29.5 us
    ppermute x9, starting transfers between devices, gather_stage(): return lax.ppermute(held, BOTH, pairs)  17.1 us
    ppermute x6, starting transfers between devices, moved(): return lax.ppermute(value, BOTH, [(i, i ^ mask) for i in range(count)])  15.7 us
    ppermute x20, starting transfers between devices, swap_head(): lax.ppermute(value, 'head', [(i, i ^ mask) for i in range(head_count)])  15.7 us
    unnamed x148, local copies, waits for them, and re-layouts  14.3 us
    pallas_call x1, Pallas kernels, feed(): pl.pallas_call(feed_kernel, out_shape=(jax.ShapeDtypeStruct((size, width)...  8.06 us
    pallas_call x1, Pallas kernels, prompt_forward(): pl.pallas_call(functools.partial(prompt_forward_kernel, block, factor), o...  7.89 us
  transfers between devices with their start and end apart: 35, of which 22 were waited for; matrix products, arithmetic and copies ran while one was open for 3% of the time, Pallas kernels for 15%

profile of v1, /device:TPU:0, one launch (start us, length us, event | category | flops | bytes accessed | tf_op | source)
XLA Modules:
  0.0 216.2 jit_solution(15368767480585940503)
XLA Ops:
  3.6 4.1 %collective-permute-start.1 = (bf16[1,512,256]{2,1,0:T(8,128)(2,1)S(1)}, bf16[1,512,256]{2,1,0:T(8,128)(2,1)S(1)}, u32[]{:S(2)}, u32[]{:S(2)}) collective-permute-start(bf16[1,512,256]{2,1,0:T(8,128)(2,1)S(1)} %fusion.2), channel_id=1, source_target_pairs={{0,16},{1,9},{2,18},{3,11},{4,20},{5,13},{6,22},{7,15},{8,24},{9,1... | collective-permute-start | bytes 786440 | tf_op jit(solution)/shard_map/ppermute | solution.py:83
  11.5 8.8 %collective-permute-done.1 = bf16[1,512,256]{2,1,0:T(8,128)(2,1)S(1)} collective-permute-done((bf16[1,512,256]{2,1,0:T(8,128)(2,1)S(1)}, bf16[1,512,256]{2,1,0:T(8,128)(2,1)S(1)}, u32[]{:S(2)}, u32[]{:S(2)}) %collective-permute-start.1) | collective-permute-done | bytes 262176 | tf_op jit(solution)/shard_map/ppermute | solution.py:83
  22.2 2.1 collective-permute-start.4
  26.0 11.6 %collective-permute-done.2 = bf16[2,272,512]{2,1,0:T(8,128)(2,1)S(1)} collective-permute-done((bf16[2,272,512]{2,1,0:T(8,128)(2,1)S(1)}, bf16[2,272,512]{2,1,0:T(8,128)(2,1)S(1)}, u32[]{:S(2)}, u32[]{:S(2)}) %collective-permute-start.2) | collective-permute-done | bytes 557088 | tf_op jit(solution)/shard_map/ppermute | solution.py:83
  42.4 13.3 %collective-permute-done.6 = bf16[2,512,256]{2,1,0:T(8,128)(2,1)S(1)} collective-permute-done((bf16[2,512,256]{2,1,0:T(8,128)(2,1)}, bf16[2,512,256]{2,1,0:T(8,128)(2,1)S(1)}, u32[]{:S(2)}, u32[]{:S(2)}) %collective-permute-start.6) | collective-permute-done | bytes 524320 | tf_op jit(solution)/shard_map/ppermute | solution.py:83
  56.8 3.2 %collective-permute-done.5.mine_high.c = bf16[4,272,512]{2,1,0:T(8,128)(2,1)S(1)} collective-permute-done((bf16[4,272,512]{2,1,0:T(8,128)(2,1)S(1)}, bf16[4,272,512]{2,1,0:T(8,128)(2,1)S(1)}, u32[]{:S(2)}, u32[]{:S(2)}) %collective-permute-start.5) | collective-permute-done | bytes 1114144 | tf_op jit(solution)/shard_map/ppermute | solution.py:83
  62.8 4.5 %token_forward.1 = (bf16[2,512,256]{2,1,0:T(8,128)(2,1)S(1)}, f32[2,512,128]{2,1,0:T(8,128)S(1)}, f32[2,512,256]{2,1,0:T(8,128)S(1)}) custom-call(s32[3]{0:T(128)S(1)} %pad_add_fusion.meta, s32[17]{0:T(128)S(1)} %convert_reduce_fusion.starts, f32[2,1,512]{2,1,0:T(1,128)S(1)} %reshape.66.ids_ref.own_ids, bf16[3,512,128]{2,1,0:T(8,128)(2,1)S(1)} %copy-done.22, ...), custom_call_target="tpu_custom_call" | custom-call | flops 8000000000 | bytes 8000000 | tf_op jit(solution)/shard_map/token_forward/pallas_call | solution.py:324
  72.7 2.8 %collective-permute-done.9.mine_high = bf16[4,512,256]{2,1,0:T(8,128)(2,1)} collective-permute-done((bf16[4,512,256]{2,1,0:T(8,128)(2,1)S(1)}, bf16[4,512,256]{2,1,0:T(8,128)(2,1)}, u32[]{:S(2)}, u32[]{:S(2)}) %collective-permute-start.9) | collective-permute-done | bytes 1048608 | tf_op jit(solution)/shard_map/ppermute | solution.py:83
  75.5 2.9 %collective-permute-done.13.theirs_high = bf16[4,512,256]{2,1,0:T(8,128)(2,1)} collective-permute-done((bf16[4,512,256]{2,1,0:T(8,128)(2,1)}, bf16[4,512,256]{2,1,0:T(8,128)(2,1)}, u32[]{:S(2)}, u32[]{:S(2)}) %collective-permute-start.13) | collective-permute-done | bytes 1048608 | tf_op jit(solution)/shard_map/ppermute | solution.py:122
  86.2 7.9 %prompt_forward.1 = (f32[512,256]{1,0:T(8,128)S(1)}, f32[2,512,128]{2,1,0:T(8,128)S(1)}, bf16[528,256]{1,0:T(8,128)(2,1)S(1)}) custom-call(s32[3]{0:T(128)S(1)} %pad_add_fusion.meta, s32[2,17]{1,0:T(2,128)S(1)} %copy.41.local, s32[2,16]{1,0:T(2,128)S(1)} %copy-done.52, bf16[2,512,256]{2,1,0:T(8,128)(2,1)S(1)} %copy-done.58, ...), custom_call_target="tpu_custom_call" | custom-call | flops 4000000000 | bytes 8000000 | tf_op jit(solution)/shard_map/prompt_forward/pallas_call | solution.py:549
  94.2 2.2 %collective-permute-start.14 = (bf16[528,256]{1,0:T(8,128)(2,1)S(1)}, bf16[528,256]{1,0:T(8,128)(2,1)S(1)}, u32[]{:S(2)}, u32[]{:S(2)}) collective-permute-start(bf16[528,256]{1,0:T(8,128)(2,1)S(1)} %get-tuple-element.99), channel_id=1, source_target_pairs={{0,2},{1,3},{2,0},{3,1},{4,6},{5,7},{6,4},{7,5},{8,10},{9,11},{10,... | collective-permute-start | bytes 811016 | tf_op jit(solution)/shard_map/ppermute | solution.py:122
  96.4 6.8 %collective-permute-done.14.other_ref = bf16[528,256]{1,0:T(8,128)(2,1)S(1)} collective-permute-done((bf16[528,256]{1,0:T(8,128)(2,1)S(1)}, bf16[528,256]{1,0:T(8,128)(2,1)S(1)}, u32[]{:S(2)}, u32[]{:S(2)}) %collective-permute-start.14) | collective-permute-done | bytes 270368 | tf_op jit(solution)/shard_map/ppermute | solution.py:122
  105.2 8.1 %feed.1 = (bf16[512,512]{1,0:T(8,128)(2,1)S(1)}, f32[512,512]{1,0:T(8,128)S(1)}, bf16[544,256]{1,0:T(8,128)(2,1)S(1)}, f32[2,512,128]{2,1,0:T(8,128)S(1)}) custom-call(s32[3]{0:T(128)S(1)} %pad_add_fusion.meta, bf16[512,256]{1,0:T(8,128)(2,1)S(1)} %get-tuple-element.100.mine, bf16[512,256]{1,0:T(8,128)(2,1)S(1)} %collective-permute-done.15.theirs, ...), custom_call_target="tpu_custom_call" | custom-call | flops 3000000000 | bytes 8000000 | tf_op jit(solution)/shard_map/feed/pallas_call | solution.py:712
  115.6 2.5 %project_query.1 = bf16[2,4,2,256,256]{4,3,2,1,0:T(8,128)(2,1)S(1)} custom-call(s32[3]{0:T(128)S(1)} %pad_add_fusion.meta, bf16[4,272,512]{2,1,0:T(8,128)(2,1)S(1)} %pad_maximum_fusion.mine_low.a, bf16[4,272,512]{2,1,0:T(8,128)(2,1)S(1)} %collective-permute-done.7.theirs_low.b, bf16[4,272,512]{2,1,0:T(8,128)(2,1)S(1)} %collective-permute-done.5.mine_high.c, ...), custom_call_target="tpu_custom_call" | custom-call | flops 1073741824 | bytes 4194304 | tf_op jit(solution)/shard_map/project_query/pallas_call | solution.py:170
  120.0 2.5 %collective-permute-done.17.pack_other = bf16[544,256]{1,0:T(8,128)(2,1)S(1)} collective-permute-done((bf16[544,256]{1,0:T(8,128)(2,1)S(1)}, bf16[544,256]{1,0:T(8,128)(2,1)S(1)}, u32[]{:S(2)}, u32[]{:S(2)}) %collective-permute-start.17) | collective-permute-done | bytes 278560 | tf_op jit(solution)/shard_map/ppermute | solution.py:122
  122.6 2.9 %collective-permute-start.18 = (bf16[2,544,256]{2,1,0:T(8,128)(2,1)S(1)}, bf16[2,544,256]{2,1,0:T(8,128)(2,1)S(1)}, u32[]{:S(2)}, u32[]{:S(2)}) collective-permute-start(bf16[2,544,256]{2,1,0:T(8,128)(2,1)S(1)} %pad_maximum_fusion.4), channel_id=1, source_target_pairs={{0,16},{1,9},{2,18},{3,11},{4,20},{5,13},{6,22},{7,15},{8,24},{9,1... | collective-permute-start | bytes 1671176 | tf_op jit(solution)/shard_map/ppermute | solution.py:83
  125.5 7.6 %prompt_query_grad.1 = (f32[2,512,128]{2,1,0:T(8,128)S(1)}, bf16[512,256]{1,0:T(8,128)(2,1)S(1)}) custom-call(s32[3]{0:T(128)S(1)} %pad_add_fusion.meta, s32[2,17]{1,0:T(2,128)S(1)} %copy.41.local, s32[2,16]{1,0:T(2,128)S(1)} %copy-done.52, bf16[2,512,256]{2,1,0:T(8,128)(2,1)S(1)} %copy-done.59, f32[2,1,512]{2,1,0:T(1,128)S(1)} %reshape.66.ids_ref.own_ids, ...), custom_call_target="tpu_custom_call" | custom-call | flops 6000000000 | bytes 16000000 | tf_op jit(solution)/shard_map/prompt_query_grad/pallas_call | solution.py:922
  133.1 5.0 %collective-permute-done.18 = bf16[2,544,256]{2,1,0:T(8,128)(2,1)S(1)} collective-permute-done((bf16[2,544,256]{2,1,0:T(8,128)(2,1)S(1)}, bf16[2,544,256]{2,1,0:T(8,128)(2,1)S(1)}, u32[]{:S(2)}, u32[]{:S(2)}) %collective-permute-start.18) | collective-permute-done | bytes 557088 | tf_op jit(solution)/shard_map/ppermute | solution.py:83
  138.2 3.2 %collective-permute-start.19 = (bf16[4,544,256]{2,1,0:T(8,128)(2,1)S(1)}, bf16[4,544,256]{2,1,0:T(8,128)(2,1)S(1)}, u32[]{:S(2)}, u32[]{:S(2)}) collective-permute-start(bf16[4,544,256]{2,1,0:T(8,128)(2,1)S(1)} %pad_maximum_fusion.1.low_ref), channel_id=1, source_target_pairs={{0,8},{1,5},{2,10},{3,7},{4,12},{5,1},{6,14},{7,3},{8,0},{9,13},{1... | collective-permute-start | bytes 3342344 | tf_op jit(solution)/shard_map/ppermute | solution.py:83
  143.7 4.5 %token_query_grad.1.dq_ref = f32[512,256]{1,0:T(8,128)S(1)} custom-call(s32[3]{0:T(128)S(1)} %copy-done.33, s32[17]{0:T(128)S(1)} %copy-done.39, bf16[2,512,256]{2,1,0:T(8,128)(2,1)S(1)} %copy-done.59, f32[2,1,512]{2,1,0:T(1,128)S(1)} %copy-done.36, f32[2,512,128]{2,1,0:T(8,128)S(1)} %get-tuple-element.102.lse_ref.lse_in, ...), custom_call_target="tpu_custom_call" | custom-call | flops 6000000000 | bytes 16000000 | tf_op jit(solution)/shard_map/token_query_grad/pallas_call | solution.py:799
  148.2 2.4 %collective-permute-done.21 = bf16[256,512]{1,0:T(8,128)(2,1)S(1)} collective-permute-done((bf16[256,512]{1,0:T(8,128)(2,1)S(1)}, bf16[256,512]{1,0:T(8,128)(2,1)S(1)}, u32[]{:S(2)}, u32[]{:S(2)}) %collective-permute-start.21) | collective-permute-done | bytes 262176 | tf_op jit(solution)/shard_map/ppermute | solution.py:122
  150.6 2.8 %collective-permute-done.20.dq_other = bf16[512,256]{1,0:T(8,128)(2,1)S(1)} collective-permute-done((bf16[512,256]{1,0:T(8,128)(2,1)S(1)}, bf16[512,256]{1,0:T(8,128)(2,1)S(1)}, u32[]{:S(2)}, u32[]{:S(2)}) %collective-permute-start.20) | collective-permute-done | bytes 262176 | tf_op jit(solution)/shard_map/ppermute | solution.py:122
  155.0 5.0 %prompt_grad.1 = (f32[1000,256]{1,0:T(8,128)S(1)}, bf16[1000,256]{1,0:T(8,128)(2,1)S(1)}) custom-call(s32[3]{0:T(128)S(1)} %copy-done.33, s32[17]{0:T(128)S(1)} %copy-done.39, s32[2,16]{1,0:T(2,128)S(1)} %copy-done.53, bf16[16,256,256]{2,1,0:T(8,128)(2,1)S(1)} %bitcast.33, f32[8,1,512]{2,1,0:T(1,128)S(1)} %maximum_convert_fusion.2.ids_ref, ...), custom_call_target="tpu_custom_call" | custom-call | flops 6000000000 | bytes 16000000 | tf_op jit(solution)/shard_map/prompt_grad/pallas_call | solution.py:1072
  162.1 4.8 %collective-permute-start.23 = (bf16[1000,256]{1,0:T(8,128)(2,1)S(1)}, bf16[1000,256]{1,0:T(8,128)(2,1)}, u32[]{:S(2)}, u32[]{:S(2)}) collective-permute-start(bf16[1000,256]{1,0:T(8,128)(2,1)S(1)} %reduce-precision_convert_fusion.1.a_ref), channel_id=1, source_target_pairs={{0,2},{1,3},{2,0},{3,1},{4,6},{5,7},{6,4},{7,5},{8,10},{9,11},{10,... | collective-permute-start | bytes 1536008 | tf_op jit(solution)/shard_map/ppermute | solution.py:122
  167.0 7.3 %token_grad.1 = bf16[512,512]{1,0:T(8,128)(2,1)} custom-call(s32[3]{0:T(128)} %copy-done.32, s32[17]{0:T(128)} %copy-done.38, bf16[16,256,256]{2,1,0:T(8,128)(2,1)} %bitcast.34, f32[8,1,512]{2,1,0:T(1,128)} %copy-done.31, bf16[4,544,256]{2,1,0:T(8,128)(2,1)} %copy-done.8, bf16[4,544,256]{2,1,0:T(8,128)(2,1)} %copy-done.40, bf16[2,512,512]{2,1,0:T(8,128)(2,1)} %tok_ref.3, ...), custom_call_target="tpu_custom_call" | custom-call | flops 4000000000 | bytes 16000000 | tf_op jit(solution)/shard_map/token_grad/pallas_call | solution.py:1144
  174.3 4.8 %collective-permute-done.23.b_ref = bf16[1000,256]{1,0:T(8,128)(2,1)} collective-permute-done((bf16[1000,256]{1,0:T(8,128)(2,1)S(1)}, bf16[1000,256]{1,0:T(8,128)(2,1)}, u32[]{:S(2)}, u32[]{:S(2)}) %collective-permute-start.23) | collective-permute-done | bytes 512032 | tf_op jit(solution)/shard_map/ppermute | solution.py:122
  181.5 2.2 %collective-permute-start.25 = (f32[8,128]{1,0:T(8,128)S(1)}, f32[8,128]{1,0:T(8,128)S(1)}, u32[]{:S(2)}, u32[]{:S(2)}) collective-permute-start(f32[8,128]{1,0:T(8,128)S(1)} %get-tuple-element.127), channel_id=1, source_target_pairs={{0,4},{1,5},{2,6},{3,7},{4,0},{5,1},{6,2},{7,3},{8,12},{9,13},{10,... | collective-permute-start | bytes 12296 | tf_op jit(solution)/shard_map/ppermute | solution.py:101
  187.1 5.7 %collective-permute-start.28 = (f32[8,128]{1,0:T(8,128)S(1)}, f32[8,128]{1,0:T(8,128)S(1)}, u32[]{:S(2)}, u32[]{:S(2)}) collective-permute-start(f32[8,128]{1,0:T(8,128)S(1)} %add_add_fusion.1), channel_id=1, source_target_pairs={{0,8},{1,9},{2,10},{3,11},{4,12},{5,13},{6,14},{7,15},{8,0},{9,1},... | collective-permute-start | bytes 12296 | tf_op jit(solution)/shard_map/ppermute | solution.py:101
  192.8 7.2 %collective-permute-start.29 = (f32[8,128]{1,0:T(8,128)S(1)}, f32[8,128]{1,0:T(8,128)S(1)}, u32[]{:S(2)}, u32[]{:S(2)}) collective-permute-start(f32[8,128]{1,0:T(8,128)S(1)} %add_add_fusion.1), channel_id=1, source_target_pairs={{0,16},{1,17},{2,18},{3,19},{4,20},{5,21},{6,22},{7,23},{8,24},{9,... | collective-permute-start | bytes 12296 | tf_op jit(solution)/shard_map/ppermute | solution.py:101
  201.7 3.6 %collective-permute-done.30 = f32[8,128]{1,0:T(8,128)S(1)} collective-permute-done((f32[8,128]{1,0:T(8,128)S(1)}, f32[8,128]{1,0:T(8,128)S(1)}, u32[]{:S(2)}, u32[]{:S(2)}) %collective-permute-start.30) | collective-permute-done | bytes 4128 | tf_op jit(solution)/shard_map/ppermute | solution.py:101
  205.4 2.3 %collective-permute-done.31 = bf16[256,512]{1,0:T(8,128)(2,1)S(1)} collective-permute-done((bf16[256,512]{1,0:T(8,128)(2,1)S(1)}, bf16[256,512]{1,0:T(8,128)(2,1)S(1)}, u32[]{:S(2)}, u32[]{:S(2)}) %collective-permute-start.31) | collective-permute-done | bytes 262176 | tf_op jit(solution)/shard_map/ppermute | solution.py:122
  209.0 4.3 %optimizer.1 = (f32[1000,512]{1,0:T(8,128)}, f32[1000,512]{1,0:T(8,128)}, f32[1000,512]{1,0:T(8,128)}, f32[1000,512]{1,0:T(8,128)}) custom-call(s32[3]{0:T(128)S(1)} %copy-done.34, f32[2]{0:T(128)S(1)} %copy-done.37, bf16[1000,256]{1,0:T(8,128)(2,1)S(1)} %get-tuple-element.135.mine, bf16[1000,256]{1,0:T(8,128)(2,1)S(1)} %collective-permute-done.34.theirs, ...), custom_call_target="tpu_custom_call" | custom-call | flops 10240000 | bytes 16384000 | tf_op jit(solution)/shard_map/optimizer/pallas_call | solution.py:1235
  (237 shorter events, 53.0 us)
Async XLA Ops:
  3.6 16.7 %collective-permute-start.1 = (bf16[1,512,256]{2,1,0:T(8,128)(2,1)S(1)}, bf16[1,512,256]{2,1,0:T(8,128)(2,1)S(1)}, u32[]{:S(2)}, u32[]{:S(2)}) collective-permute-start(bf16[1,512,256]{2,1,0:T(8,128)(2,1)S(1)} %fusion.2), channel_id=1, source_target_pairs={{0,16},{1,9},{2,18},{3,11},{4,20},{5,13},{6,22},{7,15},{8,24},{9,1... | collective-permute-start | bytes 786440 | tf_op jit(solution)/shard_map/ppermute | solution.py:83
  7.7 13.4 %collective-permute-start = (bf16[1,272,512]{2,1,0:T(8,128)(2,1)S(1)}, bf16[1,272,512]{2,1,0:T(8,128)(2,1)S(1)}, u32[]{:S(2)}, u32[]{:S(2)}) collective-permute-start(bf16[1,272,512]{2,1,0:T(8,128)(2,1)S(1)} %maximum_bitcast_fusion), channel_id=1, source_target_pairs={{0,4},{1,17},{2,6},{3,19},{4,0},{5,21},{6,2},{7,23},{8,12},{9,25},... | collective-permute-start | bytes 835592 | tf_op jit(solution)/shard_map/ppermute | solution.py:83
  9.2 12.1 %collective-permute-start.3 = (bf16[3,512,128]{2,1,0:T(8,128)(2,1)S(1)}, bf16[3,512,128]{2,1,0:T(8,128)(2,1)S(1)}, u32[]{:S(2)}, u32[]{:S(2)}) collective-permute-start(bf16[3,512,128]{2,1,0:T(8,128)(2,1)S(1)} %copy-done.21), channel_id=1, source_target_pairs={{0,2},{1,3},{2,0},{3,1},{4,6},{5,7},{6,4},{7,5},{8,10},{9,11},{10,... | collective-permute-start | bytes 1179656 | tf_op jit(solution)/shard_map/ppermute | solution.py:122
  21.2 16.5 %collective-permute-start.2 = (bf16[2,272,512]{2,1,0:T(8,128)(2,1)S(1)}, bf16[2,272,512]{2,1,0:T(8,128)(2,1)S(1)}, u32[]{:S(2)}, u32[]{:S(2)}) collective-permute-start(bf16[2,272,512]{2,1,0:T(8,128)(2,1)S(1)} %pad_maximum_fusion.3), channel_id=1, source_target_pairs={{0,16},{1,9},{2,18},{3,11},{4,20},{5,13},{6,22},{7,15},{8,24},{9,1... | collective-permute-start | bytes 1671176 | tf_op jit(solution)/shard_map/ppermute | solution.py:83
  22.2 16.7 %collective-permute-start.4 = (bf16[656,512]{1,0:T(8,128)(2,1)S(1)}, bf16[656,512]{1,0:T(8,128)(2,1)}, u32[]{:S(2)}, u32[]{:S(2)}) collective-permute-start(bf16[656,512]{1,0:T(8,128)(2,1)S(1)} %fusion.1.w_own), channel_id=1, source_target_pairs={{0,2},{1,3},{2,0},{3,1},{4,6},{5,7},{6,4},{7,5},{8,10},{9,11},{10,... | collective-permute-start | bytes 2015240 | tf_op jit(solution)/shard_map/ppermute | solution.py:122
  38.9 21.1 %collective-permute-start.5 = (bf16[4,272,512]{2,1,0:T(8,128)(2,1)S(1)}, bf16[4,272,512]{2,1,0:T(8,128)(2,1)S(1)}, u32[]{:S(2)}, u32[]{:S(2)}) collective-permute-start(bf16[4,272,512]{2,1,0:T(8,128)(2,1)S(1)} %pad_maximum_fusion.mine_low.a), channel_id=1, source_target_pairs={{0,8},{1,5},{2,10},{3,7},{4,12},{5,1},{6,14},{7,3},{8,0},{9,13},{1... | collective-permute-start | bytes 3342344 | tf_op jit(solution)/shard_map/ppermute | solution.py:83
  40.6 15.1 %collective-permute-start.6 = (bf16[2,512,256]{2,1,0:T(8,128)(2,1)}, bf16[2,512,256]{2,1,0:T(8,128)(2,1)S(1)}, u32[]{:S(2)}, u32[]{:S(2)}) collective-permute-start(bf16[2,512,256]{2,1,0:T(8,128)(2,1)} %pad_maximum_fusion.5), channel_id=1, source_target_pairs={{0,4},{1,17},{2,6},{3,19},{4,0},{5,21},{6,2},{7,23},{8,12},{9,25},... | collective-permute-start | bytes 1572872 | tf_op jit(solution)/shard_map/ppermute | solution.py:83
  42.4 19.9 %collective-permute-start.7 = (bf16[4,272,512]{2,1,0:T(8,128)(2,1)S(1)}, bf16[4,272,512]{2,1,0:T(8,128)(2,1)S(1)}, u32[]{:S(2)}, u32[]{:S(2)}) collective-permute-start(bf16[4,272,512]{2,1,0:T(8,128)(2,1)S(1)} %pad_maximum_fusion.mine_low.a), channel_id=1, source_target_pairs={{0,1},{1,0},{2,3},{3,2},{4,5},{5,4},{6,7},{7,6},{8,9},{9,8},{10,11... | collective-permute-start | bytes 3342344 | tf_op jit(solution)/shard_map/ppermute | solution.py:122
  60.0 11.6 %collective-permute-start.10 = (bf16[4,512,256]{2,1,0:T(8,128)(2,1)S(1)}, bf16[4,512,256]{2,1,0:T(8,128)(2,1)S(1)}, u32[]{:S(2)}, u32[]{:S(2)}) collective-permute-start(bf16[4,512,256]{2,1,0:T(8,128)(2,1)S(1)} %pad_maximum_fusion.2.mine_low), channel_id=1, source_target_pairs={{0,1},{1,0},{2,3},{3,2},{4,5},{5,4},{6,7},{7,6},{8,9},{9,8},{10,11... | collective-permute-start | bytes 3145736 | tf_op jit(solution)/shard_map/ppermute | solution.py:122
  60.5 14.9 %collective-permute-start.9 = (bf16[4,512,256]{2,1,0:T(8,128)(2,1)S(1)}, bf16[4,512,256]{2,1,0:T(8,128)(2,1)}, u32[]{:S(2)}, u32[]{:S(2)}) collective-permute-start(bf16[4,512,256]{2,1,0:T(8,128)(2,1)S(1)} %pad_maximum_fusion.2.mine_low), channel_id=1, source_target_pairs={{0,8},{1,5},{2,10},{3,7},{4,12},{5,1},{6,14},{7,3},{8,0},{9,13},{1... | collective-permute-start | bytes 3145736 | tf_op jit(solution)/shard_map/ppermute | solution.py:83
  61.5 8.4 %collective-permute-start.11 = (bf16[656,512]{1,0:T(8,128)(2,1)S(1)}, bf16[656,512]{1,0:T(8,128)(2,1)S(1)}, u32[]{:S(2)}, u32[]{:S(2)}) collective-permute-start(bf16[656,512]{1,0:T(8,128)(2,1)S(1)} %copy-done.19), channel_id=1, source_target_pairs={{0,1},{1,0},{2,3},{3,2},{4,5},{5,4},{6,7},{7,6},{8,9},{9,8},{10,11... | collective-permute-start | bytes 2015240 | tf_op jit(solution)/shard_map/ppermute | solution.py:122
  62.3 8.5 %collective-permute-start.12 = (bf16[656,512]{1,0:T(8,128)(2,1)}, bf16[656,512]{1,0:T(8,128)(2,1)S(1)}, u32[]{:S(2)}, u32[]{:S(2)}) collective-permute-start(bf16[656,512]{1,0:T(8,128)(2,1)} %collective-permute-done.4.w_along), channel_id=1, source_target_pairs={{0,1},{1,0},{2,3},{3,2},{4,5},{5,4},{6,7},{7,6},{8,9},{9,8},{10,11... | collective-permute-start | bytes 2015240 | tf_op jit(solution)/shard_map/ppermute | solution.py:122
  75.5 3.0 %collective-permute-start.13 = (bf16[4,512,256]{2,1,0:T(8,128)(2,1)}, bf16[4,512,256]{2,1,0:T(8,128)(2,1)}, u32[]{:S(2)}, u32[]{:S(2)}) collective-permute-start(bf16[4,512,256]{2,1,0:T(8,128)(2,1)} %collective-permute-done.9.mine_high), channel_id=1, source_target_pairs={{0,1},{1,0},{2,3},{3,2},{4,5},{5,4},{6,7},{7,6},{8,9},{9,8},{10,11... | collective-permute-start | bytes 3145736 | tf_op jit(solution)/shard_map/ppermute | solution.py:122
  94.2 9.0 %collective-permute-start.14 = (bf16[528,256]{1,0:T(8,128)(2,1)S(1)}, bf16[528,256]{1,0:T(8,128)(2,1)S(1)}, u32[]{:S(2)}, u32[]{:S(2)}) collective-permute-start(bf16[528,256]{1,0:T(8,128)(2,1)S(1)} %get-tuple-element.99), channel_id=1, source_target_pairs={{0,2},{1,3},{2,0},{3,1},{4,6},{5,7},{6,4},{7,5},{8,10},{9,11},{10,... | collective-permute-start | bytes 811016 | tf_op jit(solution)/shard_map/ppermute | solution.py:122
  113.4 6.6 %collective-permute-start.16 = (bf16[1,544,256]{2,1,0:T(8,128)(2,1)S(1)}, bf16[1,544,256]{2,1,0:T(8,128)(2,1)S(1)}, u32[]{:S(2)}, u32[]{:S(2)}) collective-permute-start(bf16[1,544,256]{2,1,0:T(8,128)(2,1)S(1)} %bitcast.35), channel_id=1, source_target_pairs={{0,4},{1,17},{2,6},{3,19},{4,0},{5,21},{6,2},{7,23},{8,12},{9,25},... | collective-permute-start | bytes 835592 | tf_op jit(solution)/shard_map/ppermute | solution.py:83
  114.3 8.3 %collective-permute-start.17 = (bf16[544,256]{1,0:T(8,128)(2,1)S(1)}, bf16[544,256]{1,0:T(8,128)(2,1)S(1)}, u32[]{:S(2)}, u32[]{:S(2)}) collective-permute-start(bf16[544,256]{1,0:T(8,128)(2,1)S(1)} %get-tuple-element.105.pack_own.do_ref), channel_id=1, source_target_pairs={{0,2},{1,3},{2,0},{3,1},{4,6},{5,7},{6,4},{7,5},{8,10},{9,11},{10,... | collective-permute-start | bytes 835592 | tf_op jit(solution)/shard_map/ppermute | solution.py:122
  122.6 15.5 %collective-permute-start.18 = (bf16[2,544,256]{2,1,0:T(8,128)(2,1)S(1)}, bf16[2,544,256]{2,1,0:T(8,128)(2,1)S(1)}, u32[]{:S(2)}, u32[]{:S(2)}) collective-permute-start(bf16[2,544,256]{2,1,0:T(8,128)(2,1)S(1)} %pad_maximum_fusion.4), channel_id=1, source_target_pairs={{0,16},{1,9},{2,18},{3,11},{4,20},{5,13},{6,22},{7,15},{8,24},{9,1... | collective-permute-start | bytes 1671176 | tf_op jit(solution)/shard_map/ppermute | solution.py:83
  138.2 16.7 %collective-permute-start.19 = (bf16[4,544,256]{2,1,0:T(8,128)(2,1)S(1)}, bf16[4,544,256]{2,1,0:T(8,128)(2,1)S(1)}, u32[]{:S(2)}, u32[]{:S(2)}) collective-permute-start(bf16[4,544,256]{2,1,0:T(8,128)(2,1)S(1)} %pad_maximum_fusion.1.low_ref), channel_id=1, source_target_pairs={{0,8},{1,5},{2,10},{3,7},{4,12},{5,1},{6,14},{7,3},{8,0},{9,13},{1... | collective-permute-start | bytes 3342344 | tf_op jit(solution)/shard_map/ppermute | solution.py:83
  141.5 9.1 %collective-permute-start.21 = (bf16[256,512]{1,0:T(8,128)(2,1)S(1)}, bf16[256,512]{1,0:T(8,128)(2,1)S(1)}, u32[]{:S(2)}, u32[]{:S(2)}) collective-permute-start(bf16[256,512]{1,0:T(8,128)(2,1)S(1)} %constant_dynamic-slice_fusion.1), channel_id=1, source_target_pairs={{0,2},{1,3},{2,0},{3,1},{4,6},{5,7},{6,4},{7,5},{8,10},{9,11},{10,... | collective-permute-start | bytes 786440 | tf_op jit(solution)/shard_map/ppermute | solution.py:122
  142.2 11.2 %collective-permute-start.20 = (bf16[512,256]{1,0:T(8,128)(2,1)S(1)}, bf16[512,256]{1,0:T(8,128)(2,1)S(1)}, u32[]{:S(2)}, u32[]{:S(2)}) collective-permute-start(bf16[512,256]{1,0:T(8,128)(2,1)S(1)} %get-tuple-element.115), channel_id=1, source_target_pairs={{0,2},{1,3},{2,0},{3,1},{4,6},{5,7},{6,4},{7,5},{8,10},{9,11},{10,... | collective-permute-start | bytes 786440 | tf_op jit(solution)/shard_map/ppermute | solution.py:122
  162.1 16.9 %collective-permute-start.23 = (bf16[1000,256]{1,0:T(8,128)(2,1)S(1)}, bf16[1000,256]{1,0:T(8,128)(2,1)}, u32[]{:S(2)}, u32[]{:S(2)}) collective-permute-start(bf16[1000,256]{1,0:T(8,128)(2,1)S(1)} %reduce-precision_convert_fusion.1.a_ref), channel_id=1, source_target_pairs={{0,2},{1,3},{2,0},{3,1},{4,6},{5,7},{6,4},{7,5},{8,10},{9,11},{10,... | collective-permute-start | bytes 1536008 | tf_op jit(solution)/shard_map/ppermute | solution.py:122
  167.0 12.1 %collective-permute-start.32 = (bf16[256,512]{1,0:T(8,128)(2,1)S(1)}, bf16[256,512]{1,0:T(8,128)(2,1)S(1)}, u32[]{:S(2)}, u32[]{:S(2)}) collective-permute-start(bf16[256,512]{1,0:T(8,128)(2,1)S(1)} %copy-done.66), channel_id=1, source_target_pairs={{0,1},{1,0},{2,3},{3,2},{4,5},{5,4},{6,7},{7,6},{8,9},{9,8},{10,11... | collective-permute-start | bytes 786440 | tf_op jit(solution)/shard_map/ppermute | solution.py:122
  179.0 7.8 %collective-permute-start.27 = (bf16[512,512]{1,0:T(8,128)(2,1)}, bf16[512,512]{1,0:T(8,128)(2,1)S(1)}, u32[]{:S(2)}, u32[]{:S(2)}) collective-permute-start(bf16[512,512]{1,0:T(8,128)(2,1)} %token_grad.1), channel_id=1, source_target_pairs={{0,1},{1,0},{2,3},{3,2},{4,5},{5,4},{6,7},{7,6},{8,9},{9,8},{10,11... | collective-permute-start | bytes 1572872 | tf_op jit(solution)/shard_map/ppermute | solution.py:122
  181.0 3.2 %collective-permute-start.24 = (f32[8,128]{1,0:T(8,128)S(1)}, f32[8,128]{1,0:T(8,128)S(1)}, u32[]{:S(2)}, u32[]{:S(2)}) collective-permute-start(f32[8,128]{1,0:T(8,128)S(1)} %get-tuple-element.127), channel_id=1, source_target_pairs={{0,1},{1,0},{2,3},{3,2},{4,5},{5,4},{6,7},{7,6},{8,9},{9,8},{10,11... | collective-permute-start | bytes 12296 | tf_op jit(solution)/shard_map/ppermute | solution.py:101
  181.5 3.8 %collective-permute-start.25 = (f32[8,128]{1,0:T(8,128)S(1)}, f32[8,128]{1,0:T(8,128)S(1)}, u32[]{:S(2)}, u32[]{:S(2)}) collective-permute-start(f32[8,128]{1,0:T(8,128)S(1)} %get-tuple-element.127), channel_id=1, source_target_pairs={{0,4},{1,5},{2,6},{3,7},{4,0},{5,1},{6,2},{7,3},{8,12},{9,13},{10,... | collective-permute-start | bytes 12296 | tf_op jit(solution)/shard_map/ppermute | solution.py:101
  183.7 3.1 %collective-permute-start.26 = (f32[8,128]{1,0:T(8,128)S(1)}, f32[8,128]{1,0:T(8,128)S(1)}, u32[]{:S(2)}, u32[]{:S(2)}) collective-permute-start(f32[8,128]{1,0:T(8,128)S(1)} %get-tuple-element.127), channel_id=1, source_target_pairs={{0,5},{1,4},{2,7},{3,6},{4,1},{5,0},{6,3},{7,2},{8,13},{9,12},{10,... | collective-permute-start | bytes 12296 | tf_op jit(solution)/shard_map/ppermute | solution.py:101
  183.9 25.0 %collective-permute-start.34 = (bf16[1000,256]{1,0:T(8,128)(2,1)S(1)}, bf16[1000,256]{1,0:T(8,128)(2,1)S(1)}, u32[]{:S(2)}, u32[]{:S(2)}) collective-permute-start(bf16[1000,256]{1,0:T(8,128)(2,1)S(1)} %get-tuple-element.135.mine), channel_id=1, source_target_pairs={{0,1},{1,0},{2,3},{3,2},{4,5},{5,4},{6,7},{7,6},{8,9},{9,8},{10,11... | collective-permute-start | bytes 1536008 | tf_op jit(solution)/shard_map/ppermute | solution.py:122
  187.1 14.6 %collective-permute-start.28 = (f32[8,128]{1,0:T(8,128)S(1)}, f32[8,128]{1,0:T(8,128)S(1)}, u32[]{:S(2)}, u32[]{:S(2)}) collective-permute-start(f32[8,128]{1,0:T(8,128)S(1)} %add_add_fusion.1), channel_id=1, source_target_pairs={{0,8},{1,9},{2,10},{3,11},{4,12},{5,13},{6,14},{7,15},{8,0},{9,1},... | collective-permute-start | bytes 12296 | tf_op jit(solution)/shard_map/ppermute | solution.py:101
  192.8 9.0 %collective-permute-start.29 = (f32[8,128]{1,0:T(8,128)S(1)}, f32[8,128]{1,0:T(8,128)S(1)}, u32[]{:S(2)}, u32[]{:S(2)}) collective-permute-start(f32[8,128]{1,0:T(8,128)S(1)} %add_add_fusion.1), channel_id=1, source_target_pairs={{0,16},{1,17},{2,18},{3,19},{4,20},{5,21},{6,22},{7,23},{8,24},{9,... | collective-permute-start | bytes 12296 | tf_op jit(solution)/shard_map/ppermute | solution.py:101
  200.0 5.4 %collective-permute-start.30 = (f32[8,128]{1,0:T(8,128)S(1)}, f32[8,128]{1,0:T(8,128)S(1)}, u32[]{:S(2)}, u32[]{:S(2)}) collective-permute-start(f32[8,128]{1,0:T(8,128)S(1)} %add_add_fusion.1), channel_id=1, source_target_pairs={{0,24},{1,25},{2,26},{3,27},{4,28},{5,29},{6,30},{7,31},{8,16},{9,... | collective-permute-start | bytes 12296 | tf_op jit(solution)/shard_map/ppermute | solution.py:101
  200.0 7.7 %collective-permute-start.31 = (bf16[256,512]{1,0:T(8,128)(2,1)S(1)}, bf16[256,512]{1,0:T(8,128)(2,1)S(1)}, u32[]{:S(2)}, u32[]{:S(2)}) collective-permute-start(bf16[256,512]{1,0:T(8,128)(2,1)S(1)} %constant_dynamic-slice_fusion), channel_id=1, source_target_pairs={{0,2},{1,3},{2,0},{3,1},{4,6},{5,7},{6,4},{7,5},{8,10},{9,11},{10,... | collective-permute-start | bytes 786440 | tf_op jit(solution)/shard_map/ppermute | solution.py:122
  207.7 5.6 %collective-permute-start.33 = (bf16[256,512]{1,0:T(8,128)(2,1)S(1)}, bf16[256,512]{1,0:T(8,128)(2,1)S(1)}, u32[]{:S(2)}, u32[]{:S(2)}) collective-permute-start(bf16[256,512]{1,0:T(8,128)(2,1)S(1)} %collective-permute-done.31), channel_id=1, source_target_pairs={{0,1},{1,0},{2,3},{3,2},{4,5},{5,4},{6,7},{7,6},{8,9},{9,8},{10,11... | collective-permute-start | bytes 786440 | tf_op jit(solution)/shard_map/ppermute | solution.py:122
  (75 other events, 1016.6 us)

commit v2 on v1

--- a/solution.py
+++ b/solution.py
@@ -134,11 +134,19 @@
     return pl.BlockSpec(memory_space=pltpu.HBM)
 
 
-def join_weights(meta, own, other, target, first):
+def flag_shape():
+    return jax.ShapeDtypeStruct((8, 128), F32)
+
+
+def raise_flag(ref):
+    ref[...] = jnp.zeros(ref.shape, F32)
+
+
+def join_weights(meta, own, other, target, kinds):
     dim = own.shape[2]
-    for kind in range(first, own.shape[0]):
+    for index, kind in enumerate(kinds):
         for place in range(2):
-            column = ((kind - first) * 2 + place) * dim
+            column = (index * 2 + place) * dim
             target[:, column : column + dim] = jnp.where(meta[1] == place, own[kind], other[kind])
 
 
@@ -146,38 +154,42 @@
     return jnp.concatenate([value] * count, axis=1)
 
 
+def line_of(columns):
+    return jnp.transpose(columns)[0:1, :]
+
+
 def column_of(line):
     return jnp.transpose(jnp.broadcast_to(line, (128, line.shape[1])))
 
 
-def project_query_kernel(meta, a, b, c, d, own, other, q_out):
+def project_query_kernel(a, b, c, d, weights, q_out, flag):
+    raise_flag(flag)
     half = a.shape[1] - PACK
-    dim = own.shape[2]
-    weights = jnp.concatenate(
-        [jnp.where(meta[1] == place, own[0], other[0]) for place in range(2)], axis=1
-    )
     for high, pair in enumerate(((a, b), (c, d))):
         for place, ref in enumerate(pair):
-            q_out[high, 0, place] = mm(ref[0, :half], weights).astype(BF)
-
-
-def project_query(meta, mine, theirs, in_own, in_other):
+            q_out[high, 0, place] = mm(ref[0, :half], weights[...]).astype(BF)
+
+
+def project_query(mine, theirs, weights):
     slots, rows, width = mine[0].shape
     half = rows - PACK
-    dim = in_own.shape[2]
+    double = weights.shape[1]
     block = pl.BlockSpec((1, rows, width), lambda g: (g, 0, 0))
-    whole = pl.BlockSpec((1,) + in_own.shape[1:], lambda g: (0, 0, 0))
-    out = pl.pallas_call(
+    whole = pl.BlockSpec(weights.shape, lambda g: (0, 0))
+    out, flag = pl.pallas_call(
         project_query_kernel,
-        out_shape=jax.ShapeDtypeStruct((2, slots, 2, half, 2 * dim), BF),
+        out_shape=(jax.ShapeDtypeStruct((2, slots, 2, half, double), BF), flag_shape()),
         grid=(slots,),
-        in_specs=[smem()] + [block] * 4 + [whole] * 2,
-        out_specs=pl.BlockSpec((2, 1, 2, half, 2 * dim), lambda g: (0, g, 0, 0, 0)),
+        in_specs=[block] * 4 + [whole],
+        out_specs=[
+            pl.BlockSpec((2, 1, 2, half, double), lambda g: (0, g, 0, 0, 0)),
+            pl.BlockSpec((8, 128), lambda g: (0, 0)),
+        ],
         compiler_params=params(),
-        cost_estimate=cost(8 * slots * half * width * 2 * dim, 8 * slots * half * width),
+        cost_estimate=cost(8 * slots * half * width * double, 8 * slots * half * width),
         name="project_query",
-    )(meta, mine[0], theirs[0], mine[1], theirs[1], in_own, in_other)
-    return out.reshape(4 * slots, half, 2 * dim)
+    )(mine[0], theirs[0], mine[1], theirs[1], weights)
+    return out.reshape(4 * slots, half, double), flag
 
 
 def key_range(starts, low, high, data_count):
@@ -267,15 +279,22 @@
     theirs_low,
     theirs_high,
     q_ref,
+    kv_own,
+    wq_ref,
+    wkv_ref,
+    m_out,
+    l_out,
+    acc_out,
+    flag,
     m_ref,
     acc_ref,
-    w_ref,
     x_ref,
     id_ref,
     tok_ref,
     sem,
     tok_sem,
 ):
+    raise_flag(flag)
     size, dim = tok_ref.shape[1], in_own.shape[2]
     tok_copy = pltpu.make_async_copy(tok_hbm, tok_ref, tok_sem)
     tok_copy.start()
@@ -284,10 +303,12 @@
     first, last = first // size, (last + size - 1) // size
     gathered = (mine_low, mine_high, theirs_low, theirs_high)
     fetch_shards(meta, first, last, gathered, x_ref, sem)
-    join_weights(meta, in_own, in_other, w_ref, 0)
+    join_weights(meta, in_own, in_other, wq_ref, (0,))
+    join_weights(meta, in_own, in_other, wkv_ref, (1, 2))
     tok_copy.wait()
     for slot in range(2):
-        q_ref[slot] = mm(tok_ref[meta[1] ^ slot], w_ref[:, : 2 * dim]).astype(BF)
+        q_ref[slot] = mm(tok_ref[meta[1] ^ slot], wq_ref[...]).astype(BF)
+    kv_own[...] = mm(tok_ref[meta[1]], wkv_ref[...]).astype(BF)
     m_ref[...] = jnp.full(m_ref.shape, NEGATIVE, F32)
     acc_ref[...] = jnp.zeros(acc_ref.shape, F32)
     id_ref[...] = column_of(ids_ref[meta[1]])
@@ -295,7 +316,7 @@
 
     def step(shard, carry):
         raw_rows, line = load_shard(meta, shard, gathered, x_ref, sem)
-        kv = mm(raw_rows, w_ref[:, 2 * dim :]).astype(BF)
+        kv = mm(raw_rows, wkv_ref[...]).astype(BF)
         mask = wide(id_ref[...], size // 128) == line
         raw = [
             mm_nt(q_ref[0, :, h * dim : (h + 1) * dim], kv[:, h * dim : (h + 1) * dim])
@@ -311,6 +332,10 @@
         return carry
 
     lax.fori_loop(first, last, step, 0)
+    for h in range(2):
+        m_out[h : h + 1, :] = line_of(m_ref[h])
+        l_out[h : h + 1, :] = line_of(acc_ref[h, :, dim:])
+        acc_out[h] = acc_ref[h, :, :dim]
 
 
 def shard_scratch(banks):
@@ -325,20 +350,26 @@
         functools.partial(token_forward_kernel, data_count, factor),
         out_shape=(
             jax.ShapeDtypeStruct((2, size, 2 * dim), BF),
-            jax.ShapeDtypeStruct((2, size, 128), F32),
-            jax.ShapeDtypeStruct((2, size, dim + 128), F32),
+            jax.ShapeDtypeStruct((size, 4 * dim), BF),
+            jax.ShapeDtypeStruct((width, 2 * dim), BF),
+            jax.ShapeDtypeStruct((width, 4 * dim), BF),
+            jax.ShapeDtypeStruct((2, size), F32),
+            jax.ShapeDtypeStruct((2, size), F32),
+            jax.ShapeDtypeStruct((2, size, dim), F32),
+            flag_shape(),
         ),
         in_specs=[smem(), smem()] + [vmem()] * 3 + [hbm()] * 5,
-        out_specs=[vmem()] * 3,
+        out_specs=[vmem()] * 8,
         scratch_shapes=[
-            pltpu.VMEM((width, 6 * dim), BF),
+            pltpu.VMEM((2, size, 128), F32),
+            pltpu.VMEM((2, size, dim + 128), F32),
             shard_scratch(mine),
             pltpu.VMEM((size, 128), F32),
             pltpu.VMEM(tokens.shape, BF),
             pltpu.SemaphoreType.DMA((2 * mine[0].shape[0], 2)),
             pltpu.SemaphoreType.DMA,
         ],
-        compiler_params=params(*mine, *theirs),
+        compiler_params=params(spare=VMEM_LIMIT),
         cost_estimate=cost(8e9, 8e6, 2e6),
         name="token_forward",
     )(meta, starts, ids_rows, in_own, in_other, tokens, *mine, *theirs)
@@ -469,9 +500,10 @@
     q_ref,
     ids_ref,
     m_in,
+    l_in,
     acc_in,
-    in_own,
-    in_other,
+    _,
+    w_ref,
     mine_low,
     mine_high,
     theirs_low,
@@ -482,7 +514,6 @@
     m_ref,
     acc_ref,
     raws,
-    w_ref,
     kv_ref,
     id_ref,
     state,
@@ -491,11 +522,12 @@
     size, dim = q_ref.shape[1], q_ref.shape[2] // 2
     sources = (mine_low, mine_high, theirs_low, theirs_high)
     fetch_prompts(meta, local, table, sources, raws, state, sem)
-    join_weights(meta, in_own, in_other, w_ref, 1)
-    m_ref[0] = m_in[...]
-    acc_ref[0] = acc_in[...]
-    m_ref[1] = jnp.full(m_in.shape, NEGATIVE, F32)
-    acc_ref[1] = jnp.zeros(acc_in.shape, F32)
+    for h in range(2):
+        m_ref[0, h] = column_of(m_in[h : h + 1, :])
+        acc_ref[0, h, :, dim:] = column_of(l_in[h : h + 1, :])
+        acc_ref[0, h, :, :dim] = acc_in[h]
+    m_ref[1] = jnp.full(m_ref.shape[1:], NEGATIVE, F32)
+    acc_ref[1] = jnp.zeros(acc_ref.shape[1:], F32)
     for slot in range(2):
         id_ref[slot] = column_of(ids_ref[meta[1] ^ slot])
 
@@ -523,49 +555,48 @@
         cols = pl.ds(h * dim, dim)
         total = acc_ref[0, h, :, dim:]
         wide_ref[:, cols] = acc_ref[0, h, :, :dim] / total
-        lse_ref[h] = m_ref[0, h] + jnp.log2(total)
+        lse_ref[h : h + 1, :] = line_of(m_ref[0, h] + jnp.log2(total))
         total = acc_ref[1, h, :, dim:]
         send_ref[pl.ds(0, size), cols] = (acc_ref[1, h, :, :dim] / total).astype(BF)
-        line = jnp.transpose(m_ref[1, h] + jnp.log2(total))[0:1, :]
+        line = line_of(m_ref[1, h] + jnp.log2(total))
         row = store_line(send_ref, row, line)
 
 
-def prompt_scratch(prompt_banks, width, dim, block):
+def prompt_scratch(prompt_banks, dim, block):
     slots, part, columns = prompt_banks[0].shape
     pieces = PLEN // block
     count = 2 * slots // pieces
     return [
         pltpu.VMEM((2, count, pieces, part, columns), BF),
-        pltpu.VMEM((width, 4 * dim), BF),
         pltpu.VMEM((count, -(-pieces * part // 128) * 128, 4 * dim), BF),
     ], [pltpu.SMEM((count,), jnp.int32), pltpu.SemaphoreType.DMA((2, count, pieces))]
 
 
 def prompt_forward(
-    meta, local, table, q_own, ids_rows, state, prompt_mine, prompt_theirs, in_own, in_other, factor, block
+    meta, local, table, q_own, ids_rows, state, flag, prompt_mine, prompt_theirs, weights, factor, block
 ):
     size, dim = q_own.shape[1], q_own.shape[2] // 2
-    buffers, flags = prompt_scratch(prompt_mine, in_own.shape[1], dim, block)
+    buffers, flags = prompt_scratch(prompt_mine, dim, block)
     return pl.pallas_call(
         functools.partial(prompt_forward_kernel, block, factor),
         out_shape=(
             jax.ShapeDtypeStruct((size, 2 * dim), F32),
-            jax.ShapeDtypeStruct((2, size, 128), F32),
+            jax.ShapeDtypeStruct((2, size), F32),
             jax.ShapeDtypeStruct((size + PACK, 2 * dim), BF),
         ),
-        in_specs=[smem()] * 3 + [vmem()] * 6 + [hbm()] * 4,
+        in_specs=[smem()] * 3 + [vmem()] * 7 + [hbm()] * 4,
         out_specs=[vmem()] * 3,
         scratch_shapes=[
-            pltpu.VMEM((2,) + state[0].shape, F32),
-            pltpu.VMEM((2,) + state[1].shape, F32),
+            pltpu.VMEM((2, 2, size, 128), F32),
+            pltpu.VMEM((2, 2, size, dim + 128), F32),
             *buffers,
             pltpu.VMEM((2, size, 128), F32),
             *flags,
         ],
-        compiler_params=params(*prompt_mine, *prompt_mine, *prompt_mine, *prompt_mine),
+        compiler_params=params(spare=VMEM_LIMIT),
         cost_estimate=cost(4e9, 8e6, 2e6),
         name="prompt_forward",
-    )(meta, local, table, q_own, ids_rows, *state, in_own, in_other, *prompt_mine, *prompt_theirs)
+    )(meta, local, table, q_own, ids_rows, *state, flag, weights, *prompt_mine, *prompt_theirs)
 
 
 def join_kernel(wide_in, lse_in, other_ref, o_ref, wide_ref, lse_ref):
@@ -573,7 +604,7 @@
     rows_per = size // (2 * dim)
     for h in range(2):
         cols = pl.ds(h * dim, dim)
-        first = lse_in[h]
+        first = column_of(lse_in[h : h + 1, :])
         second = column_of(load_line(other_ref, size + h * 3 * rows_per, size))
         top = jnp.maximum(first, second)
         first, second = jnp.exp2(first - top), jnp.exp2(second - top)
@@ -582,7 +613,7 @@
         attended = (first * wide_in[:, cols] + second * other) / total
         wide_ref[:, cols] = attended
         o_ref[:, cols] = attended.astype(BF)
-        lse_ref[h] = top + jnp.log2(total)
+        lse_ref[h : h + 1, :] = line_of(top + jnp.log2(total))
 
 
 def join_halves(wide_half, lse_half, other):
@@ -638,18 +669,29 @@
     w_ref,
     sem,
 ):
-    size, width = tok_ref.shape[1:]
+    size, width = tok_ref.shape
     dim = mine.shape[1] // 2
     heads = w_ref.shape[0]
     hid = (w_ref.shape[1] - PACK - dim) // 2
     batch, parity = meta[1], meta[2]
     even = parity == 0
+    cuts = (pl.ds(hid, dim), pl.ds(hid + dim, hid + PACK), pl.ds(0, hid))
+
+    def arrived(part):
+        for q in range(heads):
+            pltpu.make_async_copy(
+                w_own.at[cuts[part]], w_ref.at[q, cuts[part]], sem.at[q, part]
+            ).wait()
+
     for q in range(heads):
         for place, ref in enumerate((w_own, w_along, w_core, w_far)):
 
             @pl.when((2 * batch + parity) == (q ^ (0, 2, 1, 3)[place]))
             def _():
-                pltpu.make_async_copy(ref, w_ref.at[q], sem.at[q]).start()
+                for part, rows in enumerate(cuts):
+                    pltpu.make_async_copy(
+                        ref.at[rows], w_ref.at[q, rows], sem.at[q, part]
+                    ).start()
 
     place_out = slice(hid, hid + dim)
     place_up = slice(hid + dim, 2 * hid + dim)
@@ -657,22 +699,25 @@
     sub = min(256, size)
     pack_ref[pl.ds(size, STATS), :] = jnp.zeros((STATS, 2 * dim), BF)
     g0, g1 = gains[0:1, :], gains[1:2, :]
-    for q in range(heads):
-        pltpu.make_async_copy(w_own, w_ref.at[q], sem.at[q]).wait()
     for part in range(size // sub):
         rows = pl.ds(part * sub, sub)
         a, b = mine[rows, :], theirs[rows, :]
+        if part == 0:
+            arrived(0)
         first = jnp.where(even, a, b)
         second = jnp.where(even, b, a)
         attn = mm(first[:, :dim], w_ref[0, place_out, :])
         attn += mm(second[:, :dim], w_ref[1, place_out, :])
         attn += mm(first[:, dim:], w_ref[2, place_out, :])
         attn += mm(second[:, dim:], w_ref[3, place_out, :])
-        unit_one, scale_one = norm_parts(tok_ref[batch, rows, :].astype(F32) + attn)
+        unit_one, scale_one = norm_parts(tok_ref[rows, :].astype(F32) + attn)
         normed = unit_one * g0 + shifts[0:1, :]
         normed_low = normed.astype(BF)
         branch = down_bias[...]
         slopes = []
+        if part == 0:
+            arrived(1)
+            arrived(2)
         for q in range(heads):
             bias = (
                 w_ref[q, place_bias : place_bias + 1, :hid].astype(F32)
@@ -685,7 +730,7 @@
             branch = branch + mm((pre * cdf).astype(BF), w_ref[q, :hid, :])
         unit_two, scale_two = norm_parts(normed + branch)
         out_ref[rows, :] = (unit_two * g1 + shifts[1:2, :]).astype(BF)
-        grad_mixed = norm_back(cot_ref[batch, rows, :].astype(F32), unit_two, scale_two, g1)
+        grad_mixed = norm_back(cot_ref[rows, :].astype(F32), unit_two, scale_two, g1)
         mixed_low = grad_mixed.astype(BF)
         grad_normed = grad_mixed
         for q in range(heads):
@@ -699,15 +744,15 @@
             grad_out = mm_nt(sum_low, w_ref[2 * head + parity, place_out, :]).astype(BF)
             pack_ref[rows, cols] = grad_out
             delta = jnp.sum(grad_out.astype(F32) * wide_ref[rows, cols], axis=1, keepdims=True)
-            delta_ref[head, rows, :] = jnp.broadcast_to(delta, (sub, 128))
+            delta_ref[head : head + 1, rows] = line_of(jnp.broadcast_to(delta, (sub, 128)))
     row = size
     for head in range(2):
         for ref in (lse_ref, delta_ref):
-            row = store_line(pack_ref, row, jnp.transpose(ref[head])[0:1, :])
+            row = store_line(pack_ref, row, ref[head : head + 1, :])
 
 
 def feed(meta, mine, theirs, wide_out, lse, tokens, cotangent, w, down_bias, gains, shifts):
-    size, width = tokens.shape[1:]
+    size, width = tokens.shape
     dim = mine.shape[1] // 2
     return pl.pallas_call(
         feed_kernel,
@@ -715,11 +760,11 @@
             jax.ShapeDtypeStruct((size, width), BF),
             jax.ShapeDtypeStruct((size, width), F32),
             jax.ShapeDtypeStruct((size + STATS, 2 * dim), BF),
-            jax.ShapeDtypeStruct((2, size, 128), F32),
+            jax.ShapeDtypeStruct((2, size), F32),
         ),
         in_specs=[smem()] + [vmem()] * 9 + [hbm()] * 4,
         out_specs=[vmem()] * 4,
-        scratch_shapes=[pltpu.VMEM((4,) + w[0].shape, BF), pltpu.SemaphoreType.DMA((4,))],
+        scratch_shapes=[pltpu.VMEM((4,) + w[0].shape, BF), pltpu.SemaphoreType.DMA((4, 3))],
         compiler_params=params(),
         cost_estimate=cost(3e9, 8e6, 1e6),
         name="feed",
@@ -743,26 +788,30 @@
     delta_ref,
     do_ref,
     acc_in,
-    in_own,
-    in_other,
+    w_ref,
     mine_low,
     mine_high,
     theirs_low,
     theirs_high,
     dq_ref,
+    flag,
     acc_ref,
     x_ref,
-    w_ref,
     id_ref,
+    lse_cols,
+    delta_cols,
     sem,
 ):
+    raise_flag(flag)
     size, dim = q_ref.shape[1], q_ref.shape[2] // 2
     base = meta[0] * size
     first, last = key_range(starts, base, base + size, data_count)
     first, last = first // size, (last + size - 1) // size
     gathered = (mine_low, mine_high, theirs_low, theirs_high)
     fetch_shards(meta, first, last, gathered, x_ref, sem)
-    join_weights(meta, in_own, in_other, w_ref, 1)
+    for h in range(2):
+        lse_cols[h] = column_of(lse_ref[h : h + 1, :])
+        delta_cols[h] = column_of(delta_ref[h : h + 1, :])
     acc_ref[...] = acc_in[...]
     id_ref[...] = column_of(ids_ref[meta[1]])
 
@@ -781,7 +830,7 @@
             )
         for h in range(2):
             scores = jnp.where(mask, raw[h], NEGATIVE)
-            low.append(low_grads(scores, factor, lse_ref[h], grads[h], delta_ref[h]))
+            low.append(low_grads(scores, factor, lse_cols[h], grads[h], delta_cols[h]))
         for h in range(2):
             acc_ref[h] += mm(low[h], kv[:, h * dim : (h + 1) * dim])
         return carry
@@ -792,20 +841,20 @@
 
 
 def token_query_grad(
-    meta, starts, q_own, ids_rows, lse, delta, pack, acc, mine, theirs, in_own, in_other, factor, data_count
+    meta, starts, q_own, ids_rows, lse, delta, pack, acc, mine, theirs, weights, factor, data_count
 ):
     size, dim = q_own.shape[1], q_own.shape[2] // 2
-    width = in_own.shape[1]
     return pl.pallas_call(
         functools.partial(token_query_grad_kernel, data_count, factor),
-        out_shape=jax.ShapeDtypeStruct((size, 2 * dim), F32),
-        in_specs=[smem()] * 2 + [vmem()] * 8 + [hbm()] * 4,
-        out_specs=vmem(),
+        out_shape=(jax.ShapeDtypeStruct((size, 2 * dim), F32), flag_shape()),
+        in_specs=[smem()] * 2 + [vmem()] * 7 + [hbm()] * 4,
+        out_specs=[vmem()] * 2,
         scratch_shapes=[
             pltpu.VMEM((2, size, dim), F32),
             shard_scratch(mine),
-            pltpu.VMEM((width, 4 * dim), BF),
             pltpu.VMEM((size, 128), F32),
+            pltpu.VMEM((2, size, 128), F32),
+            pltpu.VMEM((2, size, 128), F32),
             pltpu.SemaphoreType.DMA((2 * mine[0].shape[0], 2)),
         ],
         compiler_params=params(*mine, *theirs),
@@ -820,8 +869,7 @@
         delta,
         pack,
         acc,
-        in_own,
-        in_other,
+        weights,
         *mine,
         *theirs,
     )
@@ -839,8 +887,8 @@
     delta_in,
     pack_own,
     pack_other,
-    in_own,
-    in_other,
+    _,
+    w_ref,
     mine_low,
     mine_high,
     theirs_low,
@@ -852,7 +900,6 @@
     delta_ref,
     do_ref,
     raws,
-    w_ref,
     kv_ref,
     id_ref,
     state,
@@ -862,10 +909,10 @@
     rows_per = size // (2 * dim)
     sources = (mine_low, mine_high, theirs_low, theirs_high)
     fetch_prompts(meta, local, table, sources, raws, state, sem)
-    join_weights(meta, in_own, in_other, w_ref, 1)
     acc_ref[...] = jnp.zeros(acc_ref.shape, F32)
-    lse_ref[0] = lse_in[...]
-    delta_ref[0] = delta_in[...]
+    for h in range(2):
+        lse_ref[0, h] = column_of(lse_in[h : h + 1, :])
+        delta_ref[0, h] = column_of(delta_in[h : h + 1, :])
     do_ref[0] = pack_own[pl.ds(0, size), :]
     do_ref[1] = pack_other[pl.ds(0, size), :]
     for h in range(2):
@@ -910,15 +957,15 @@
     delta,
     pack,
     pack_other,
+    flag,
     prompt_mine,
     prompt_theirs,
-    in_own,
-    in_other,
+    weights,
     factor,
     block,
 ):
     size, dim = q_own.shape[1], q_own.shape[2] // 2
-    buffers, flags = prompt_scratch(prompt_mine, in_own.shape[1], dim, block)
+    buffers, flags = prompt_scratch(prompt_mine, dim, block)
     return pl.pallas_call(
         functools.partial(prompt_query_grad_kernel, block, factor),
         out_shape=(
@@ -949,8 +996,8 @@
         delta,
         pack,
         pack_other,
-        in_own,
-        in_other,
+        flag,
+        weights,
         *prompt_mine,
         *prompt_theirs,
     )
@@ -1019,24 +1066,20 @@
     ids_ref,
     low_ref,
     high_ref,
-    own_ref,
-    in_own,
-    in_other,
+    kv_ref,
+    _,
+    w_ref,
     keep_ref,
     send_ref,
     dk_ref,
     dv_ref,
-    w_ref,
-    kv_ref,
 ):
     half = q_ref.shape[1]
-    block, width = own_ref.shape
-    dim = in_own.shape[2]
+    block, width = kv_ref.shape[0], w_ref.shape[0]
+    dim = kv_ref.shape[1] // 4
     number = meta[0] * block // PLEN
     dk_ref[...] = jnp.zeros(dk_ref.shape, F32)
     dv_ref[...] = jnp.zeros(dv_ref.shape, F32)
-    join_weights(meta, in_own, in_other, w_ref, 1)
-    kv_ref[...] = mm(own_ref[...].astype(BF), w_ref[...]).astype(BF)
 
     def visit(data, carry):
         begin, end = starts[data], starts[data + 1]
@@ -1066,9 +1109,9 @@
     keep_ref[...] = mm_nt(grads, keep)
 
 
-def prompt_grad(meta, starts, table, q_all, ids_all, packs, own, in_own, in_other, factor, data_count):
-    block, width = own.shape
-    dim = in_own.shape[2]
+def prompt_grad(meta, starts, table, q_all, ids_all, packs, kv, flag, weights, factor, data_count):
+    block, width = kv.shape[0], weights.shape[0]
+    dim = kv.shape[1] // 4
     return pl.pallas_call(
         functools.partial(prompt_grad_kernel, data_count, factor),
         out_shape=(
@@ -1080,13 +1123,11 @@
         scratch_shapes=[
             pltpu.VMEM((block, 2 * dim), F32),
             pltpu.VMEM((block, 2 * dim), F32),
-            pltpu.VMEM((width, 4 * dim), BF),
-            pltpu.VMEM((block, 4 * dim), BF),
         ],
         compiler_params=params(q_all, *packs),
         cost_estimate=cost(6e9, 16e6, 4e6),
         name="prompt_grad",
-    )(meta, starts, table, q_all, ids_all, *packs, own, in_own, in_other)
+    )(meta, starts, table, q_all, ids_all, *packs, kv, flag, weights)
 
 
 def token_grad_kernel(
@@ -1098,28 +1139,26 @@
     ids_ref,
     low_ref,
     high_ref,
-    tok_ref,
+    kv_ref,
     own_ids,
     dq_ref,
     dq_other,
-    in_own,
-    in_other,
+    wq_ref,
+    wkv_ref,
     out_ref,
+    flag,
     dk_ref,
     dv_ref,
-    w_ref,
-    kv_ref,
     id_ref,
 ):
-    size = tok_ref.shape[1]
+    raise_flag(flag)
+    size = kv_ref.shape[0]
     half = q_ref.shape[1]
-    dim = in_own.shape[2]
+    dim = kv_ref.shape[1] // 4
     base = meta[0] * size
     first, last = key_range(starts, base, base + size, data_count)
     dk_ref[...] = jnp.zeros(dk_ref.shape, F32)
     dv_ref[...] = jnp.zeros(dv_ref.shape, F32)
-    join_weights(meta, in_own, in_other, w_ref, 0)
-    kv_ref[...] = mm(tok_ref[meta[1]], w_ref[:, 2 * dim :]).astype(BF)
     id_ref[...] = column_of(own_ids[meta[1]])
 
     def step(index, carry):
@@ -1131,54 +1170,52 @@
     lax.fori_loop(first // half, (last + half - 1) // half, step, 0)
     dq = (dq_ref[...] + dq_other[...].astype(F32)).astype(BF)
     grads = jnp.concatenate(
-        [dq, (dk_ref[...] * dim ** (-0.5)).astype(BF), dv_ref[...].astype(BF)], axis=1
-    )
-    out_ref[...] = mm_nt(grads, w_ref[...]).astype(BF)
+        [(dk_ref[...] * dim ** (-0.5)).astype(BF), dv_ref[...].astype(BF)], axis=1
+    )
+    out_ref[...] = (mm_nt(dq, wq_ref[...]) + mm_nt(grads, wkv_ref[...])).astype(BF)
 
 
 def token_grad(
-    meta, starts, q_all, ids_all, packs, tokens, ids_rows, dq, in_own, in_other, factor, data_count
+    meta, starts, q_all, ids_all, packs, kv_own, ids_rows, dq, weights, factor, data_count
 ):
-    size, width = tokens.shape[1:]
-    dim = in_own.shape[2]
+    size, dim = kv_own.shape[0], kv_own.shape[1] // 4
+    width = weights[0].shape[0]
     return pl.pallas_call(
         functools.partial(token_grad_kernel, data_count, factor),
-        out_shape=jax.ShapeDtypeStruct((size, width), BF),
+        out_shape=(jax.ShapeDtypeStruct((size, width), BF), flag_shape()),
         in_specs=[smem()] * 2 + [vmem()] * 10,
-        out_specs=vmem(),
+        out_specs=[vmem()] * 2,
         scratch_shapes=[
             pltpu.VMEM((size, 2 * dim), F32),
             pltpu.VMEM((size, 2 * dim), F32),
-            pltpu.VMEM((width, 6 * dim), BF),
-            pltpu.VMEM((size, 4 * dim), BF),
             pltpu.VMEM((size, 128), F32),
         ],
         compiler_params=params(spare=VMEM_LIMIT),
         cost_estimate=cost(4e9, 16e6, 4e6),
         name="token_grad",
-    )(meta, starts, q_all, ids_all, *packs, tokens, ids_rows, *dq, in_own, in_other)
-
-
-def sum_prompt_kernel(a_ref, b_ref, sum_ref, square_ref):
+    )(meta, starts, q_all, ids_all, *packs, kv_own, ids_rows, *dq, *weights)
+
+
+def sum_prompt_kernel(a_ref, b_ref, _, sum_ref, square_ref):
     low = (a_ref[...].astype(F32) + b_ref[...].astype(F32)).astype(BF)
     sum_ref[...] = low
     value = low.astype(F32)
     square_ref[...] = jnp.broadcast_to(jnp.sum(value * value, keepdims=True), square_ref.shape)
 
 
-def sum_prompt(a, b):
+def sum_prompt(a, b, flag):
     return pl.pallas_call(
         sum_prompt_kernel,
         out_shape=(
             jax.ShapeDtypeStruct(a.shape, BF),
             jax.ShapeDtypeStruct((8, 128), F32),
         ),
-        in_specs=[vmem(), vmem()],
+        in_specs=[vmem()] * 3,
         out_specs=[vmem(), vmem()],
         compiler_params=params(),
         cost_estimate=cost(4 * a.size, 6 * a.size),
         name="sum_prompt",
-    )(a, b)
+    )(a, b, flag)
 
 
 def optimizer_kernel(
@@ -1194,6 +1231,7 @@
     one_out,
     two_out,
     new_out,
+    norm_ref,
     held,
     sem,
 ):
@@ -1201,7 +1239,8 @@
     block = prompts.shape[0]
     tiles = sem.shape[1]
     tile = block // tiles
-    norm = jnp.sqrt(squares[0:1, :])
+    norm_ref[...] = jnp.sqrt(squares[...])
+    norm = norm_ref[0:1, :]
     factor = jnp.minimum(1.0, CLIP_NORM / (norm + 1e-06))
     copies = []
     for index in range(tiles):
@@ -1234,9 +1273,9 @@
     shape = jax.ShapeDtypeStruct((block, width), F32)
     return pl.pallas_call(
         optimizer_kernel,
-        out_shape=(shape,) * 4,
+        out_shape=(shape,) * 4 + (jax.ShapeDtypeStruct(squares.shape, F32),),
         in_specs=[smem(), smem()] + [vmem()] * 6,
-        out_specs=[hbm()] * 4,
+        out_specs=[hbm()] * 4 + [vmem()],
         scratch_shapes=[
             pltpu.VMEM((4, block, width), F32),
             pltpu.SemaphoreType.DMA((4, tiles)),
@@ -1311,6 +1350,8 @@
     orders, later = bit_orders(row_count), prompt_orders(row_count)
     stages = len(orders[0])
     held, prompt_held = shard[None], prompt_own[None]
+    tok = lax.dynamic_index_in_dim(tokens, batch, 0, keepdims=False)
+    cot = lax.dynamic_index_in_dim(cotangent, batch, 0, keepdims=False)
 
     def prompt_stage(place):
         other = gather_stage(prompt_held, place, later, row_count, head_count)
@@ -1318,8 +1359,8 @@
 
     for place in range(stages):
         if place == stages - 1:
-            held, in_other, w_along, meta, (biases, local, ids_rows) = lax.optimization_barrier(
-                (held, in_other, w_along, meta, (biases, local, ids_rows))
+            held, in_other, meta, (biases, local, ids_rows, tok, cot) = lax.optimization_barrier(
+                (held, in_other, meta, (biases, local, ids_rows, tok, cot))
             )
         if place != 1:
             held, prompt_held = lax.optimization_barrier((held, prompt_held))
@@ -1331,7 +1372,7 @@
         if place == 0:
             held, prompt_held = lax.optimization_barrier((held, prompt_held))
     theirs_low = swap_head(held, 1, head_count)
-    other, prompt_held = lax.optimization_barrier((other, prompt_held))
+    other, prompt_held, w_along = lax.optimization_barrier((other, prompt_held, w_along))
     mine = (held, other)
     prompt_high = gather_stage(prompt_held, stages - 1, later, row_count, head_count)
     theirs = (theirs_low, swap_head(other, 1, head_count))
@@ -1343,12 +1384,12 @@
         (ids_all.reshape(1, -1) < numbers.astype(F32)[:, None]).astype(jnp.int32), axis=1
     )
     ids_all = ids_all.reshape(row_count, 1, size)
-    q_own, *state = token_forward(
+    q_own, kv_own, w_q, w_kv, *state, flag = token_forward(
         meta, starts, tokens, ids_rows, mine, theirs, attn_in, in_other, factor, data_count
     )
     prompt_theirs_low = swap_head(prompt_held, 1, head_count)
-    prompt_high, state, prompt_theirs_low, w_core, w_far = lax.optimization_barrier(
-        (prompt_high, state, prompt_theirs_low, w_core, w_far)
+    prompt_high, flag, prompt_theirs_low, w_core, w_far = lax.optimization_barrier(
+        (prompt_high, flag, prompt_theirs_low, w_core, w_far)
     )
     prompt_mine = (prompt_held, prompt_high)
     prompt_theirs = (prompt_theirs_low, swap_head(prompt_high, 1, head_count))
@@ -1359,14 +1400,17 @@
         q_own,
         ids_rows,
         state,
+        flag,
         prompt_mine,
         prompt_theirs,
-        attn_in,
-        in_other,
+        w_kv,
         factor,
         block,
     )
+    prompt_low, send_half = lax.optimization_barrier((prompts.astype(BF), send_half))
+    prompt_kv = jnp.dot(prompt_low, w_kv, preferred_element_type=F32).astype(BF)
     o_mine, wide_out, lse = join_halves(wide_half, lse_half, swap_head(send_half, 2, head_count))
+    o_mine, prompt_kv = lax.optimization_barrier((o_mine, prompt_kv))
     o_theirs = swap_head(o_mine, 1, head_count)
     out, grad_sum, pack, delta = feed(
         meta,
@@ -1374,8 +1418,8 @@
         o_theirs,
         wide_out,
         lse,
-        tokens,
-        cotangent,
+        tok,
+        cot,
         (w_own, w_along, w_core, w_far),
         down_bias.reshape(1, width),
         norm_gains,
@@ -1385,10 +1429,10 @@
 
     def tie_query_grads(stages_left, held):
         if stages_left == 3:
-            held, here = lax.optimization_barrier((held, in_other))
-            tied["q"] = project_query(meta, mine, theirs, attn_in, here)
+            held, here = lax.optimization_barrier((held, w_q))
+            tied["q"], tied["flag"] = project_query(mine, theirs, here)
         if stages_left == 2:
-            held, other, tied["q"] = lax.optimization_barrier((held, pack_other, tied["q"]))
+            held, other, flag = lax.optimization_barrier((held, pack_other, tied["flag"]))
             tied["dq"] = prompt_query_grad(
                 meta,
                 local,
@@ -1399,29 +1443,29 @@
                 delta,
                 pack,
                 other,
+                flag,
                 prompt_mine,
                 prompt_theirs,
-                attn_in,
-                in_other,
+                w_kv,
                 factor,
                 block,
             )
         if stages_left == 1:
-            held, (acc, dq_send) = lax.optimization_barrier((held, tied["dq"]))
+            acc, dq_send = tied["dq"]
+            held, dq_send, ids_here = lax.optimization_barrier((held, dq_send, ids_rows))
             tied["dq_other"] = swap_head(dq_send, 2, head_count)
-            tied["dq"] = token_query_grad(
+            tied["dq"], tied["flag"] = token_query_grad(
                 meta,
                 starts,
                 q_own,
-                ids_rows,
+                ids_here,
                 lse,
                 delta,
                 pack,
                 acc,
                 mine,
                 theirs,
-                attn_in,
-                in_other,
+                w_kv,
                 factor,
                 data_count,
             )
@@ -1431,34 +1475,34 @@
     out_half = swap_head(out_half, 2, head_count)
     packs = gather_rows(pack, row_count, head_count, tie_query_grads)
     q_all = tied["q"]
-    packs, dq, dq_other, out_half = lax.optimization_barrier(
-        (packs, tied["dq"], tied["dq_other"], out_half)
+    dq = tied["dq"]
+    packs, dq_other, out_half, flag = lax.optimization_barrier(
+        (packs, tied["dq_other"], out_half, tied["flag"])
     )
     keep, send = prompt_grad(
-        meta, starts, prompt_map, q_all, ids_all, packs, prompts, attn_in, in_other, factor, data_count
+        meta, starts, prompt_map, q_all, ids_all, packs, prompt_kv, flag, w_kv, factor, data_count
     )
 
     pair = keep + swap_head(send, 1, head_count).astype(F32)
     pair_low = lax.reduce_precision(pair, 8, 7).astype(BF)
-    dq, pair_low = lax.optimization_barrier((dq, pair_low))
+    pair_low, ids_here = lax.optimization_barrier((pair_low, ids_rows))
     pair_other = swap_head(pair_low, 2, head_count)
     out_rest = swap_head(out_half, 1, head_count)
-    token_part = token_grad(
+    token_part, flag = token_grad(
         meta,
         starts,
         q_all,
         ids_all,
         packs,
-        tokens,
-        ids_rows,
+        kv_own,
+        ids_here,
         (dq, dq_other),
-        attn_in,
-        in_other,
+        (w_q, w_kv),
         factor,
         data_count,
     )
-    token_part, pair_other = lax.optimization_barrier((token_part, pair_other))
-    full_low, squares = sum_prompt(pair_low, pair_other)
+    pair_other, flag = lax.optimization_barrier((pair_other, flag))
+    full_low, squares = sum_prompt(pair_low, pair_other, flag)
     full_other = swap_head(full_low, 1, head_count)
 
     def both_batches(own, here, rest):
@@ -1478,18 +1522,16 @@
         if stages_done == 1:
             value, _ = lax.optimization_barrier((value, total))
         if stages_done == 2:
-            value, tied["half"], tied["out"] = lax.optimization_barrier(
-                (value, other_half, layer_out)
-            )
+            value, tied["out"] = lax.optimization_barrier((value, layer_out))
         return value
 
     squares = xor_sum(squares, row_count, head_count, tie_sum)
-    other_half, layer_out = tied["half"], tied["out"]
+    clipped, new_one, new_two, new_prompts, norm = optimizer(
+        meta, biases, full_low, full_other, squares, prompts, moment_one, moment_two
+    )
+    other_half, norm = lax.optimization_barrier((other_half, norm))
     input_grad = both_batches(total, other_half, swap_head(other_half, 1, head_count))
-    clipped, new_one, new_two, new_prompts = optimizer(
-        meta, biases, full_low, full_other, squares, prompts, moment_one, moment_two
-    )
-    return (layer_out, input_grad, clipped, jnp.sqrt(squares[0, 0]), new_one, new_two, new_prompts)
+    return (tied["out"], input_grad, clipped, norm[0, 0], new_one, new_two, new_prompts)
 
 
 def solution(mesh):

time: 219 us -> 210 us (0.959)
  waiting for transfers between devices: 83.8 us -> 69.5 us
  Pallas kernels: 53.9 us -> 66.4 us
  other arithmetic: 8.23 us -> 14.1 us
  local copies, waits for them, and re-layouts: 17.6 us -> 11.8 us
  starting transfers between devices: 48.5 us -> 43.1 us
    unnamed x148 -> x90, local copies, waits for them, and re-layouts: 14.3 us -> 5.74 us
    ppermute x9, starting transfers between devices: 17.1 us -> 10.1 us  [gather_stage(): return lax.ppermute(held, BOTH, pairs)]
    pallas_call x1, Pallas kernels: 7.89 us -> 14.8 us  [prompt_forward(): pl.pallas_call(functools.partial(prompt_forward_kernel, block, factor), o...]
    ppermute x20, starting transfers between devices: 15.7 us -> 22.4 us  [swap_head(): lax.ppermute(value, 'head', [(i, i ^ mask) for i in range(head_count)])]
    ppermute x20, waiting for transfers between devices: 29.5 us -> 22.9 us  [swap_head(): lax.ppermute(value, 'head', [(i, i ^ mask) for i in range(head_count)])]
    ppermute x6, starting transfers between devices: 15.7 us -> 10.6 us  [moved(): return lax.ppermute(value, BOTH, [(i, i ^ mask) for i in range(count)])]
    pallas_call x1, Pallas kernels: 7.59 us -> 11.8 us  [prompt_query_grad(): pl.pallas_call(functools.partial(prompt_query_grad_kernel, block, factor)...]
    ppermute x6, waiting for transfers between devices: 6.29 us -> 2.38 us  [moved(): return lax.ppermute(value, BOTH, [(i, i ^ mask) for i in range(count)])]
  transfers between devices with their start and end apart: 35 -> 35, of which waited for: 22 -> 19; matrix products, arithmetic and copies ran while one was open for 3% -> 8% of each run, Pallas kernels for 15% -> 19%
where the time goes in v2:
time: 210 us; the launch traced here: 209 us
  waiting for transfers between devices  69.5 us (33%)
  Pallas kernels  66.4 us (32%)
  starting transfers between devices  43.1 us (21%)
  other arithmetic  14.1 us (7%)
  local copies, waits for them, and re-layouts  11.8 us (6%)
  between operations  2.15 us (1%)
    ppermute x9, waiting for transfers between devices, gather_stage(): return lax.ppermute(held, BOTH, pairs)  44.2 us
    ppermute x20, waiting for transfers between devices, swap_head(): lax.ppermute(value, 'head', [(i, i ^ mask) for i in range(head_count)])  22.9 us
    ppermute x20, starting transfers between devices, swap_head(): lax.ppermute(value, 'head', [(i, i ^ mask) for i in range(head_count)])  22.4 us
    pallas_call x1, Pallas kernels, prompt_forward(): pl.pallas_call(functools.partial(prompt_forward_kernel, block, factor), o...  14.8 us
    pallas_call x1, Pallas kernels, prompt_query_grad(): pl.pallas_call(functools.partial(prompt_query_grad_kernel, block, factor)...  11.8 us
    ppermute x6, starting transfers between devices, moved(): return lax.ppermute(value, BOTH, [(i, i ^ mask) for i in range(count)])  10.6 us
    ppermute x9, starting transfers between devices, gather_stage(): return lax.ppermute(held, BOTH, pairs)  10.1 us
    pallas_call x1, Pallas kernels, feed(): pl.pallas_call(feed_kernel, out_shape=(jax.ShapeDtypeStruct((size, width)...  8.5 us
  transfers between devices with their start and end apart: 35, of which 19 were waited for; matrix products, arithmetic and copies ran while one was open for 8% of the time, Pallas kernels for 19%

profile of v2, /device:TPU:0, one launch (start us, length us, event | category | flops | bytes accessed | tf_op | source)
XLA Modules:
  0.0 209.0 jit_solution(248762302292705531)
XLA Ops:
  3.6 4.1 %collective-permute-start.1 = (bf16[1,512,256]{2,1,0:T(8,128)(2,1)S(1)}, bf16[1,512,256]{2,1,0:T(8,128)(2,1)S(1)}, u32[]{:S(2)}, u32[]{:S(2)}) collective-permute-start(bf16[1,512,256]{2,1,0:T(8,128)(2,1)S(1)} %fusion.2), channel_id=1, source_target_pairs={{0,16},{1,9},{2,18},{3,11},{4,20},{5,13},{6,22},{7,15},{8,24},{9,1... | collective-permute-start | bytes 786440 | tf_op jit(solution)/shard_map/ppermute | solution.py:83
  11.5 8.8 %collective-permute-done.1 = bf16[1,512,256]{2,1,0:T(8,128)(2,1)S(1)} collective-permute-done((bf16[1,512,256]{2,1,0:T(8,128)(2,1)S(1)}, bf16[1,512,256]{2,1,0:T(8,128)(2,1)S(1)}, u32[]{:S(2)}, u32[]{:S(2)}) %collective-permute-start.1) | collective-permute-done | bytes 262176 | tf_op jit(solution)/shard_map/ppermute | solution.py:83
  22.3 1.8 fusion.1.w_own
  24.1 2.2 %dynamic-slice_bitcast_fusion = (bf16[512,512]{1,0:T(8,128)(2,1)}, bf16[512,512]{1,0:T(8,128)(2,1)}) fusion(bf16[2,512,512]{2,1,0:T(8,128)(2,1)} %param.17, s32[]{:T(128)S(6)} %select_n.76, bf16[2,512,512]{2,1,0:T(8,128)(2,1)S(1)} %copy-done.36), kind=kLoop, calls=%fused_computation.20 | loop fusion | bytes 2097156 | tf_op jit(solution)/shard_map/jit(dynamic_index_in_dim)/squeeze | solution.py:1354
  26.3 10.7 %collective-permute-done.2 = bf16[2,272,512]{2,1,0:T(8,128)(2,1)} collective-permute-done((bf16[2,272,512]{2,1,0:T(8,128)(2,1)S(1)}, bf16[2,272,512]{2,1,0:T(8,128)(2,1)}, u32[]{:S(2)}, u32[]{:S(2)}) %collective-permute-start.2) | collective-permute-done | bytes 557088 | tf_op jit(solution)/shard_map/ppermute | solution.py:83
  38.2 2.1 %collective-permute-start.6 = (bf16[656,512]{1,0:T(8,128)(2,1)}, bf16[656,512]{1,0:T(8,128)(2,1)}, u32[]{:S(2)}, u32[]{:S(2)}) collective-permute-start(bf16[656,512]{1,0:T(8,128)(2,1)} %fusion.1.w_own), channel_id=1, source_target_pairs={{0,2},{1,3},{2,0},{3,1},{4,6},{5,7},{6,4},{7,5},{8,10},{9,11},{10,... | collective-permute-start | bytes 2015240 | tf_op jit(solution)/shard_map/ppermute | solution.py:122
  41.9 13.3 %collective-permute-done.5 = bf16[2,512,256]{2,1,0:T(8,128)(2,1)S(1)} collective-permute-done((bf16[2,512,256]{2,1,0:T(8,128)(2,1)S(1)}, bf16[2,512,256]{2,1,0:T(8,128)(2,1)S(1)}, u32[]{:S(2)}, u32[]{:S(2)}) %collective-permute-start.5) | collective-permute-done | bytes 524320 | tf_op jit(solution)/shard_map/ppermute | solution.py:83
  56.3 2.6 %collective-permute-done.4.mine_high.c = bf16[4,272,512]{2,1,0:T(8,128)(2,1)S(1)} collective-permute-done((bf16[4,272,512]{2,1,0:T(8,128)(2,1)S(1)}, bf16[4,272,512]{2,1,0:T(8,128)(2,1)S(1)}, u32[]{:S(2)}, u32[]{:S(2)}) %collective-permute-start.4) | collective-permute-done | bytes 1114144 | tf_op jit(solution)/shard_map/ppermute | solution.py:83
  63.3 7.6 %token_forward.1 = (bf16[2,512,256]{2,1,0:T(8,128)(2,1)}, bf16[512,512]{1,0:T(8,128)(2,1)}, bf16[512,256]{1,0:T(8,128)(2,1)}, bf16[512,512]{1,0:T(8,128)(2,1)}, ...) custom-call(s32[3]{0:T(128)} %pad_add_fusion.meta, ...), custom_call_target="tpu_custom_call" | custom-call | flops 8000000000 | bytes 8000000 | tf_op jit(solution)/shard_map/token_forward/pallas_call | solution.py:349
  71.0 3.5 %collective-permute-done.9.mine_high = bf16[4,512,256]{2,1,0:T(8,128)(2,1)} collective-permute-done((bf16[4,512,256]{2,1,0:T(8,128)(2,1)}, bf16[4,512,256]{2,1,0:T(8,128)(2,1)}, u32[]{:S(2)}, u32[]{:S(2)}) %collective-permute-start.9) | collective-permute-done | bytes 1048608 | tf_op jit(solution)/shard_map/ppermute | solution.py:83
  78.4 14.8 %prompt_forward.1 = (f32[512,256]{1,0:T(8,128)}, f32[2,512]{1,0:T(2,128)}, bf16[528,256]{1,0:T(8,128)(2,1)}) custom-call(s32[3]{0:T(128)} %pad_add_fusion.meta, s32[2,17]{1,0:T(2,128)} %copy.41.local, s32[2,16]{1,0:T(2,128)} %table.5, bf16[2,512,256]{2,1,0:T(8,128)(2,1)} %get-tuple-element.106.q_ref, f32[2,1,512]{2,1,0:T(1,128)} %reshape.65.ids_ref.own_ids, ...), custom_call_target="tpu_custom_call" | custom-call | flops 4000000000 | bytes 8000000 | tf_op jit(solution)/shard_map/prompt_forward/pallas_call | solution.py:580
  94.6 1.9 convolution_convert_fusion.kv_ref
  96.6 5.4 %collective-permute-done.14.other_ref = bf16[528,256]{1,0:T(8,128)(2,1)S(1)} collective-permute-done((bf16[528,256]{1,0:T(8,128)(2,1)}, bf16[528,256]{1,0:T(8,128)(2,1)S(1)}, u32[]{:S(2)}, u32[]{:S(2)}) %collective-permute-start.14) | collective-permute-done | bytes 270368 | tf_op jit(solution)/shard_map/ppermute | solution.py:122
  104.3 8.5 %feed.1 = (bf16[512,512]{1,0:T(8,128)(2,1)S(1)}, f32[512,512]{1,0:T(8,128)S(1)}, bf16[544,256]{1,0:T(8,128)(2,1)S(1)}, f32[2,512]{1,0:T(2,128)S(1)}) custom-call(s32[3]{0:T(128)S(1)} %copy-done.19, bf16[512,256]{1,0:T(8,128)(2,1)S(1)} %get-tuple-element.123.mine, bf16[512,256]{1,0:T(8,128)(2,1)S(1)} %collective-permute-done.15.theirs, ...), custom_call_target="tpu_custom_call" | custom-call | flops 3000000000 | bytes 8000000 | tf_op jit(solution)/shard_map/feed/pallas_call | solution.py:757
  113.8 2.5 %collective-permute-start.16 = (bf16[1,544,256]{2,1,0:T(8,128)(2,1)S(1)}, bf16[1,544,256]{2,1,0:T(8,128)(2,1)S(1)}, u32[]{:S(2)}, u32[]{:S(2)}) collective-permute-start(bf16[1,544,256]{2,1,0:T(8,128)(2,1)S(1)} %bitcast.39), channel_id=1, source_target_pairs={{0,4},{1,17},{2,6},{3,19},{4,0},{5,21},{6,2},{7,23},{8,12},{9,25},... | collective-permute-start | bytes 835592 | tf_op jit(solution)/shard_map/ppermute | solution.py:83
  116.3 1.7 collective-permute-start.17
  118.1 3.4 %project_query.1 = (bf16[2,4,2,256,256]{4,3,2,1,0:T(8,128)(2,1)S(1)}, f32[8,128]{1,0:T(8,128)S(1)}) custom-call(bf16[4,272,512]{2,1,0:T(8,128)(2,1)S(1)} %copy-done.2, bf16[4,272,512]{2,1,0:T(8,128)(2,1)S(1)} %copy-done.8, bf16[4,272,512]{2,1,0:T(8,128)(2,1)S(1)} %copy-done.6, bf16[4,272,512]{2,1,0:T(8,128)(2,1)} %collective-permute-done.8.theirs_high.d, ...), custom_call_target="tpu_custom_call" | custom-call | flops 1073741824 | bytes 4194304 | tf_op jit(solution)/shard_map/project_query/pallas_call | solution.py:179
  122.9 11.8 %prompt_query_grad.1 = (f32[2,512,128]{2,1,0:T(8,128)S(1)}, bf16[512,256]{1,0:T(8,128)(2,1)S(1)}) custom-call(s32[3]{0:T(128)S(1)} %copy-done.19, s32[2,17]{1,0:T(2,128)S(1)} %copy-done.21, s32[2,16]{1,0:T(2,128)S(1)} %copy-done.30, bf16[2,512,256]{2,1,0:T(8,128)(2,1)S(1)} %copy-done.34, f32[2,1,512]{2,1,0:T(1,128)S(1)} %copy-done.18, ...), custom_call_target="tpu_custom_call" | custom-call | flops 6000000000 | bytes 16000000 | tf_op jit(solution)/shard_map/prompt_query_grad/pallas_call | solution.py:969
  134.7 2.6 %collective-permute-done.18 = bf16[2,544,256]{2,1,0:T(8,128)(2,1)S(1)} collective-permute-done((bf16[2,544,256]{2,1,0:T(8,128)(2,1)S(1)}, bf16[2,544,256]{2,1,0:T(8,128)(2,1)S(1)}, u32[]{:S(2)}, u32[]{:S(2)}) %collective-permute-start.18) | collective-permute-done | bytes 557088 | tf_op jit(solution)/shard_map/ppermute | solution.py:83
  139.7 4.5 %token_query_grad.1 = (f32[512,256]{1,0:T(8,128)S(1)}, f32[8,128]{1,0:T(8,128)S(1)}) custom-call(s32[3]{0:T(128)S(1)} %copy-done.19, s32[17]{0:T(128)S(1)} %copy-done.22, bf16[2,512,256]{2,1,0:T(8,128)(2,1)S(1)} %copy-done.34, f32[2,1,512]{2,1,0:T(1,128)S(1)} %copy-done.18, f32[2,512]{1,0:T(2,128)S(1)} %get-tuple-element.125.lse_ref.lse_in, ...), custom_call_target="tpu_custom_call" | custom-call | flops 6000000000 | bytes 16000000 | tf_op jit(solution)/shard_map/token_query_grad/pallas_call | solution.py:847
  144.2 2.7 %collective-permute-done.21 = bf16[256,512]{1,0:T(8,128)(2,1)S(1)} collective-permute-done((bf16[256,512]{1,0:T(8,128)(2,1)S(1)}, bf16[256,512]{1,0:T(8,128)(2,1)S(1)}, u32[]{:S(2)}, u32[]{:S(2)}) %collective-permute-start.21) | collective-permute-done | bytes 262176 | tf_op jit(solution)/shard_map/ppermute | solution.py:122
  146.9 3.4 %collective-permute-done.20.dq_other = bf16[512,256]{1,0:T(8,128)(2,1)S(1)} collective-permute-done((bf16[512,256]{1,0:T(8,128)(2,1)S(1)}, bf16[512,256]{1,0:T(8,128)(2,1)S(1)}, u32[]{:S(2)}, u32[]{:S(2)}) %collective-permute-start.20) | collective-permute-done | bytes 262176 | tf_op jit(solution)/shard_map/ppermute | solution.py:122
  150.3 2.7 %collective-permute-done.19.high_ref = bf16[4,544,256]{2,1,0:T(8,128)(2,1)S(1)} collective-permute-done((bf16[4,544,256]{2,1,0:T(8,128)(2,1)S(1)}, bf16[4,544,256]{2,1,0:T(8,128)(2,1)S(1)}, u32[]{:S(2)}, u32[]{:S(2)}) %collective-permute-start.19) | collective-permute-done | bytes 1114144 | tf_op jit(solution)/shard_map/ppermute | solution.py:83
  153.0 3.0 %prompt_grad.1 = (f32[1000,256]{1,0:T(8,128)S(1)}, bf16[1000,256]{1,0:T(8,128)(2,1)S(1)}) custom-call(s32[3]{0:T(128)S(1)} %copy-done.19, s32[17]{0:T(128)S(1)} %copy-done.22, s32[2,16]{1,0:T(2,128)S(1)} %copy-done.30, bf16[16,256,256]{2,1,0:T(8,128)(2,1)S(1)} %bitcast.41, f32[8,1,512]{2,1,0:T(1,128)S(1)} %maximum_convert_fusion.2.ids_ref, ...), custom_call_target="tpu_custom_call" | custom-call | flops 6000000000 | bytes 16000000 | tf_op jit(solution)/shard_map/prompt_grad/pallas_call | solution.py:1115
  160.5 8.0 %collective-permute-start.23 = (bf16[1000,256]{1,0:T(8,128)(2,1)S(1)}, bf16[1000,256]{1,0:T(8,128)(2,1)S(1)}, u32[]{:S(2)}, u32[]{:S(2)}) collective-permute-start(bf16[1000,256]{1,0:T(8,128)(2,1)S(1)} %reduce-precision_convert_fusion.1.a_ref), channel_id=1, source_target_pairs={{0,2},{1,3},{2,0},{3,1},{4,6},{5,7},{6,4},{7,5},{8,10},{9,11},{10,... | collective-permute-start | bytes 1536008 | tf_op jit(solution)/shard_map/ppermute | solution.py:122
  168.5 6.9 %token_grad.1 = (bf16[512,512]{1,0:T(8,128)(2,1)}, f32[8,128]{1,0:T(8,128)}) custom-call(s32[3]{0:T(128)} %pad_add_fusion.meta, s32[17]{0:T(128)} %convert_reduce_fusion.starts, bf16[16,256,256]{2,1,0:T(8,128)(2,1)} %bitcast.42, f32[8,1,512]{2,1,0:T(1,128)} %copy-done.16, bf16[4,544,256]{2,1,0:T(8,128)(2,1)} %copy-done.9, bf16[4,544,256]{2,1,0:T(8,128)(2,1)} %copy-done.24, ...), custom_call_target="tpu_custom_call" | custom-call | flops 4000000000 | bytes 16000000 | tf_op jit(solution)/shard_map/token_grad/pallas_call | solution.py:1183
  176.4 4.1 %collective-permute-done.23.b_ref = bf16[1000,256]{1,0:T(8,128)(2,1)S(1)} collective-permute-done((bf16[1000,256]{1,0:T(8,128)(2,1)S(1)}, bf16[1000,256]{1,0:T(8,128)(2,1)S(1)}, u32[]{:S(2)}, u32[]{:S(2)}) %collective-permute-start.23) | collective-permute-done | bytes 512032 | tf_op jit(solution)/shard_map/ppermute | solution.py:122
  181.9 5.6 %collective-permute-start.26 = (f32[8,128]{1,0:T(8,128)S(1)}, f32[8,128]{1,0:T(8,128)S(1)}, u32[]{:S(2)}, u32[]{:S(2)}) collective-permute-start(f32[8,128]{1,0:T(8,128)S(1)} %get-tuple-element.161), channel_id=1, source_target_pairs={{0,5},{1,4},{2,7},{3,6},{4,1},{5,0},{6,3},{7,2},{8,13},{9,12},{10,... | collective-permute-start | bytes 12296 | tf_op jit(solution)/shard_map/ppermute | solution.py:101
  188.8 2.3 %collective-permute-done.25 = f32[8,128]{1,0:T(8,128)S(1)} collective-permute-done((f32[8,128]{1,0:T(8,128)S(1)}, f32[8,128]{1,0:T(8,128)S(1)}, u32[]{:S(2)}, u32[]{:S(2)}) %collective-permute-start.25) | collective-permute-done | bytes 4128 | tf_op jit(solution)/shard_map/ppermute | solution.py:101
  191.4 4.1 %collective-permute-start.29 = (f32[8,128]{1,0:T(8,128)S(1)}, f32[8,128]{1,0:T(8,128)S(1)}, u32[]{:S(2)}, u32[]{:S(2)}) collective-permute-start(f32[8,128]{1,0:T(8,128)S(1)} %add_add_fusion.1), channel_id=1, source_target_pairs={{0,16},{1,17},{2,18},{3,19},{4,20},{5,21},{6,22},{7,23},{8,24},{9,... | collective-permute-start | bytes 12296 | tf_op jit(solution)/shard_map/ppermute | solution.py:101
  195.8 2.8 %collective-permute-start.32 = (bf16[256,512]{1,0:T(8,128)(2,1)S(1)}, bf16[256,512]{1,0:T(8,128)(2,1)S(1)}, u32[]{:S(2)}, u32[]{:S(2)}) collective-permute-start(bf16[256,512]{1,0:T(8,128)(2,1)S(1)} %constant_dynamic-slice_fusion), channel_id=1, source_target_pairs={{0,2},{1,3},{2,0},{3,1},{4,6},{5,7},{6,4},{7,5},{8,10},{9,11},{10,... | collective-permute-start | bytes 786440 | tf_op jit(solution)/shard_map/ppermute | solution.py:122
  201.0 4.7 %optimizer.1 = (f32[1000,512]{1,0:T(8,128)}, f32[1000,512]{1,0:T(8,128)}, f32[1000,512]{1,0:T(8,128)}, f32[1000,512]{1,0:T(8,128)}, f32[8,128]{1,0:T(8,128)S(1)}) custom-call(s32[3]{0:T(128)S(1)} %copy-done.20, f32[2]{0:T(128)S(1)} %pad_maximum_fusion.9.biases, bf16[1000,256]{1,0:T(8,128)(2,1)S(1)} %get-tuple-element.168.mine, ...), custom_call_target="tpu_custom_call" | custom-call | flops 10240000 | bytes 16384000 | tf_op jit(solution)/shard_map/optimizer/pallas_call | solution.py:1274
  (182 shorter events, 42.7 us)
Async XLA Ops:
  3.6 16.7 %collective-permute-start.1 = (bf16[1,512,256]{2,1,0:T(8,128)(2,1)S(1)}, bf16[1,512,256]{2,1,0:T(8,128)(2,1)S(1)}, u32[]{:S(2)}, u32[]{:S(2)}) collective-permute-start(bf16[1,512,256]{2,1,0:T(8,128)(2,1)S(1)} %fusion.2), channel_id=1, source_target_pairs={{0,16},{1,9},{2,18},{3,11},{4,20},{5,13},{6,22},{7,15},{8,24},{9,1... | collective-permute-start | bytes 786440 | tf_op jit(solution)/shard_map/ppermute | solution.py:83
  7.7 12.6 %collective-permute-start = (bf16[1,272,512]{2,1,0:T(8,128)(2,1)S(1)}, bf16[1,272,512]{2,1,0:T(8,128)(2,1)S(1)}, u32[]{:S(2)}, u32[]{:S(2)}) collective-permute-start(bf16[1,272,512]{2,1,0:T(8,128)(2,1)S(1)} %maximum_bitcast_fusion), channel_id=1, source_target_pairs={{0,4},{1,17},{2,6},{3,19},{4,0},{5,21},{6,2},{7,23},{8,12},{9,25},... | collective-permute-start | bytes 835592 | tf_op jit(solution)/shard_map/ppermute | solution.py:83
  9.2 17.1 %collective-permute-start.3 = (bf16[3,512,128]{2,1,0:T(8,128)(2,1)}, bf16[3,512,128]{2,1,0:T(8,128)(2,1)}, u32[]{:S(2)}, u32[]{:S(2)}) collective-permute-start(bf16[3,512,128]{2,1,0:T(8,128)(2,1)} %in_own.1), channel_id=1, source_target_pairs={{0,2},{1,3},{2,0},{3,1},{4,6},{5,7},{6,4},{7,5},{8,10},{9,11},{10,... | collective-permute-start | bytes 1179656 | tf_op jit(solution)/shard_map/ppermute | solution.py:122
  20.4 16.6 %collective-permute-start.2 = (bf16[2,272,512]{2,1,0:T(8,128)(2,1)S(1)}, bf16[2,272,512]{2,1,0:T(8,128)(2,1)}, u32[]{:S(2)}, u32[]{:S(2)}) collective-permute-start(bf16[2,272,512]{2,1,0:T(8,128)(2,1)S(1)} %pad_maximum_fusion.3), channel_id=1, source_target_pairs={{0,16},{1,9},{2,18},{3,11},{4,20},{5,13},{6,22},{7,15},{8,24},{9,1... | collective-permute-start | bytes 1671176 | tf_op jit(solution)/shard_map/ppermute | solution.py:83
  38.1 20.7 %collective-permute-start.4 = (bf16[4,272,512]{2,1,0:T(8,128)(2,1)S(1)}, bf16[4,272,512]{2,1,0:T(8,128)(2,1)S(1)}, u32[]{:S(2)}, u32[]{:S(2)}) collective-permute-start(bf16[4,272,512]{2,1,0:T(8,128)(2,1)S(1)} %pad_maximum_fusion.mine_low.a), channel_id=1, source_target_pairs={{0,8},{1,5},{2,10},{3,7},{4,12},{5,1},{6,14},{7,3},{8,0},{9,13},{1... | collective-permute-start | bytes 3342344 | tf_op jit(solution)/shard_map/ppermute | solution.py:83
  38.2 18.1 %collective-permute-start.6 = (bf16[656,512]{1,0:T(8,128)(2,1)}, bf16[656,512]{1,0:T(8,128)(2,1)}, u32[]{:S(2)}, u32[]{:S(2)}) collective-permute-start(bf16[656,512]{1,0:T(8,128)(2,1)} %fusion.1.w_own), channel_id=1, source_target_pairs={{0,2},{1,3},{2,0},{3,1},{4,6},{5,7},{6,4},{7,5},{8,10},{9,11},{10,... | collective-permute-start | bytes 2015240 | tf_op jit(solution)/shard_map/ppermute | solution.py:122
  40.4 14.9 %collective-permute-start.5 = (bf16[2,512,256]{2,1,0:T(8,128)(2,1)S(1)}, bf16[2,512,256]{2,1,0:T(8,128)(2,1)S(1)}, u32[]{:S(2)}, u32[]{:S(2)}) collective-permute-start(bf16[2,512,256]{2,1,0:T(8,128)(2,1)S(1)} %pad_maximum_fusion.5), channel_id=1, source_target_pairs={{0,4},{1,17},{2,6},{3,19},{4,0},{5,21},{6,2},{7,23},{8,12},{9,25},... | collective-permute-start | bytes 1572872 | tf_op jit(solution)/shard_map/ppermute | solution.py:83
  41.9 19.6 %collective-permute-start.7 = (bf16[4,272,512]{2,1,0:T(8,128)(2,1)S(1)}, bf16[4,272,512]{2,1,0:T(8,128)(2,1)S(1)}, u32[]{:S(2)}, u32[]{:S(2)}) collective-permute-start(bf16[4,272,512]{2,1,0:T(8,128)(2,1)S(1)} %pad_maximum_fusion.mine_low.a), channel_id=1, source_target_pairs={{0,1},{1,0},{2,3},{3,2},{4,5},{5,4},{6,7},{7,6},{8,9},{9,8},{10,11... | collective-permute-start | bytes 3342344 | tf_op jit(solution)/shard_map/ppermute | solution.py:122
  58.9 4.4 %collective-permute-start.8 = (bf16[4,272,512]{2,1,0:T(8,128)(2,1)S(1)}, bf16[4,272,512]{2,1,0:T(8,128)(2,1)}, u32[]{:S(2)}, u32[]{:S(2)}) collective-permute-start(bf16[4,272,512]{2,1,0:T(8,128)(2,1)S(1)} %collective-permute-done.4.mine_high.c), channel_id=1, source_target_pairs={{0,1},{1,0},{2,3},{3,2},{4,5},{5,4},{6,7},{7,6},{8,9},{9,8},{10,11... | collective-permute-start | bytes 3342344 | tf_op jit(solution)/shard_map/ppermute | solution.py:122
  58.9 12.1 %collective-permute-start.10 = (bf16[4,512,256]{2,1,0:T(8,128)(2,1)}, bf16[4,512,256]{2,1,0:T(8,128)(2,1)}, u32[]{:S(2)}, u32[]{:S(2)}) collective-permute-start(bf16[4,512,256]{2,1,0:T(8,128)(2,1)} %pad_maximum_fusion.2.mine_low), channel_id=1, source_target_pairs={{0,1},{1,0},{2,3},{3,2},{4,5},{5,4},{6,7},{7,6},{8,9},{9,8},{10,11... | collective-permute-start | bytes 3145736 | tf_op jit(solution)/shard_map/ppermute | solution.py:122
  59.4 15.1 %collective-permute-start.9 = (bf16[4,512,256]{2,1,0:T(8,128)(2,1)}, bf16[4,512,256]{2,1,0:T(8,128)(2,1)}, u32[]{:S(2)}, u32[]{:S(2)}) collective-permute-start(bf16[4,512,256]{2,1,0:T(8,128)(2,1)} %pad_maximum_fusion.2.mine_low), channel_id=1, source_target_pairs={{0,8},{1,5},{2,10},{3,7},{4,12},{5,1},{6,14},{7,3},{8,0},{9,13},{1... | collective-permute-start | bytes 3145736 | tf_op jit(solution)/shard_map/ppermute | solution.py:83
  59.7 11.3 %collective-permute-start.11 = (bf16[656,512]{1,0:T(8,128)(2,1)}, bf16[656,512]{1,0:T(8,128)(2,1)}, u32[]{:S(2)}, u32[]{:S(2)}) collective-permute-start(bf16[656,512]{1,0:T(8,128)(2,1)} %fusion.1.w_own), channel_id=1, source_target_pairs={{0,1},{1,0},{2,3},{3,2},{4,5},{5,4},{6,7},{7,6},{8,9},{9,8},{10,11... | collective-permute-start | bytes 2015240 | tf_op jit(solution)/shard_map/ppermute | solution.py:122
  61.5 9.5 %collective-permute-start.12 = (bf16[656,512]{1,0:T(8,128)(2,1)}, bf16[656,512]{1,0:T(8,128)(2,1)}, u32[]{:S(2)}, u32[]{:S(2)}) collective-permute-start(bf16[656,512]{1,0:T(8,128)(2,1)} %collective-permute-done.6.w_along), channel_id=1, source_target_pairs={{0,1},{1,0},{2,3},{3,2},{4,5},{5,4},{6,7},{7,6},{8,9},{9,8},{10,11... | collective-permute-start | bytes 2015240 | tf_op jit(solution)/shard_map/ppermute | solution.py:122
  74.5 2.9 %collective-permute-start.13 = (bf16[4,512,256]{2,1,0:T(8,128)(2,1)}, bf16[4,512,256]{2,1,0:T(8,128)(2,1)S(1)}, u32[]{:S(2)}, u32[]{:S(2)}) collective-permute-start(bf16[4,512,256]{2,1,0:T(8,128)(2,1)} %collective-permute-done.9.mine_high), channel_id=1, source_target_pairs={{0,1},{1,0},{2,3},{3,2},{4,5},{5,4},{6,7},{7,6},{8,9},{9,8},{10,11... | collective-permute-start | bytes 3145736 | tf_op jit(solution)/shard_map/ppermute | solution.py:122
  93.2 8.8 %collective-permute-start.14 = (bf16[528,256]{1,0:T(8,128)(2,1)}, bf16[528,256]{1,0:T(8,128)(2,1)S(1)}, u32[]{:S(2)}, u32[]{:S(2)}) collective-permute-start(bf16[528,256]{1,0:T(8,128)(2,1)} %get-tuple-element.120), channel_id=1, source_target_pairs={{0,2},{1,3},{2,0},{3,1},{4,6},{5,7},{6,4},{7,5},{8,10},{9,11},{10,... | collective-permute-start | bytes 811016 | tf_op jit(solution)/shard_map/ppermute | solution.py:122
  113.8 7.6 %collective-permute-start.16 = (bf16[1,544,256]{2,1,0:T(8,128)(2,1)S(1)}, bf16[1,544,256]{2,1,0:T(8,128)(2,1)S(1)}, u32[]{:S(2)}, u32[]{:S(2)}) collective-permute-start(bf16[1,544,256]{2,1,0:T(8,128)(2,1)S(1)} %bitcast.39), channel_id=1, source_target_pairs={{0,4},{1,17},{2,6},{3,19},{4,0},{5,21},{6,2},{7,23},{8,12},{9,25},... | collective-permute-start | bytes 835592 | tf_op jit(solution)/shard_map/ppermute | solution.py:83
  116.3 6.5 %collective-permute-start.17 = (bf16[544,256]{1,0:T(8,128)(2,1)S(1)}, bf16[544,256]{1,0:T(8,128)(2,1)S(1)}, u32[]{:S(2)}, u32[]{:S(2)}) collective-permute-start(bf16[544,256]{1,0:T(8,128)(2,1)S(1)} %get-tuple-element.130.pack_own.do_ref), channel_id=1, source_target_pairs={{0,2},{1,3},{2,0},{3,1},{4,6},{5,7},{6,4},{7,5},{8,10},{9,11},{10,... | collective-permute-start | bytes 835592 | tf_op jit(solution)/shard_map/ppermute | solution.py:122
  122.9 14.5 %collective-permute-start.18 = (bf16[2,544,256]{2,1,0:T(8,128)(2,1)S(1)}, bf16[2,544,256]{2,1,0:T(8,128)(2,1)S(1)}, u32[]{:S(2)}, u32[]{:S(2)}) collective-permute-start(bf16[2,544,256]{2,1,0:T(8,128)(2,1)S(1)} %pad_maximum_fusion.4), channel_id=1, source_target_pairs={{0,16},{1,9},{2,18},{3,11},{4,20},{5,13},{6,22},{7,15},{8,24},{9,1... | collective-permute-start | bytes 1671176 | tf_op jit(solution)/shard_map/ppermute | solution.py:83
  137.4 15.6 %collective-permute-start.19 = (bf16[4,544,256]{2,1,0:T(8,128)(2,1)S(1)}, bf16[4,544,256]{2,1,0:T(8,128)(2,1)S(1)}, u32[]{:S(2)}, u32[]{:S(2)}) collective-permute-start(bf16[4,544,256]{2,1,0:T(8,128)(2,1)S(1)} %pad_maximum_fusion.1.low_ref), channel_id=1, source_target_pairs={{0,8},{1,5},{2,10},{3,7},{4,12},{5,1},{6,14},{7,3},{8,0},{9,13},{1... | collective-permute-start | bytes 3342344 | tf_op jit(solution)/shard_map/ppermute | solution.py:83
  137.6 9.3 %collective-permute-start.21 = (bf16[256,512]{1,0:T(8,128)(2,1)S(1)}, bf16[256,512]{1,0:T(8,128)(2,1)S(1)}, u32[]{:S(2)}, u32[]{:S(2)}) collective-permute-start(bf16[256,512]{1,0:T(8,128)(2,1)S(1)} %constant_dynamic-slice_fusion.1), channel_id=1, source_target_pairs={{0,2},{1,3},{2,0},{3,1},{4,6},{5,7},{6,4},{7,5},{8,10},{9,11},{10,... | collective-permute-start | bytes 786440 | tf_op jit(solution)/shard_map/ppermute | solution.py:122
  139.3 11.0 %collective-permute-start.20 = (bf16[512,256]{1,0:T(8,128)(2,1)S(1)}, bf16[512,256]{1,0:T(8,128)(2,1)S(1)}, u32[]{:S(2)}, u32[]{:S(2)}) collective-permute-start(bf16[512,256]{1,0:T(8,128)(2,1)S(1)} %get-tuple-element.142), channel_id=1, source_target_pairs={{0,2},{1,3},{2,0},{3,1},{4,6},{5,7},{6,4},{7,5},{8,10},{9,11},{10,... | collective-permute-start | bytes 786440 | tf_op jit(solution)/shard_map/ppermute | solution.py:122
  157.0 18.4 %collective-permute-start.31 = (bf16[256,512]{1,0:T(8,128)(2,1)S(1)}, bf16[256,512]{1,0:T(8,128)(2,1)}, u32[]{:S(2)}, u32[]{:S(2)}) collective-permute-start(bf16[256,512]{1,0:T(8,128)(2,1)S(1)} %collective-permute-done.21), channel_id=1, source_target_pairs={{0,1},{1,0},{2,3},{3,2},{4,5},{5,4},{6,7},{7,6},{8,9},{9,8},{10,11... | collective-permute-start | bytes 786440 | tf_op jit(solution)/shard_map/ppermute | solution.py:122
  160.5 20.0 %collective-permute-start.23 = (bf16[1000,256]{1,0:T(8,128)(2,1)S(1)}, bf16[1000,256]{1,0:T(8,128)(2,1)S(1)}, u32[]{:S(2)}, u32[]{:S(2)}) collective-permute-start(bf16[1000,256]{1,0:T(8,128)(2,1)S(1)} %reduce-precision_convert_fusion.1.a_ref), channel_id=1, source_target_pairs={{0,2},{1,3},{2,0},{3,1},{4,6},{5,7},{6,4},{7,5},{8,10},{9,11},{10,... | collective-permute-start | bytes 1536008 | tf_op jit(solution)/shard_map/ppermute | solution.py:122
  175.4 15.7 %collective-permute-start.27 = (bf16[512,512]{1,0:T(8,128)(2,1)}, bf16[512,512]{1,0:T(8,128)(2,1)S(1)}, u32[]{:S(2)}, u32[]{:S(2)}) collective-permute-start(bf16[512,512]{1,0:T(8,128)(2,1)} %get-tuple-element.163), channel_id=1, source_target_pairs={{0,1},{1,0},{2,3},{3,2},{4,5},{5,4},{6,7},{7,6},{8,9},{9,8},{10,11... | collective-permute-start | bytes 1572872 | tf_op jit(solution)/shard_map/ppermute | solution.py:122
  181.9 7.0 %collective-permute-start.26 = (f32[8,128]{1,0:T(8,128)S(1)}, f32[8,128]{1,0:T(8,128)S(1)}, u32[]{:S(2)}, u32[]{:S(2)}) collective-permute-start(f32[8,128]{1,0:T(8,128)S(1)} %get-tuple-element.161), channel_id=1, source_target_pairs={{0,5},{1,4},{2,7},{3,6},{4,1},{5,0},{6,3},{7,2},{8,13},{9,12},{10,... | collective-permute-start | bytes 12296 | tf_op jit(solution)/shard_map/ppermute | solution.py:101
  187.5 3.6 %collective-permute-start.25 = (f32[8,128]{1,0:T(8,128)S(1)}, f32[8,128]{1,0:T(8,128)S(1)}, u32[]{:S(2)}, u32[]{:S(2)}) collective-permute-start(f32[8,128]{1,0:T(8,128)S(1)} %get-tuple-element.161), channel_id=1, source_target_pairs={{0,4},{1,5},{2,6},{3,7},{4,0},{5,1},{6,2},{7,3},{8,12},{9,13},{10,... | collective-permute-start | bytes 12296 | tf_op jit(solution)/shard_map/ppermute | solution.py:101
  187.9 3.1 %collective-permute-start.24 = (f32[8,128]{1,0:T(8,128)S(1)}, f32[8,128]{1,0:T(8,128)S(1)}, u32[]{:S(2)}, u32[]{:S(2)}) collective-permute-start(f32[8,128]{1,0:T(8,128)S(1)} %get-tuple-element.161), channel_id=1, source_target_pairs={{0,1},{1,0},{2,3},{3,2},{4,5},{5,4},{6,7},{7,6},{8,9},{9,8},{10,11... | collective-permute-start | bytes 12296 | tf_op jit(solution)/shard_map/ppermute | solution.py:101
  188.2 12.0 %collective-permute-start.33 = (bf16[1000,256]{1,0:T(8,128)(2,1)S(1)}, bf16[1000,256]{1,0:T(8,128)(2,1)S(1)}, u32[]{:S(2)}, u32[]{:S(2)}) collective-permute-start(bf16[1000,256]{1,0:T(8,128)(2,1)S(1)} %get-tuple-element.168.mine), channel_id=1, source_target_pairs={{0,1},{1,0},{2,3},{3,2},{4,5},{5,4},{6,7},{7,6},{8,9},{9,8},{10,11... | collective-permute-start | bytes 1536008 | tf_op jit(solution)/shard_map/ppermute | solution.py:122
  191.4 8.8 %collective-permute-start.30 = (f32[8,128]{1,0:T(8,128)S(1)}, f32[8,128]{1,0:T(8,128)S(1)}, u32[]{:S(2)}, u32[]{:S(2)}) collective-permute-start(f32[8,128]{1,0:T(8,128)S(1)} %add_add_fusion.1), channel_id=1, source_target_pairs={{0,24},{1,25},{2,26},{3,27},{4,28},{5,29},{6,30},{7,31},{8,16},{9,... | collective-permute-start | bytes 12296 | tf_op jit(solution)/shard_map/ppermute | solution.py:101
  191.4 8.7 %collective-permute-start.29 = (f32[8,128]{1,0:T(8,128)S(1)}, f32[8,128]{1,0:T(8,128)S(1)}, u32[]{:S(2)}, u32[]{:S(2)}) collective-permute-start(f32[8,128]{1,0:T(8,128)S(1)} %add_add_fusion.1), channel_id=1, source_target_pairs={{0,16},{1,17},{2,18},{3,19},{4,20},{5,21},{6,22},{7,23},{8,24},{9,... | collective-permute-start | bytes 12296 | tf_op jit(solution)/shard_map/ppermute | solution.py:101
  195.5 4.6 %collective-permute-start.28 = (f32[8,128]{1,0:T(8,128)S(1)}, f32[8,128]{1,0:T(8,128)S(1)}, u32[]{:S(2)}, u32[]{:S(2)}) collective-permute-start(f32[8,128]{1,0:T(8,128)S(1)} %add_add_fusion.1), channel_id=1, source_target_pairs={{0,8},{1,9},{2,10},{3,11},{4,12},{5,13},{6,14},{7,15},{8,0},{9,1},... | collective-permute-start | bytes 12296 | tf_op jit(solution)/shard_map/ppermute | solution.py:101
  195.8 9.8 %collective-permute-start.32 = (bf16[256,512]{1,0:T(8,128)(2,1)S(1)}, bf16[256,512]{1,0:T(8,128)(2,1)S(1)}, u32[]{:S(2)}, u32[]{:S(2)}) collective-permute-start(bf16[256,512]{1,0:T(8,128)(2,1)S(1)} %constant_dynamic-slice_fusion), channel_id=1, source_target_pairs={{0,2},{1,3},{2,0},{3,1},{4,6},{5,7},{6,4},{7,5},{8,10},{9,11},{10,... | collective-permute-start | bytes 786440 | tf_op jit(solution)/shard_map/ppermute | solution.py:122
  (46 other events, 408.3 us)

commit v3 on v2

--- a/solution.py
+++ b/solution.py
@@ -696,7 +696,7 @@
     place_out = slice(hid, hid + dim)
     place_up = slice(hid + dim, 2 * hid + dim)
     place_bias = 2 * hid + dim
-    sub = min(256, size)
+    sub = size
     pack_ref[pl.ds(size, STATS), :] = jnp.zeros((STATS, 2 * dim), BF)
     g0, g1 = gains[0:1, :], gains[1:2, :]
     for part in range(size // sub):
@@ -1003,8 +1003,13 @@
     )
 
 
+def in_bank(meta, index, bank, slots):
+    slot = slot_of((index // 2) ^ meta[0], meta[2], bit_orders(2 * slots))
+    return (slot < slots) if bank == 0 else (slot >= slots)
+
+
 def half_shard(meta, index, q_ref, ids_ref, low_ref, high_ref):
-    slots, rows, double = low_ref.shape
+    slots, rows, double = (high_ref if low_ref is None else low_ref).shape
     half = q_ref.shape[1]
     size = rows - STATS
     shard, part = index // 2, index % 2
@@ -1014,12 +1019,19 @@
     in_low = slot < slots
     place_low, place_high = jnp.minimum(slot, slots - 1), jnp.maximum(slot - slots, 0)
     span = pl.ds(pl.multiple_of(part * half, half), half)
-    grad = jnp.where(in_low, low_ref[place_low, span, :], high_ref[place_high, span, :])
+    tail = pl.ds(size, STATS)
+
+    def take(rows):
+        if high_ref is None:
+            return low_ref[place_low, rows, :]
+        if low_ref is None:
+            return high_ref[place_high, rows, :]
+        return jnp.where(in_low, low_ref[place_low, rows, :], high_ref[place_high, rows, :])
+
+    grad = take(span)
     line = ids_ref[slot]
     line = jnp.where(part == 0, line[:, :half], line[:, half : 2 * half])
-    tail = pl.ds(size, STATS)
-    stats = jnp.where(in_low, low_ref[place_low, tail, :], high_ref[place_high, tail, :])
-    stats = stats.astype(F32)
+    stats = take(tail).astype(F32)
     rows_per = size // double
 
     def stat(head, kind):
@@ -1056,7 +1068,35 @@
         dk_ref[:, cols[h]] += mm(low[h], query[:, cols[h]])
 
 
-def prompt_grad_kernel(
+def prompt_terms(data_count, factor, bank, meta, starts, table, q_ref, ids_ref, pack_ref, kv_ref, dk_ref, dv_ref):
+    half = q_ref.shape[1]
+    number = meta[0] * kv_ref.shape[0] // PLEN
+    low_ref, high_ref = (pack_ref, None) if bank == 0 else (None, pack_ref)
+
+    def visit(data, carry):
+        begin, end = starts[data], starts[data + 1]
+
+        @pl.when((table[meta[1], data] == number) & (begin < end))
+        def _():
+            def step(index, inner):
+                @pl.when(in_bank(meta, index, bank, pack_ref.shape[0]))
+                def _():
+                    query, grad, line, stat = half_shard(
+                        meta, index, q_ref, ids_ref, low_ref, high_ref
+                    )
+                    mask = line == data.astype(F32)
+                    key_update(query, grad, kv_ref, mask, None, stat, factor, dk_ref, dv_ref)
+
+                return inner
+
+            lax.fori_loop(begin // half, (end + half - 1) // half, step, 0)
+
+        return carry
+
+    lax.fori_loop(0, data_count, visit, 0)
+
+
+def prompt_grad_first_kernel(
     data_count,
     factor,
     meta,
@@ -1064,40 +1104,46 @@
     table,
     q_ref,
     ids_ref,
-    low_ref,
-    high_ref,
+    pack_ref,
     kv_ref,
     _,
+    dk_ref,
+    dv_ref,
+    flag,
+):
+    raise_flag(flag)
+    dk_ref[...] = jnp.zeros(dk_ref.shape, F32)
+    dv_ref[...] = jnp.zeros(dv_ref.shape, F32)
+    prompt_terms(
+        data_count, factor, 0, meta, starts, table, q_ref, ids_ref, pack_ref, kv_ref, dk_ref, dv_ref
+    )
+
+
+def prompt_grad_last_kernel(
+    data_count,
+    factor,
+    meta,
+    starts,
+    table,
+    q_ref,
+    ids_ref,
+    pack_ref,
+    kv_ref,
+    dk_in,
+    dv_in,
     w_ref,
     keep_ref,
     send_ref,
     dk_ref,
     dv_ref,
 ):
-    half = q_ref.shape[1]
-    block, width = kv_ref.shape[0], w_ref.shape[0]
+    width = w_ref.shape[0]
     dim = kv_ref.shape[1] // 4
-    number = meta[0] * block // PLEN
-    dk_ref[...] = jnp.zeros(dk_ref.shape, F32)
-    dv_ref[...] = jnp.zeros(dv_ref.shape, F32)
-
-    def visit(data, carry):
-        begin, end = starts[data], starts[data + 1]
-
-        @pl.when((table[meta[1], data] == number) & (begin < end))
-        def _():
-            def step(index, inner):
-                query, grad, line, stat = half_shard(meta, index, q_ref, ids_ref, low_ref, high_ref)
-                key_update(
-                    query, grad, kv_ref, line == data.astype(F32), None, stat, factor, dk_ref, dv_ref
-                )
-                return inner
-
-            lax.fori_loop(begin // half, (end + half - 1) // half, step, 0)
-
-        return carry
-
-    lax.fori_loop(0, data_count, visit, 0)
+    dk_ref[...] = dk_in[...]
+    dv_ref[...] = dv_in[...]
+    prompt_terms(
+        data_count, factor, 1, meta, starts, table, q_ref, ids_ref, pack_ref, kv_ref, dk_ref, dv_ref
+    )
     grads = jnp.concatenate(
         [(dk_ref[...] * dim ** (-0.5)).astype(BF), dv_ref[...].astype(BF)], axis=1
     )
@@ -1109,11 +1155,25 @@
     keep_ref[...] = mm_nt(grads, keep)
 
 
-def prompt_grad(meta, starts, table, q_all, ids_all, packs, kv, flag, weights, factor, data_count):
+def prompt_grad_first(meta, starts, table, q_all, ids_all, pack, kv, flag, factor, data_count):
+    block, dim = kv.shape[0], kv.shape[1] // 4
+    shape = jax.ShapeDtypeStruct((block, 2 * dim), F32)
+    return pl.pallas_call(
+        functools.partial(prompt_grad_first_kernel, data_count, factor),
+        out_shape=(shape, shape, flag_shape()),
+        in_specs=[smem()] * 3 + [vmem()] * 5,
+        out_specs=[vmem()] * 3,
+        compiler_params=params(q_all, pack),
+        cost_estimate=cost(6e9, 16e6, 4e6),
+        name="prompt_grad_first",
+    )(meta, starts, table, q_all, ids_all, pack, kv, flag)
+
+
+def prompt_grad_last(meta, starts, table, q_all, ids_all, pack, kv, terms, weights, factor, data_count):
     block, width = kv.shape[0], weights.shape[0]
     dim = kv.shape[1] // 4
     return pl.pallas_call(
-        functools.partial(prompt_grad_kernel, data_count, factor),
+        functools.partial(prompt_grad_last_kernel, data_count, factor),
         out_shape=(
             jax.ShapeDtypeStruct((block, width // 2), F32),
             jax.ShapeDtypeStruct((block, width // 2), BF),
@@ -1124,10 +1184,10 @@
             pltpu.VMEM((block, 2 * dim), F32),
             pltpu.VMEM((block, 2 * dim), F32),
         ],
-        compiler_params=params(q_all, *packs),
+        compiler_params=params(q_all, pack),
         cost_estimate=cost(6e9, 16e6, 4e6),
-        name="prompt_grad",
-    )(meta, starts, table, q_all, ids_all, *packs, kv, flag, weights)
+        name="prompt_grad_last",
+    )(meta, starts, table, q_all, ids_all, pack, kv, *terms, weights)
 
 
 def token_grad_kernel(
@@ -1469,6 +1529,18 @@
                 factor,
                 data_count,
             )
+            *tied["terms"], tied["flag"] = prompt_grad_first(
+                meta,
+                starts,
+                prompt_map,
+                tied["q"],
+                ids_all,
+                held,
+                prompt_kv,
+                tied["flag"],
+                factor,
+                data_count,
+            )
         return held
 
     out_half = lax.dynamic_slice_in_dim(out, parity * half, half, 0)
@@ -1476,11 +1548,19 @@
     packs = gather_rows(pack, row_count, head_count, tie_query_grads)
     q_all = tied["q"]
     dq = tied["dq"]
-    packs, dq_other, out_half, flag = lax.optimization_barrier(
-        (packs, tied["dq_other"], out_half, tied["flag"])
-    )
-    keep, send = prompt_grad(
-        meta, starts, prompt_map, q_all, ids_all, packs, prompt_kv, flag, w_kv, factor, data_count
+    packs, dq_other, out_half = lax.optimization_barrier((packs, tied["dq_other"], out_half))
+    keep, send = prompt_grad_last(
+        meta,
+        starts,
+        prompt_map,
+        q_all,
+        ids_all,
+        packs[1],
+        prompt_kv,
+        tied["terms"],
+        w_kv,
+        factor,
+        data_count,
     )
 
     pair = keep + swap_head(send, 1, head_count).astype(F32)

time: 210 us -> 212 us (level); the launches traced: 209 us -> 209 us
  starting transfers between devices: 43.1 us -> 36.6 us
  waiting for transfers between devices: 69.5 us -> 73.7 us
    ppermute x20, starting transfers between devices: 22.4 us -> 14.7 us  [swap_head(): lax.ppermute(value, 'head', [(i, i ^ mask) for i in range(head_count)])]
    ppermute x9, waiting for transfers between devices: 44.2 us -> 51.1 us  [gather_stage(): return lax.ppermute(held, BOTH, pairs)]
    ppermute x20, waiting for transfers between devices: 22.9 us -> 18.9 us  [swap_head(): lax.ppermute(value, 'head', [(i, i ^ mask) for i in range(head_count)])]
    ppermute x6, starting transfers between devices: 10.6 us -> 14.3 us  [moved(): return lax.ppermute(value, BOTH, [(i, i ^ mask) for i in range(count)])]
    ppermute x9, starting transfers between devices: 10.1 us -> 7.59 us  [gather_stage(): return lax.ppermute(held, BOTH, pairs)]
    pallas_call x1 -> x2, Pallas kernels: 2.99 us -> 4.62 us  [the longest x1 3.01 us: prompt_grad_last(): pl.pallas_call(functools.partial(prompt_grad_last_kernel, data_count, fac...]
  transfers between devices with their start and end apart: 35 -> 35, of which waited for: 19 -> 19; matrix products, arithmetic and copies ran while one was open for 8% -> 8% of each run, Pallas kernels for 19% -> 20%
where the time goes in v3:
time: 212 us; the launch traced here: 209 us
  waiting for transfers between devices  73.7 us (35%)
  Pallas kernels  68.5 us (32%)
  starting transfers between devices  36.6 us (17%)
  other arithmetic  14.1 us (7%)
  local copies, waits for them, and re-layouts  11.8 us (6%)
  between operations  2.12 us (1%)
    ppermute x9, waiting for transfers between devices, gather_stage(): return lax.ppermute(held, BOTH, pairs)  51.1 us
    ppermute x20, waiting for transfers between devices, swap_head(): lax.ppermute(value, 'head', [(i, i ^ mask) for i in range(head_count)])  18.9 us
    pallas_call x1, Pallas kernels, prompt_forward(): pl.pallas_call(functools.partial(prompt_forward_kernel, block, factor), o...  14.9 us
    ppermute x20, starting transfers between devices, swap_head(): lax.ppermute(value, 'head', [(i, i ^ mask) for i in range(head_count)])  14.7 us
    ppermute x6, starting transfers between devices, moved(): return lax.ppermute(value, BOTH, [(i, i ^ mask) for i in range(count)])  14.3 us
    pallas_call x1, Pallas kernels, prompt_query_grad(): pl.pallas_call(functools.partial(prompt_query_grad_kernel, block, factor)...  12 us
    pallas_call x1, Pallas kernels, feed(): pl.pallas_call(feed_kernel, out_shape=(jax.ShapeDtypeStruct((size, width)...  7.7 us
    pallas_call x1, Pallas kernels, token_grad(): pl.pallas_call(functools.partial(token_grad_kernel, data_count, factor),...  7.7 us
  transfers between devices with their start and end apart: 35, of which 19 were waited for; matrix products, arithmetic and copies ran while one was open for 8% of the time, Pallas kernels for 20%

profile of v3, /device:TPU:0, one launch (start us, length us, event | category | flops | bytes accessed | tf_op | source)
XLA Modules:
  0.0 208.6 jit_solution(16766131343328407296)
XLA Ops:
  3.6 4.1 %collective-permute-start.1 = (bf16[1,512,256]{2,1,0:T(8,128)(2,1)S(1)}, bf16[1,512,256]{2,1,0:T(8,128)(2,1)S(1)}, u32[]{:S(2)}, u32[]{:S(2)}) collective-permute-start(bf16[1,512,256]{2,1,0:T(8,128)(2,1)S(1)} %fusion.2), channel_id=1, source_target_pairs={{0,16},{1,9},{2,18},{3,11},{4,20},{5,13},{6,22},{7,15},{8,24},{9,1... | collective-permute-start | bytes 786440 | tf_op jit(solution)/shard_map/ppermute | solution.py:83
  11.5 8.8 %collective-permute-done.1 = bf16[1,512,256]{2,1,0:T(8,128)(2,1)S(1)} collective-permute-done((bf16[1,512,256]{2,1,0:T(8,128)(2,1)S(1)}, bf16[1,512,256]{2,1,0:T(8,128)(2,1)S(1)}, u32[]{:S(2)}, u32[]{:S(2)}) %collective-permute-start.1) | collective-permute-done | bytes 262176 | tf_op jit(solution)/shard_map/ppermute | solution.py:83
  22.3 1.8 fusion.1.w_own
  24.1 2.2 %dynamic-slice_bitcast_fusion = (bf16[512,512]{1,0:T(8,128)(2,1)}, bf16[512,512]{1,0:T(8,128)(2,1)}) fusion(bf16[2,512,512]{2,1,0:T(8,128)(2,1)} %param.17, s32[]{:T(128)S(6)} %select_n.76, bf16[2,512,512]{2,1,0:T(8,128)(2,1)S(1)} %copy-done.36), kind=kLoop, calls=%fused_computation.20 | loop fusion | bytes 2097156 | tf_op jit(solution)/shard_map/jit(dynamic_index_in_dim)/squeeze | solution.py:1414
  26.4 10.6 %collective-permute-done.2 = bf16[2,272,512]{2,1,0:T(8,128)(2,1)} collective-permute-done((bf16[2,272,512]{2,1,0:T(8,128)(2,1)S(1)}, bf16[2,272,512]{2,1,0:T(8,128)(2,1)}, u32[]{:S(2)}, u32[]{:S(2)}) %collective-permute-start.2) | collective-permute-done | bytes 557088 | tf_op jit(solution)/shard_map/ppermute | solution.py:83
  38.2 2.1 %collective-permute-start.6 = (bf16[656,512]{1,0:T(8,128)(2,1)}, bf16[656,512]{1,0:T(8,128)(2,1)}, u32[]{:S(2)}, u32[]{:S(2)}) collective-permute-start(bf16[656,512]{1,0:T(8,128)(2,1)} %fusion.1.w_own), channel_id=1, source_target_pairs={{0,2},{1,3},{2,0},{3,1},{4,6},{5,7},{6,4},{7,5},{8,10},{9,11},{10,... | collective-permute-start | bytes 2015240 | tf_op jit(solution)/shard_map/ppermute | solution.py:122
  41.9 13.3 %collective-permute-done.5 = bf16[2,512,256]{2,1,0:T(8,128)(2,1)S(1)} collective-permute-done((bf16[2,512,256]{2,1,0:T(8,128)(2,1)S(1)}, bf16[2,512,256]{2,1,0:T(8,128)(2,1)S(1)}, u32[]{:S(2)}, u32[]{:S(2)}) %collective-permute-start.5) | collective-permute-done | bytes 524320 | tf_op jit(solution)/shard_map/ppermute | solution.py:83
  56.3 2.6 %collective-permute-done.4.mine_high.c = bf16[4,272,512]{2,1,0:T(8,128)(2,1)S(1)} collective-permute-done((bf16[4,272,512]{2,1,0:T(8,128)(2,1)S(1)}, bf16[4,272,512]{2,1,0:T(8,128)(2,1)S(1)}, u32[]{:S(2)}, u32[]{:S(2)}) %collective-permute-start.4) | collective-permute-done | bytes 1114144 | tf_op jit(solution)/shard_map/ppermute | solution.py:83
  63.3 7.6 %token_forward.1 = (bf16[2,512,256]{2,1,0:T(8,128)(2,1)}, bf16[512,512]{1,0:T(8,128)(2,1)}, bf16[512,256]{1,0:T(8,128)(2,1)}, bf16[512,512]{1,0:T(8,128)(2,1)}, ...) custom-call(s32[3]{0:T(128)} %pad_add_fusion.meta, ...), custom_call_target="tpu_custom_call" | custom-call | flops 8000000000 | bytes 8000000 | tf_op jit(solution)/shard_map/token_forward/pallas_call | solution.py:349
  71.0 3.5 %collective-permute-done.9.mine_high = bf16[4,512,256]{2,1,0:T(8,128)(2,1)} collective-permute-done((bf16[4,512,256]{2,1,0:T(8,128)(2,1)}, bf16[4,512,256]{2,1,0:T(8,128)(2,1)}, u32[]{:S(2)}, u32[]{:S(2)}) %collective-permute-start.9) | collective-permute-done | bytes 1048608 | tf_op jit(solution)/shard_map/ppermute | solution.py:83
  78.4 14.9 %prompt_forward.1 = (f32[512,256]{1,0:T(8,128)}, f32[2,512]{1,0:T(2,128)}, bf16[528,256]{1,0:T(8,128)(2,1)}) custom-call(s32[3]{0:T(128)} %pad_add_fusion.meta, s32[2,17]{1,0:T(2,128)} %copy.41.local, s32[2,16]{1,0:T(2,128)} %table.7, bf16[2,512,256]{2,1,0:T(8,128)(2,1)} %get-tuple-element.107.q_ref, f32[2,1,512]{2,1,0:T(1,128)} %reshape.65.ids_ref.own_ids, ...), custom_call_target="tpu_custom_call" | custom-call | flops 4000000000 | bytes 8000000 | tf_op jit(solution)/shard_map/prompt_forward/pallas_call | solution.py:580
  93.3 2.7 %collective-permute-start.14 = (bf16[528,256]{1,0:T(8,128)(2,1)}, bf16[528,256]{1,0:T(8,128)(2,1)S(1)}, u32[]{:S(2)}, u32[]{:S(2)}) collective-permute-start(bf16[528,256]{1,0:T(8,128)(2,1)} %get-tuple-element.121), channel_id=1, source_target_pairs={{0,2},{1,3},{2,0},{3,1},{4,6},{5,7},{6,4},{7,5},{8,10},{9,11},{10,... | collective-permute-start | bytes 811016 | tf_op jit(solution)/shard_map/ppermute | solution.py:122
  96.0 1.9 convolution_convert_fusion.kv_ref
  98.0 5.0 %collective-permute-done.14.other_ref = bf16[528,256]{1,0:T(8,128)(2,1)S(1)} collective-permute-done((bf16[528,256]{1,0:T(8,128)(2,1)}, bf16[528,256]{1,0:T(8,128)(2,1)S(1)}, u32[]{:S(2)}, u32[]{:S(2)}) %collective-permute-start.14) | collective-permute-done | bytes 270368 | tf_op jit(solution)/shard_map/ppermute | solution.py:122
  105.2 7.7 %feed.1 = (bf16[512,512]{1,0:T(8,128)(2,1)S(1)}, f32[512,512]{1,0:T(8,128)S(1)}, bf16[544,256]{1,0:T(8,128)(2,1)S(1)}, f32[2,512]{1,0:T(2,128)S(1)}) custom-call(s32[3]{0:T(128)S(1)} %copy-done.19, bf16[512,256]{1,0:T(8,128)(2,1)S(1)} %get-tuple-element.124.mine, bf16[512,256]{1,0:T(8,128)(2,1)S(1)} %collective-permute-done.15.theirs, ...), custom_call_target="tpu_custom_call" | custom-call | flops 3000000000 | bytes 8000000 | tf_op jit(solution)/shard_map/feed/pallas_call | solution.py:757
  114.0 1.8 collective-permute-start.17
  116.2 3.5 %project_query.1 = (bf16[2,4,2,256,256]{4,3,2,1,0:T(8,128)(2,1)S(1)}, f32[8,128]{1,0:T(8,128)S(1)}) custom-call(bf16[4,272,512]{2,1,0:T(8,128)(2,1)S(1)} %copy-done.2, bf16[4,272,512]{2,1,0:T(8,128)(2,1)S(1)} %copy-done.8, bf16[4,272,512]{2,1,0:T(8,128)(2,1)S(1)} %copy-done.6, bf16[4,272,512]{2,1,0:T(8,128)(2,1)} %collective-permute-done.8.theirs_high.d, ...), custom_call_target="tpu_custom_call" | custom-call | flops 1073741824 | bytes 4194304 | tf_op jit(solution)/shard_map/project_query/pallas_call | solution.py:179
  120.6 3.0 %collective-permute-done.17.pack_other = bf16[544,256]{1,0:T(8,128)(2,1)S(1)} collective-permute-done((bf16[544,256]{1,0:T(8,128)(2,1)S(1)}, bf16[544,256]{1,0:T(8,128)(2,1)S(1)}, u32[]{:S(2)}, u32[]{:S(2)}) %collective-permute-start.17) | collective-permute-done | bytes 278560 | tf_op jit(solution)/shard_map/ppermute | solution.py:122
  123.6 12.0 %prompt_query_grad.1 = (f32[2,512,128]{2,1,0:T(8,128)S(1)}, bf16[512,256]{1,0:T(8,128)(2,1)S(1)}) custom-call(s32[3]{0:T(128)S(1)} %copy-done.19, s32[2,17]{1,0:T(2,128)S(1)} %copy-done.21, s32[2,16]{1,0:T(2,128)S(1)} %copy-done.30, bf16[2,512,256]{2,1,0:T(8,128)(2,1)S(1)} %copy-done.34, f32[2,1,512]{2,1,0:T(1,128)S(1)} %copy-done.18, ...), custom_call_target="tpu_custom_call" | custom-call | flops 6000000000 | bytes 16000000 | tf_op jit(solution)/shard_map/prompt_query_grad/pallas_call | solution.py:969
  135.6 2.9 %collective-permute-done.18 = bf16[2,544,256]{2,1,0:T(8,128)(2,1)S(1)} collective-permute-done((bf16[2,544,256]{2,1,0:T(8,128)(2,1)S(1)}, bf16[2,544,256]{2,1,0:T(8,128)(2,1)S(1)}, u32[]{:S(2)}, u32[]{:S(2)}) %collective-permute-start.18) | collective-permute-done | bytes 557088 | tf_op jit(solution)/shard_map/ppermute | solution.py:83
  138.6 2.2 %collective-permute-start.20 = (bf16[512,256]{1,0:T(8,128)(2,1)S(1)}, bf16[512,256]{1,0:T(8,128)(2,1)S(1)}, u32[]{:S(2)}, u32[]{:S(2)}) collective-permute-start(bf16[512,256]{1,0:T(8,128)(2,1)S(1)} %get-tuple-element.143), channel_id=1, source_target_pairs={{0,2},{1,3},{2,0},{3,1},{4,6},{5,7},{6,4},{7,5},{8,10},{9,11},{10,... | collective-permute-start | bytes 786440 | tf_op jit(solution)/shard_map/ppermute | solution.py:122
  140.9 4.5 %token_query_grad.1 = (f32[512,256]{1,0:T(8,128)S(1)}, f32[8,128]{1,0:T(8,128)S(1)}) custom-call(s32[3]{0:T(128)S(1)} %copy-done.19, s32[17]{0:T(128)S(1)} %copy-done.22, bf16[2,512,256]{2,1,0:T(8,128)(2,1)S(1)} %copy-done.34, f32[2,1,512]{2,1,0:T(1,128)S(1)} %copy-done.18, f32[2,512]{1,0:T(2,128)S(1)} %get-tuple-element.126.lse_ref.lse_in, ...), custom_call_target="tpu_custom_call" | custom-call | flops 6000000000 | bytes 16000000 | tf_op jit(solution)/shard_map/token_query_grad/pallas_call | solution.py:847
  146.2 1.6 prompt_grad_first.1
  147.8 8.6 %collective-permute-done.19.pack_ref.high_ref = bf16[4,544,256]{2,1,0:T(8,128)(2,1)S(1)} collective-permute-done((bf16[4,544,256]{2,1,0:T(8,128)(2,1)S(1)}, bf16[4,544,256]{2,1,0:T(8,128)(2,1)S(1)}, u32[]{:S(2)}, u32[]{:S(2)}) %collective-permute-start.19) | collective-permute-done | bytes 1114144 | tf_op jit(solution)/shard_map/ppermute | solution.py:83
  156.4 3.0 %prompt_grad_last.1 = (f32[1000,256]{1,0:T(8,128)S(1)}, bf16[1000,256]{1,0:T(8,128)(2,1)S(1)}) custom-call(s32[3]{0:T(128)S(1)} %copy-done.19, s32[17]{0:T(128)S(1)} %copy-done.22, s32[2,16]{1,0:T(2,128)S(1)} %copy-done.30, bf16[16,256,256]{2,1,0:T(8,128)(2,1)S(1)} %bitcast.42, f32[8,1,512]{2,1,0:T(1,128)S(1)} %maximum_convert_fusion.2.ids_ref, ...), custom_call_target="tpu_custom_call" | custom-call | flops 6000000000 | bytes 16000000 | tf_op jit(solution)/shard_map/prompt_grad_last/pallas_call | solution.py:1175
  164.0 7.7 %token_grad.1 = (bf16[512,512]{1,0:T(8,128)(2,1)}, f32[8,128]{1,0:T(8,128)}) custom-call(s32[3]{0:T(128)} %pad_add_fusion.meta, s32[17]{0:T(128)} %convert_reduce_fusion.starts, bf16[16,256,256]{2,1,0:T(8,128)(2,1)} %bitcast.43, f32[8,1,512]{2,1,0:T(1,128)} %copy-done.16, bf16[4,544,256]{2,1,0:T(8,128)(2,1)} %copy-done.9, bf16[4,544,256]{2,1,0:T(8,128)(2,1)} %copy-done.24, ...), custom_call_target="tpu_custom_call" | custom-call | flops 4000000000 | bytes 16000000 | tf_op jit(solution)/shard_map/token_grad/pallas_call | solution.py:1243
  172.8 4.8 %collective-permute-done.23.b_ref = bf16[1000,256]{1,0:T(8,128)(2,1)S(1)} collective-permute-done((bf16[1000,256]{1,0:T(8,128)(2,1)S(1)}, bf16[1000,256]{1,0:T(8,128)(2,1)S(1)}, u32[]{:S(2)}, u32[]{:S(2)}) %collective-permute-start.23) | collective-permute-done | bytes 512032 | tf_op jit(solution)/shard_map/ppermute | solution.py:122
  179.0 2.2 %collective-permute-start.26 = (f32[8,128]{1,0:T(8,128)S(1)}, f32[8,128]{1,0:T(8,128)S(1)}, u32[]{:S(2)}, u32[]{:S(2)}) collective-permute-start(f32[8,128]{1,0:T(8,128)S(1)} %get-tuple-element.163), channel_id=1, source_target_pairs={{0,5},{1,4},{2,7},{3,6},{4,1},{5,0},{6,3},{7,2},{8,13},{9,12},{10,... | collective-permute-start | bytes 12296 | tf_op jit(solution)/shard_map/ppermute | solution.py:101
  182.6 2.3 %collective-permute-done.25 = f32[8,128]{1,0:T(8,128)S(1)} collective-permute-done((f32[8,128]{1,0:T(8,128)S(1)}, f32[8,128]{1,0:T(8,128)S(1)}, u32[]{:S(2)}, u32[]{:S(2)}) %collective-permute-start.25) | collective-permute-done | bytes 4128 | tf_op jit(solution)/shard_map/ppermute | solution.py:101
  185.1 5.1 %collective-permute-start.30 = (f32[8,128]{1,0:T(8,128)S(1)}, f32[8,128]{1,0:T(8,128)S(1)}, u32[]{:S(2)}, u32[]{:S(2)}) collective-permute-start(f32[8,128]{1,0:T(8,128)S(1)} %add_add_fusion.1), channel_id=1, source_target_pairs={{0,24},{1,25},{2,26},{3,27},{4,28},{5,29},{6,30},{7,31},{8,16},{9,... | collective-permute-start | bytes 12296 | tf_op jit(solution)/shard_map/ppermute | solution.py:101
  190.2 6.8 %collective-permute-start.29 = (f32[8,128]{1,0:T(8,128)S(1)}, f32[8,128]{1,0:T(8,128)S(1)}, u32[]{:S(2)}, u32[]{:S(2)}) collective-permute-start(f32[8,128]{1,0:T(8,128)S(1)} %add_add_fusion.1), channel_id=1, source_target_pairs={{0,16},{1,17},{2,18},{3,19},{4,20},{5,21},{6,22},{7,23},{8,24},{9,... | collective-permute-start | bytes 12296 | tf_op jit(solution)/shard_map/ppermute | solution.py:101
  200.6 4.7 %optimizer.1 = (f32[1000,512]{1,0:T(8,128)}, f32[1000,512]{1,0:T(8,128)}, f32[1000,512]{1,0:T(8,128)}, f32[1000,512]{1,0:T(8,128)}, f32[8,128]{1,0:T(8,128)S(1)}) custom-call(s32[3]{0:T(128)S(1)} %copy-done.20, f32[2]{0:T(128)S(1)} %pad_maximum_fusion.9.biases, bf16[1000,256]{1,0:T(8,128)(2,1)S(1)} %get-tuple-element.170.mine, ...), custom_call_target="tpu_custom_call" | custom-call | flops 10240000 | bytes 16384000 | tf_op jit(solution)/shard_map/optimizer/pallas_call | solution.py:1334
  (183 shorter events, 40.8 us)
Async XLA Ops:
  3.6 16.7 %collective-permute-start.1 = (bf16[1,512,256]{2,1,0:T(8,128)(2,1)S(1)}, bf16[1,512,256]{2,1,0:T(8,128)(2,1)S(1)}, u32[]{:S(2)}, u32[]{:S(2)}) collective-permute-start(bf16[1,512,256]{2,1,0:T(8,128)(2,1)S(1)} %fusion.2), channel_id=1, source_target_pairs={{0,16},{1,9},{2,18},{3,11},{4,20},{5,13},{6,22},{7,15},{8,24},{9,1... | collective-permute-start | bytes 786440 | tf_op jit(solution)/shard_map/ppermute | solution.py:83
  7.7 12.6 %collective-permute-start = (bf16[1,272,512]{2,1,0:T(8,128)(2,1)S(1)}, bf16[1,272,512]{2,1,0:T(8,128)(2,1)S(1)}, u32[]{:S(2)}, u32[]{:S(2)}) collective-permute-start(bf16[1,272,512]{2,1,0:T(8,128)(2,1)S(1)} %maximum_bitcast_fusion), channel_id=1, source_target_pairs={{0,4},{1,17},{2,6},{3,19},{4,0},{5,21},{6,2},{7,23},{8,12},{9,25},... | collective-permute-start | bytes 835592 | tf_op jit(solution)/shard_map/ppermute | solution.py:83
  9.2 17.2 %collective-permute-start.3 = (bf16[3,512,128]{2,1,0:T(8,128)(2,1)}, bf16[3,512,128]{2,1,0:T(8,128)(2,1)}, u32[]{:S(2)}, u32[]{:S(2)}) collective-permute-start(bf16[3,512,128]{2,1,0:T(8,128)(2,1)} %in_own.1), channel_id=1, source_target_pairs={{0,2},{1,3},{2,0},{3,1},{4,6},{5,7},{6,4},{7,5},{8,10},{9,11},{10,... | collective-permute-start | bytes 1179656 | tf_op jit(solution)/shard_map/ppermute | solution.py:122
  20.4 16.6 %collective-permute-start.2 = (bf16[2,272,512]{2,1,0:T(8,128)(2,1)S(1)}, bf16[2,272,512]{2,1,0:T(8,128)(2,1)}, u32[]{:S(2)}, u32[]{:S(2)}) collective-permute-start(bf16[2,272,512]{2,1,0:T(8,128)(2,1)S(1)} %pad_maximum_fusion.3), channel_id=1, source_target_pairs={{0,16},{1,9},{2,18},{3,11},{4,20},{5,13},{6,22},{7,15},{8,24},{9,1... | collective-permute-start | bytes 1671176 | tf_op jit(solution)/shard_map/ppermute | solution.py:83
  38.1 20.7 %collective-permute-start.4 = (bf16[4,272,512]{2,1,0:T(8,128)(2,1)S(1)}, bf16[4,272,512]{2,1,0:T(8,128)(2,1)S(1)}, u32[]{:S(2)}, u32[]{:S(2)}) collective-permute-start(bf16[4,272,512]{2,1,0:T(8,128)(2,1)S(1)} %pad_maximum_fusion.mine_low.a), channel_id=1, source_target_pairs={{0,8},{1,5},{2,10},{3,7},{4,12},{5,1},{6,14},{7,3},{8,0},{9,13},{1... | collective-permute-start | bytes 3342344 | tf_op jit(solution)/shard_map/ppermute | solution.py:83
  38.2 18.1 %collective-permute-start.6 = (bf16[656,512]{1,0:T(8,128)(2,1)}, bf16[656,512]{1,0:T(8,128)(2,1)}, u32[]{:S(2)}, u32[]{:S(2)}) collective-permute-start(bf16[656,512]{1,0:T(8,128)(2,1)} %fusion.1.w_own), channel_id=1, source_target_pairs={{0,2},{1,3},{2,0},{3,1},{4,6},{5,7},{6,4},{7,5},{8,10},{9,11},{10,... | collective-permute-start | bytes 2015240 | tf_op jit(solution)/shard_map/ppermute | solution.py:122
  40.4 14.9 %collective-permute-start.5 = (bf16[2,512,256]{2,1,0:T(8,128)(2,1)S(1)}, bf16[2,512,256]{2,1,0:T(8,128)(2,1)S(1)}, u32[]{:S(2)}, u32[]{:S(2)}) collective-permute-start(bf16[2,512,256]{2,1,0:T(8,128)(2,1)S(1)} %pad_maximum_fusion.5), channel_id=1, source_target_pairs={{0,4},{1,17},{2,6},{3,19},{4,0},{5,21},{6,2},{7,23},{8,12},{9,25},... | collective-permute-start | bytes 1572872 | tf_op jit(solution)/shard_map/ppermute | solution.py:83
  41.9 19.7 %collective-permute-start.7 = (bf16[4,272,512]{2,1,0:T(8,128)(2,1)S(1)}, bf16[4,272,512]{2,1,0:T(8,128)(2,1)S(1)}, u32[]{:S(2)}, u32[]{:S(2)}) collective-permute-start(bf16[4,272,512]{2,1,0:T(8,128)(2,1)S(1)} %pad_maximum_fusion.mine_low.a), channel_id=1, source_target_pairs={{0,1},{1,0},{2,3},{3,2},{4,5},{5,4},{6,7},{7,6},{8,9},{9,8},{10,11... | collective-permute-start | bytes 3342344 | tf_op jit(solution)/shard_map/ppermute | solution.py:122
  58.9 4.4 %collective-permute-start.8 = (bf16[4,272,512]{2,1,0:T(8,128)(2,1)S(1)}, bf16[4,272,512]{2,1,0:T(8,128)(2,1)}, u32[]{:S(2)}, u32[]{:S(2)}) collective-permute-start(bf16[4,272,512]{2,1,0:T(8,128)(2,1)S(1)} %collective-permute-done.4.mine_high.c), channel_id=1, source_target_pairs={{0,1},{1,0},{2,3},{3,2},{4,5},{5,4},{6,7},{7,6},{8,9},{9,8},{10,11... | collective-permute-start | bytes 3342344 | tf_op jit(solution)/shard_map/ppermute | solution.py:122
  58.9 12.1 %collective-permute-start.10 = (bf16[4,512,256]{2,1,0:T(8,128)(2,1)}, bf16[4,512,256]{2,1,0:T(8,128)(2,1)}, u32[]{:S(2)}, u32[]{:S(2)}) collective-permute-start(bf16[4,512,256]{2,1,0:T(8,128)(2,1)} %pad_maximum_fusion.2.mine_low), channel_id=1, source_target_pairs={{0,1},{1,0},{2,3},{3,2},{4,5},{5,4},{6,7},{7,6},{8,9},{9,8},{10,11... | collective-permute-start | bytes 3145736 | tf_op jit(solution)/shard_map/ppermute | solution.py:122
  59.4 15.1 %collective-permute-start.9 = (bf16[4,512,256]{2,1,0:T(8,128)(2,1)}, bf16[4,512,256]{2,1,0:T(8,128)(2,1)}, u32[]{:S(2)}, u32[]{:S(2)}) collective-permute-start(bf16[4,512,256]{2,1,0:T(8,128)(2,1)} %pad_maximum_fusion.2.mine_low), channel_id=1, source_target_pairs={{0,8},{1,5},{2,10},{3,7},{4,12},{5,1},{6,14},{7,3},{8,0},{9,13},{1... | collective-permute-start | bytes 3145736 | tf_op jit(solution)/shard_map/ppermute | solution.py:83
  59.7 11.3 %collective-permute-start.11 = (bf16[656,512]{1,0:T(8,128)(2,1)}, bf16[656,512]{1,0:T(8,128)(2,1)}, u32[]{:S(2)}, u32[]{:S(2)}) collective-permute-start(bf16[656,512]{1,0:T(8,128)(2,1)} %fusion.1.w_own), channel_id=1, source_target_pairs={{0,1},{1,0},{2,3},{3,2},{4,5},{5,4},{6,7},{7,6},{8,9},{9,8},{10,11... | collective-permute-start | bytes 2015240 | tf_op jit(solution)/shard_map/ppermute | solution.py:122
  61.6 9.5 %collective-permute-start.12 = (bf16[656,512]{1,0:T(8,128)(2,1)}, bf16[656,512]{1,0:T(8,128)(2,1)}, u32[]{:S(2)}, u32[]{:S(2)}) collective-permute-start(bf16[656,512]{1,0:T(8,128)(2,1)} %collective-permute-done.6.w_along), channel_id=1, source_target_pairs={{0,1},{1,0},{2,3},{3,2},{4,5},{5,4},{6,7},{7,6},{8,9},{9,8},{10,11... | collective-permute-start | bytes 2015240 | tf_op jit(solution)/shard_map/ppermute | solution.py:122
  74.5 2.9 %collective-permute-start.13 = (bf16[4,512,256]{2,1,0:T(8,128)(2,1)}, bf16[4,512,256]{2,1,0:T(8,128)(2,1)S(1)}, u32[]{:S(2)}, u32[]{:S(2)}) collective-permute-start(bf16[4,512,256]{2,1,0:T(8,128)(2,1)} %collective-permute-done.9.mine_high), channel_id=1, source_target_pairs={{0,1},{1,0},{2,3},{3,2},{4,5},{5,4},{6,7},{7,6},{8,9},{9,8},{10,11... | collective-permute-start | bytes 3145736 | tf_op jit(solution)/shard_map/ppermute | solution.py:122
  93.3 9.7 %collective-permute-start.14 = (bf16[528,256]{1,0:T(8,128)(2,1)}, bf16[528,256]{1,0:T(8,128)(2,1)S(1)}, u32[]{:S(2)}, u32[]{:S(2)}) collective-permute-start(bf16[528,256]{1,0:T(8,128)(2,1)} %get-tuple-element.121), channel_id=1, source_target_pairs={{0,2},{1,3},{2,0},{3,1},{4,6},{5,7},{6,4},{7,5},{8,10},{9,11},{10,... | collective-permute-start | bytes 811016 | tf_op jit(solution)/shard_map/ppermute | solution.py:122
  114.0 6.5 %collective-permute-start.16 = (bf16[1,544,256]{2,1,0:T(8,128)(2,1)S(1)}, bf16[1,544,256]{2,1,0:T(8,128)(2,1)S(1)}, u32[]{:S(2)}, u32[]{:S(2)}) collective-permute-start(bf16[1,544,256]{2,1,0:T(8,128)(2,1)S(1)} %bitcast.39), channel_id=1, source_target_pairs={{0,4},{1,17},{2,6},{3,19},{4,0},{5,21},{6,2},{7,23},{8,12},{9,25},... | collective-permute-start | bytes 835592 | tf_op jit(solution)/shard_map/ppermute | solution.py:83
  114.0 9.6 %collective-permute-start.17 = (bf16[544,256]{1,0:T(8,128)(2,1)S(1)}, bf16[544,256]{1,0:T(8,128)(2,1)S(1)}, u32[]{:S(2)}, u32[]{:S(2)}) collective-permute-start(bf16[544,256]{1,0:T(8,128)(2,1)S(1)} %get-tuple-element.131.pack_own.do_ref), channel_id=1, source_target_pairs={{0,2},{1,3},{2,0},{3,1},{4,6},{5,7},{6,4},{7,5},{8,10},{9,11},{10,... | collective-permute-start | bytes 835592 | tf_op jit(solution)/shard_map/ppermute | solution.py:122
  115.9 31.9 %collective-permute-start.21 = (bf16[256,512]{1,0:T(8,128)(2,1)S(1)}, bf16[256,512]{1,0:T(8,128)(2,1)S(1)}, u32[]{:S(2)}, u32[]{:S(2)}) collective-permute-start(bf16[256,512]{1,0:T(8,128)(2,1)S(1)} %constant_dynamic-slice_fusion.1), channel_id=1, source_target_pairs={{0,2},{1,3},{2,0},{3,1},{4,6},{5,7},{6,4},{7,5},{8,10},{9,11},{10,... | collective-permute-start | bytes 786440 | tf_op jit(solution)/shard_map/ppermute | solution.py:122
  123.6 15.0 %collective-permute-start.18 = (bf16[2,544,256]{2,1,0:T(8,128)(2,1)S(1)}, bf16[2,544,256]{2,1,0:T(8,128)(2,1)S(1)}, u32[]{:S(2)}, u32[]{:S(2)}) collective-permute-start(bf16[2,544,256]{2,1,0:T(8,128)(2,1)S(1)} %pad_maximum_fusion.4), channel_id=1, source_target_pairs={{0,16},{1,9},{2,18},{3,11},{4,20},{5,13},{6,22},{7,15},{8,24},{9,1... | collective-permute-start | bytes 1671176 | tf_op jit(solution)/shard_map/ppermute | solution.py:83
  138.6 9.2 %collective-permute-start.20 = (bf16[512,256]{1,0:T(8,128)(2,1)S(1)}, bf16[512,256]{1,0:T(8,128)(2,1)S(1)}, u32[]{:S(2)}, u32[]{:S(2)}) collective-permute-start(bf16[512,256]{1,0:T(8,128)(2,1)S(1)} %get-tuple-element.143), channel_id=1, source_target_pairs={{0,2},{1,3},{2,0},{3,1},{4,6},{5,7},{6,4},{7,5},{8,10},{9,11},{10,... | collective-permute-start | bytes 786440 | tf_op jit(solution)/shard_map/ppermute | solution.py:122
  140.9 15.5 %collective-permute-start.19 = (bf16[4,544,256]{2,1,0:T(8,128)(2,1)S(1)}, bf16[4,544,256]{2,1,0:T(8,128)(2,1)S(1)}, u32[]{:S(2)}, u32[]{:S(2)}) collective-permute-start(bf16[4,544,256]{2,1,0:T(8,128)(2,1)S(1)} %pad_maximum_fusion.1.pack_ref.low_ref), channel_id=1, source_target_pairs={{0,8},{1,5},{2,10},{3,7},{4,12},{5,1},{6,14},{7,3},{8,0},{9,13},{1... | collective-permute-start | bytes 3342344 | tf_op jit(solution)/shard_map/ppermute | solution.py:83
  160.4 11.4 %collective-permute-start.31 = (bf16[256,512]{1,0:T(8,128)(2,1)S(1)}, bf16[256,512]{1,0:T(8,128)(2,1)}, u32[]{:S(2)}, u32[]{:S(2)}) collective-permute-start(bf16[256,512]{1,0:T(8,128)(2,1)S(1)} %collective-permute-done.21), channel_id=1, source_target_pairs={{0,1},{1,0},{2,3},{3,2},{4,5},{5,4},{6,7},{7,6},{8,9},{9,8},{10,11... | collective-permute-start | bytes 786440 | tf_op jit(solution)/shard_map/ppermute | solution.py:122
  163.9 13.8 %collective-permute-start.23 = (bf16[1000,256]{1,0:T(8,128)(2,1)S(1)}, bf16[1000,256]{1,0:T(8,128)(2,1)S(1)}, u32[]{:S(2)}, u32[]{:S(2)}) collective-permute-start(bf16[1000,256]{1,0:T(8,128)(2,1)S(1)} %reduce-precision_convert_fusion.1.a_ref), channel_id=1, source_target_pairs={{0,2},{1,3},{2,0},{3,1},{4,6},{5,7},{6,4},{7,5},{8,10},{9,11},{10,... | collective-permute-start | bytes 1536008 | tf_op jit(solution)/shard_map/ppermute | solution.py:122
  171.7 13.1 %collective-permute-start.27 = (bf16[512,512]{1,0:T(8,128)(2,1)}, bf16[512,512]{1,0:T(8,128)(2,1)S(1)}, u32[]{:S(2)}, u32[]{:S(2)}) collective-permute-start(bf16[512,512]{1,0:T(8,128)(2,1)} %get-tuple-element.165), channel_id=1, source_target_pairs={{0,1},{1,0},{2,3},{3,2},{4,5},{5,4},{6,7},{7,6},{8,9},{9,8},{10,11... | collective-permute-start | bytes 1572872 | tf_op jit(solution)/shard_map/ppermute | solution.py:122
  179.0 3.6 %collective-permute-start.26 = (f32[8,128]{1,0:T(8,128)S(1)}, f32[8,128]{1,0:T(8,128)S(1)}, u32[]{:S(2)}, u32[]{:S(2)}) collective-permute-start(f32[8,128]{1,0:T(8,128)S(1)} %get-tuple-element.163), channel_id=1, source_target_pairs={{0,5},{1,4},{2,7},{3,6},{4,1},{5,0},{6,3},{7,2},{8,13},{9,12},{10,... | collective-permute-start | bytes 12296 | tf_op jit(solution)/shard_map/ppermute | solution.py:101
  181.2 3.6 %collective-permute-start.25 = (f32[8,128]{1,0:T(8,128)S(1)}, f32[8,128]{1,0:T(8,128)S(1)}, u32[]{:S(2)}, u32[]{:S(2)}) collective-permute-start(f32[8,128]{1,0:T(8,128)S(1)} %get-tuple-element.163), channel_id=1, source_target_pairs={{0,4},{1,5},{2,6},{3,7},{4,0},{5,1},{6,2},{7,3},{8,12},{9,13},{10,... | collective-permute-start | bytes 12296 | tf_op jit(solution)/shard_map/ppermute | solution.py:101
  181.3 3.5 %collective-permute-start.24 = (f32[8,128]{1,0:T(8,128)S(1)}, f32[8,128]{1,0:T(8,128)S(1)}, u32[]{:S(2)}, u32[]{:S(2)}) collective-permute-start(f32[8,128]{1,0:T(8,128)S(1)} %get-tuple-element.163), channel_id=1, source_target_pairs={{0,1},{1,0},{2,3},{3,2},{4,5},{5,4},{6,7},{7,6},{8,9},{9,8},{10,11... | collective-permute-start | bytes 12296 | tf_op jit(solution)/shard_map/ppermute | solution.py:101
  181.6 19.0 %collective-permute-start.33 = (bf16[1000,256]{1,0:T(8,128)(2,1)S(1)}, bf16[1000,256]{1,0:T(8,128)(2,1)S(1)}, u32[]{:S(2)}, u32[]{:S(2)}) collective-permute-start(bf16[1000,256]{1,0:T(8,128)(2,1)S(1)} %get-tuple-element.170.mine), channel_id=1, source_target_pairs={{0,1},{1,0},{2,3},{3,2},{4,5},{5,4},{6,7},{7,6},{8,9},{9,8},{10,11... | collective-permute-start | bytes 1536008 | tf_op jit(solution)/shard_map/ppermute | solution.py:122
  185.1 14.5 %collective-permute-start.30 = (f32[8,128]{1,0:T(8,128)S(1)}, f32[8,128]{1,0:T(8,128)S(1)}, u32[]{:S(2)}, u32[]{:S(2)}) collective-permute-start(f32[8,128]{1,0:T(8,128)S(1)} %add_add_fusion.1), channel_id=1, source_target_pairs={{0,24},{1,25},{2,26},{3,27},{4,28},{5,29},{6,30},{7,31},{8,16},{9,... | collective-permute-start | bytes 12296 | tf_op jit(solution)/shard_map/ppermute | solution.py:101
  190.2 9.4 %collective-permute-start.29 = (f32[8,128]{1,0:T(8,128)S(1)}, f32[8,128]{1,0:T(8,128)S(1)}, u32[]{:S(2)}, u32[]{:S(2)}) collective-permute-start(f32[8,128]{1,0:T(8,128)S(1)} %add_add_fusion.1), channel_id=1, source_target_pairs={{0,16},{1,17},{2,18},{3,19},{4,20},{5,21},{6,22},{7,23},{8,24},{9,... | collective-permute-start | bytes 12296 | tf_op jit(solution)/shard_map/ppermute | solution.py:101
  197.0 3.6 %collective-permute-start.28 = (f32[8,128]{1,0:T(8,128)S(1)}, f32[8,128]{1,0:T(8,128)S(1)}, u32[]{:S(2)}, u32[]{:S(2)}) collective-permute-start(f32[8,128]{1,0:T(8,128)S(1)} %add_add_fusion.1), channel_id=1, source_target_pairs={{0,8},{1,9},{2,10},{3,11},{4,12},{5,13},{6,14},{7,15},{8,0},{9,1},... | collective-permute-start | bytes 12296 | tf_op jit(solution)/shard_map/ppermute | solution.py:101
  197.0 8.3 %collective-permute-start.32 = (bf16[256,512]{1,0:T(8,128)(2,1)S(1)}, bf16[256,512]{1,0:T(8,128)(2,1)S(1)}, u32[]{:S(2)}, u32[]{:S(2)}) collective-permute-start(bf16[256,512]{1,0:T(8,128)(2,1)S(1)} %constant_dynamic-slice_fusion), channel_id=1, source_target_pairs={{0,2},{1,3},{2,0},{3,1},{4,6},{5,7},{6,4},{7,5},{8,10},{9,11},{10,... | collective-permute-start | bytes 786440 | tf_op jit(solution)/shard_map/ppermute | solution.py:122
  (46 other events, 410.8 us)

commit v4 on v3

--- a/solution.py
+++ b/solution.py
@@ -593,7 +593,7 @@
             pltpu.VMEM((2, size, 128), F32),
             *flags,
         ],
-        compiler_params=params(spare=VMEM_LIMIT),
+        compiler_params=params(*prompt_mine, *prompt_mine, *prompt_mine),
         cost_estimate=cost(4e9, 8e6, 2e6),
         name="prompt_forward",
     )(meta, local, table, q_own, ids_rows, *state, flag, weights, *prompt_mine, *prompt_theirs)

time: 212 us -> 207 us (0.976)
    pallas_call x1, Pallas kernels: 1.61 us -> 4.3 us  [prompt_grad_first(): pl.pallas_call(functools.partial(prompt_grad_first_kernel, data_count, fa...]
    pallas_call x1, Pallas kernels: 14.9 us -> 12.3 us  [prompt_forward(): pl.pallas_call(functools.partial(prompt_forward_kernel, block, factor), o...]
    unnamed x90 -> x94, local copies, waits for them, and re-layouts: 5.71 us -> 5.95 us
  transfers between devices with their start and end apart: 35 -> 35, of which waited for: 19 -> 18; matrix products, arithmetic and copies ran while one was open for 8% -> 7% of each run, Pallas kernels for 20% -> 21%
where the time goes in v4:
time: 207 us; the launch traced here: 206 us
  waiting for transfers between devices  72.6 us (35%)
  Pallas kernels  67.1 us (32%)
  starting transfers between devices  37.6 us (18%)
  other arithmetic  14.1 us (7%)
  local copies, waits for them, and re-layouts  11.5 us (6%)
  between operations  2.15 us (1%)
    ppermute x9, waiting for transfers between devices, gather_stage(): return lax.ppermute(held, BOTH, pairs)  50.5 us
    ppermute x20, waiting for transfers between devices, swap_head(): lax.ppermute(value, 'head', [(i, i ^ mask) for i in range(head_count)])  19.7 us
    ppermute x20, starting transfers between devices, swap_head(): lax.ppermute(value, 'head', [(i, i ^ mask) for i in range(head_count)])  15.1 us
    ppermute x6, starting transfers between devices, moved(): return lax.ppermute(value, BOTH, [(i, i ^ mask) for i in range(count)])  14.9 us
    pallas_call x1, Pallas kernels, prompt_forward(): pl.pallas_call(functools.partial(prompt_forward_kernel, block, factor), o...  12.3 us
    pallas_call x1, Pallas kernels, prompt_query_grad(): pl.pallas_call(functools.partial(prompt_query_grad_kernel, block, factor)...  11.3 us
    pallas_call x1, Pallas kernels, token_forward(): pl.pallas_call(functools.partial(token_forward_kernel, data_count, factor...  7.71 us
    pallas_call x1, Pallas kernels, feed(): pl.pallas_call(feed_kernel, out_shape=(jax.ShapeDtypeStruct((size, width)...  7.69 us
  transfers between devices with their start and end apart: 35, of which 18 were waited for; matrix products, arithmetic and copies ran while one was open for 7% of the time, Pallas kernels for 21%

profile of v4, /device:TPU:0, one launch (start us, length us, event | category | flops | bytes accessed | tf_op | source)
XLA Modules:
  0.0 205.7 jit_solution(16979352439021176262)
XLA Ops:
  3.6 4.1 %collective-permute-start.1 = (bf16[1,512,256]{2,1,0:T(8,128)(2,1)S(1)}, bf16[1,512,256]{2,1,0:T(8,128)(2,1)S(1)}, u32[]{:S(2)}, u32[]{:S(2)}) collective-permute-start(bf16[1,512,256]{2,1,0:T(8,128)(2,1)S(1)} %fusion.2), channel_id=1, source_target_pairs={{0,16},{1,9},{2,18},{3,11},{4,20},{5,13},{6,22},{7,15},{8,24},{9,1... | collective-permute-start | bytes 786440 | tf_op jit(solution)/shard_map/ppermute | solution.py:83
  11.5 8.8 %collective-permute-done.1 = bf16[1,512,256]{2,1,0:T(8,128)(2,1)S(1)} collective-permute-done((bf16[1,512,256]{2,1,0:T(8,128)(2,1)S(1)}, bf16[1,512,256]{2,1,0:T(8,128)(2,1)S(1)}, u32[]{:S(2)}, u32[]{:S(2)}) %collective-permute-start.1) | collective-permute-done | bytes 262176 | tf_op jit(solution)/shard_map/ppermute | solution.py:83
  22.3 1.8 fusion.1.w_own
  24.1 2.2 %dynamic-slice_bitcast_fusion = (bf16[512,512]{1,0:T(8,128)(2,1)}, bf16[512,512]{1,0:T(8,128)(2,1)}) fusion(bf16[2,512,512]{2,1,0:T(8,128)(2,1)} %param.17, s32[]{:T(128)S(6)} %select_n.76, bf16[2,512,512]{2,1,0:T(8,128)(2,1)S(1)} %copy-done.38), kind=kLoop, calls=%fused_computation.20 | loop fusion | bytes 2097156 | tf_op jit(solution)/shard_map/jit(dynamic_index_in_dim)/squeeze | solution.py:1414
  26.3 10.6 %collective-permute-done.2 = bf16[2,272,512]{2,1,0:T(8,128)(2,1)} collective-permute-done((bf16[2,272,512]{2,1,0:T(8,128)(2,1)S(1)}, bf16[2,272,512]{2,1,0:T(8,128)(2,1)}, u32[]{:S(2)}, u32[]{:S(2)}) %collective-permute-start.2) | collective-permute-done | bytes 557088 | tf_op jit(solution)/shard_map/ppermute | solution.py:83
  38.2 2.1 %collective-permute-start.6 = (bf16[656,512]{1,0:T(8,128)(2,1)}, bf16[656,512]{1,0:T(8,128)(2,1)}, u32[]{:S(2)}, u32[]{:S(2)}) collective-permute-start(bf16[656,512]{1,0:T(8,128)(2,1)} %fusion.1.w_own), channel_id=1, source_target_pairs={{0,2},{1,3},{2,0},{3,1},{4,6},{5,7},{6,4},{7,5},{8,10},{9,11},{10,... | collective-permute-start | bytes 2015240 | tf_op jit(solution)/shard_map/ppermute | solution.py:122
  41.9 13.3 %collective-permute-done.5 = bf16[2,512,256]{2,1,0:T(8,128)(2,1)S(1)} collective-permute-done((bf16[2,512,256]{2,1,0:T(8,128)(2,1)S(1)}, bf16[2,512,256]{2,1,0:T(8,128)(2,1)S(1)}, u32[]{:S(2)}, u32[]{:S(2)}) %collective-permute-start.5) | collective-permute-done | bytes 524320 | tf_op jit(solution)/shard_map/ppermute | solution.py:83
  56.3 2.6 %collective-permute-done.4.mine_high.c = bf16[4,272,512]{2,1,0:T(8,128)(2,1)S(1)} collective-permute-done((bf16[4,272,512]{2,1,0:T(8,128)(2,1)S(1)}, bf16[4,272,512]{2,1,0:T(8,128)(2,1)S(1)}, u32[]{:S(2)}, u32[]{:S(2)}) %collective-permute-start.4) | collective-permute-done | bytes 1114144 | tf_op jit(solution)/shard_map/ppermute | solution.py:83
  63.3 7.7 %token_forward.1 = (bf16[2,512,256]{2,1,0:T(8,128)(2,1)}, bf16[512,512]{1,0:T(8,128)(2,1)}, bf16[512,256]{1,0:T(8,128)(2,1)}, bf16[512,512]{1,0:T(8,128)(2,1)}, ...) custom-call(s32[3]{0:T(128)} %pad_add_fusion.meta, ...), custom_call_target="tpu_custom_call" | custom-call | flops 8000000000 | bytes 8000000 | tf_op jit(solution)/shard_map/token_forward/pallas_call | solution.py:349
  71.1 3.4 %collective-permute-done.9.mine_high = bf16[4,512,256]{2,1,0:T(8,128)(2,1)} collective-permute-done((bf16[4,512,256]{2,1,0:T(8,128)(2,1)}, bf16[4,512,256]{2,1,0:T(8,128)(2,1)}, u32[]{:S(2)}, u32[]{:S(2)}) %collective-permute-start.9) | collective-permute-done | bytes 1048608 | tf_op jit(solution)/shard_map/ppermute | solution.py:83
  75.8 1.8 collective-permute-done.13.theirs_high
  78.7 12.3 %prompt_forward.1 = (f32[512,256]{1,0:T(8,128)S(1)}, f32[2,512]{1,0:T(2,128)S(1)}, bf16[528,256]{1,0:T(8,128)(2,1)S(1)}) custom-call(s32[3]{0:T(128)S(1)} %copy-done.19, s32[2,17]{1,0:T(2,128)S(1)} %copy.41.local, s32[2,16]{1,0:T(2,128)S(1)} %copy-done.27, bf16[2,512,256]{2,1,0:T(8,128)(2,1)S(1)} %copy-done.31, f32[2,1,512]{2,1,0:T(1,128)S(1)} %copy-done.18, ...), custom_call_target="tpu_custom_call" | custom-call | flops 4000000000 | bytes 8000000 | tf_op jit(solution)/shard_map/prompt_forward/pallas_call | solution.py:580
  91.0 1.7 collective-permute-start.14
  93.5 6.1 %collective-permute-done.14.other_ref = bf16[528,256]{1,0:T(8,128)(2,1)S(1)} collective-permute-done((bf16[528,256]{1,0:T(8,128)(2,1)S(1)}, bf16[528,256]{1,0:T(8,128)(2,1)S(1)}, u32[]{:S(2)}, u32[]{:S(2)}) %collective-permute-start.14) | collective-permute-done | bytes 270368 | tf_op jit(solution)/shard_map/ppermute | solution.py:122
  100.3 1.5 collective-permute-done.15.theirs
  101.9 7.7 %feed.1 = (bf16[512,512]{1,0:T(8,128)(2,1)S(1)}, f32[512,512]{1,0:T(8,128)S(1)}, bf16[544,256]{1,0:T(8,128)(2,1)S(1)}, f32[2,512]{1,0:T(2,128)S(1)}) custom-call(s32[3]{0:T(128)S(1)} %copy-done.19, bf16[512,256]{1,0:T(8,128)(2,1)S(1)} %get-tuple-element.124.mine, bf16[512,256]{1,0:T(8,128)(2,1)S(1)} %collective-permute-done.15.theirs, ...), custom_call_target="tpu_custom_call" | custom-call | flops 3000000000 | bytes 8000000 | tf_op jit(solution)/shard_map/feed/pallas_call | solution.py:757
  110.6 1.8 collective-permute-start.17
  112.8 3.4 %project_query.1 = (bf16[2,4,2,256,256]{4,3,2,1,0:T(8,128)(2,1)S(1)}, f32[8,128]{1,0:T(8,128)S(1)}) custom-call(bf16[4,272,512]{2,1,0:T(8,128)(2,1)S(1)} %copy-done.2, bf16[4,272,512]{2,1,0:T(8,128)(2,1)S(1)} %copy-done.8, bf16[4,272,512]{2,1,0:T(8,128)(2,1)S(1)} %copy-done.6, bf16[4,272,512]{2,1,0:T(8,128)(2,1)} %collective-permute-done.8.theirs_high.d, ...), custom_call_target="tpu_custom_call" | custom-call | flops 1073741824 | bytes 4194304 | tf_op jit(solution)/shard_map/project_query/pallas_call | solution.py:179
  117.1 3.0 %collective-permute-done.17.pack_other = bf16[544,256]{1,0:T(8,128)(2,1)S(1)} collective-permute-done((bf16[544,256]{1,0:T(8,128)(2,1)S(1)}, bf16[544,256]{1,0:T(8,128)(2,1)S(1)}, u32[]{:S(2)}, u32[]{:S(2)}) %collective-permute-start.17) | collective-permute-done | bytes 278560 | tf_op jit(solution)/shard_map/ppermute | solution.py:122
  120.1 11.3 %prompt_query_grad.1 = (f32[2,512,128]{2,1,0:T(8,128)S(1)}, bf16[512,256]{1,0:T(8,128)(2,1)S(1)}) custom-call(s32[3]{0:T(128)S(1)} %copy-done.19, s32[2,17]{1,0:T(2,128)S(1)} %copy.41.local, s32[2,16]{1,0:T(2,128)S(1)} %copy-done.27, bf16[2,512,256]{2,1,0:T(8,128)(2,1)S(1)} %copy-done.32, f32[2,1,512]{2,1,0:T(1,128)S(1)} %copy-done.18, ...), custom_call_target="tpu_custom_call" | custom-call | flops 6000000000 | bytes 16000000 | tf_op jit(solution)/shard_map/prompt_query_grad/pallas_call | solution.py:969
  131.5 4.9 %collective-permute-done.18 = bf16[2,544,256]{2,1,0:T(8,128)(2,1)S(1)} collective-permute-done((bf16[2,544,256]{2,1,0:T(8,128)(2,1)S(1)}, bf16[2,544,256]{2,1,0:T(8,128)(2,1)S(1)}, u32[]{:S(2)}, u32[]{:S(2)}) %collective-permute-start.18) | collective-permute-done | bytes 557088 | tf_op jit(solution)/shard_map/ppermute | solution.py:83
  137.2 4.4 %token_query_grad.1 = (f32[512,256]{1,0:T(8,128)S(1)}, f32[8,128]{1,0:T(8,128)S(1)}) custom-call(s32[3]{0:T(128)S(1)} %copy-done.19, s32[17]{0:T(128)S(1)} %copy-done.21, bf16[2,512,256]{2,1,0:T(8,128)(2,1)S(1)} %copy-done.32, f32[2,1,512]{2,1,0:T(1,128)S(1)} %copy-done.18, f32[2,512]{1,0:T(2,128)S(1)} %get-tuple-element.126.lse_ref.lse_in, ...), custom_call_target="tpu_custom_call" | custom-call | flops 6000000000 | bytes 16000000 | tf_op jit(solution)/shard_map/token_query_grad/pallas_call | solution.py:847
  142.5 4.3 %prompt_grad_first.1 = (f32[1000,256]{1,0:T(8,128)S(1)}, f32[1000,256]{1,0:T(8,128)S(1)}, f32[8,128]{1,0:T(8,128)}) custom-call(s32[3]{0:T(128)S(1)} %copy-done.19, s32[17]{0:T(128)S(1)} %copy-done.21, s32[2,16]{1,0:T(2,128)S(1)} %copy-done.27, bf16[16,256,256]{2,1,0:T(8,128)(2,1)S(1)} %bitcast.41, f32[8,1,512]{2,1,0:T(1,128)S(1)} %maximum_convert_fusion.2.ids_ref, ...), custom_call_target="tpu_custom_call" | custom-call | flops 6000000000 | bytes 16000000 | tf_op jit(solution)/shard_map/prompt_grad_first/pallas_call | solution.py:1161
  146.8 5.9 %collective-permute-done.19.pack_ref.high_ref = bf16[4,544,256]{2,1,0:T(8,128)(2,1)S(1)} collective-permute-done((bf16[4,544,256]{2,1,0:T(8,128)(2,1)S(1)}, bf16[4,544,256]{2,1,0:T(8,128)(2,1)S(1)}, u32[]{:S(2)}, u32[]{:S(2)}) %collective-permute-start.19) | collective-permute-done | bytes 1114144 | tf_op jit(solution)/shard_map/ppermute | solution.py:83
  152.7 3.1 %prompt_grad_last.1 = (f32[1000,256]{1,0:T(8,128)S(1)}, bf16[1000,256]{1,0:T(8,128)(2,1)S(1)}) custom-call(s32[3]{0:T(128)S(1)} %copy-done.19, s32[17]{0:T(128)S(1)} %copy-done.21, s32[2,16]{1,0:T(2,128)S(1)} %copy-done.27, bf16[16,256,256]{2,1,0:T(8,128)(2,1)S(1)} %bitcast.42, f32[8,1,512]{2,1,0:T(1,128)S(1)} %maximum_convert_fusion.2.ids_ref, ...), custom_call_target="tpu_custom_call" | custom-call | flops 6000000000 | bytes 16000000 | tf_op jit(solution)/shard_map/prompt_grad_last/pallas_call | solution.py:1175
  160.2 2.7 %collective-permute-start.23 = (bf16[1000,256]{1,0:T(8,128)(2,1)S(1)}, bf16[1000,256]{1,0:T(8,128)(2,1)S(1)}, u32[]{:S(2)}, u32[]{:S(2)}) collective-permute-start(bf16[1000,256]{1,0:T(8,128)(2,1)S(1)} %reduce-precision_convert_fusion.1.a_ref), channel_id=1, source_target_pairs={{0,2},{1,3},{2,0},{3,1},{4,6},{5,7},{6,4},{7,5},{8,10},{9,11},{10,... | collective-permute-start | bytes 1536008 | tf_op jit(solution)/shard_map/ppermute | solution.py:122
  162.9 7.0 %token_grad.1 = (bf16[512,512]{1,0:T(8,128)(2,1)}, f32[8,128]{1,0:T(8,128)}) custom-call(s32[3]{0:T(128)} %pad_add_fusion.meta, s32[17]{0:T(128)} %convert_reduce_fusion.starts, bf16[16,256,256]{2,1,0:T(8,128)(2,1)} %bitcast.43, f32[8,1,512]{2,1,0:T(1,128)} %copy-done.16, bf16[4,544,256]{2,1,0:T(8,128)(2,1)} %copy-done.9, bf16[4,544,256]{2,1,0:T(8,128)(2,1)} %copy-done.23, ...), custom_call_target="tpu_custom_call" | custom-call | flops 4000000000 | bytes 16000000 | tf_op jit(solution)/shard_map/token_grad/pallas_call | solution.py:1243
  170.9 4.0 %collective-permute-done.23.b_ref = bf16[1000,256]{1,0:T(8,128)(2,1)S(1)} collective-permute-done((bf16[1000,256]{1,0:T(8,128)(2,1)S(1)}, bf16[1000,256]{1,0:T(8,128)(2,1)S(1)}, u32[]{:S(2)}, u32[]{:S(2)}) %collective-permute-start.23) | collective-permute-done | bytes 512032 | tf_op jit(solution)/shard_map/ppermute | solution.py:122
  176.3 8.5 %collective-permute-start.26 = (f32[8,128]{1,0:T(8,128)S(1)}, f32[8,128]{1,0:T(8,128)S(1)}, u32[]{:S(2)}, u32[]{:S(2)}) collective-permute-start(f32[8,128]{1,0:T(8,128)S(1)} %get-tuple-element.163), channel_id=1, source_target_pairs={{0,5},{1,4},{2,7},{3,6},{4,1},{5,0},{6,3},{7,2},{8,13},{9,12},{10,... | collective-permute-start | bytes 12296 | tf_op jit(solution)/shard_map/ppermute | solution.py:101
  186.7 1.6 collective-permute-done.25
  188.8 5.1 %collective-permute-start.29 = (f32[8,128]{1,0:T(8,128)S(1)}, f32[8,128]{1,0:T(8,128)S(1)}, u32[]{:S(2)}, u32[]{:S(2)}) collective-permute-start(f32[8,128]{1,0:T(8,128)S(1)} %add_add_fusion.1), channel_id=1, source_target_pairs={{0,16},{1,17},{2,18},{3,19},{4,20},{5,21},{6,22},{7,23},{8,24},{9,... | collective-permute-start | bytes 12296 | tf_op jit(solution)/shard_map/ppermute | solution.py:101
  197.7 4.7 %optimizer.1 = (f32[1000,512]{1,0:T(8,128)}, f32[1000,512]{1,0:T(8,128)}, f32[1000,512]{1,0:T(8,128)}, f32[1000,512]{1,0:T(8,128)}, f32[8,128]{1,0:T(8,128)S(1)}) custom-call(s32[3]{0:T(128)S(1)} %copy-done.20, f32[2]{0:T(128)S(1)} %pad_maximum_fusion.9.biases, bf16[1000,256]{1,0:T(8,128)(2,1)S(1)} %get-tuple-element.170.mine, ...), custom_call_target="tpu_custom_call" | custom-call | flops 10240000 | bytes 16384000 | tf_op jit(solution)/shard_map/optimizer/pallas_call | solution.py:1334
  (187 shorter events, 40.0 us)
Async XLA Ops:
  3.6 16.7 %collective-permute-start.1 = (bf16[1,512,256]{2,1,0:T(8,128)(2,1)S(1)}, bf16[1,512,256]{2,1,0:T(8,128)(2,1)S(1)}, u32[]{:S(2)}, u32[]{:S(2)}) collective-permute-start(bf16[1,512,256]{2,1,0:T(8,128)(2,1)S(1)} %fusion.2), channel_id=1, source_target_pairs={{0,16},{1,9},{2,18},{3,11},{4,20},{5,13},{6,22},{7,15},{8,24},{9,1... | collective-permute-start | bytes 786440 | tf_op jit(solution)/shard_map/ppermute | solution.py:83
  7.7 12.6 %collective-permute-start = (bf16[1,272,512]{2,1,0:T(8,128)(2,1)S(1)}, bf16[1,272,512]{2,1,0:T(8,128)(2,1)S(1)}, u32[]{:S(2)}, u32[]{:S(2)}) collective-permute-start(bf16[1,272,512]{2,1,0:T(8,128)(2,1)S(1)} %maximum_bitcast_fusion), channel_id=1, source_target_pairs={{0,4},{1,17},{2,6},{3,19},{4,0},{5,21},{6,2},{7,23},{8,12},{9,25},... | collective-permute-start | bytes 835592 | tf_op jit(solution)/shard_map/ppermute | solution.py:83
  9.2 17.1 %collective-permute-start.3 = (bf16[3,512,128]{2,1,0:T(8,128)(2,1)}, bf16[3,512,128]{2,1,0:T(8,128)(2,1)}, u32[]{:S(2)}, u32[]{:S(2)}) collective-permute-start(bf16[3,512,128]{2,1,0:T(8,128)(2,1)} %in_own.1), channel_id=1, source_target_pairs={{0,2},{1,3},{2,0},{3,1},{4,6},{5,7},{6,4},{7,5},{8,10},{9,11},{10,... | collective-permute-start | bytes 1179656 | tf_op jit(solution)/shard_map/ppermute | solution.py:122
  20.4 16.6 %collective-permute-start.2 = (bf16[2,272,512]{2,1,0:T(8,128)(2,1)S(1)}, bf16[2,272,512]{2,1,0:T(8,128)(2,1)}, u32[]{:S(2)}, u32[]{:S(2)}) collective-permute-start(bf16[2,272,512]{2,1,0:T(8,128)(2,1)S(1)} %pad_maximum_fusion.3), channel_id=1, source_target_pairs={{0,16},{1,9},{2,18},{3,11},{4,20},{5,13},{6,22},{7,15},{8,24},{9,1... | collective-permute-start | bytes 1671176 | tf_op jit(solution)/shard_map/ppermute | solution.py:83
  38.1 20.7 %collective-permute-start.4 = (bf16[4,272,512]{2,1,0:T(8,128)(2,1)S(1)}, bf16[4,272,512]{2,1,0:T(8,128)(2,1)S(1)}, u32[]{:S(2)}, u32[]{:S(2)}) collective-permute-start(bf16[4,272,512]{2,1,0:T(8,128)(2,1)S(1)} %pad_maximum_fusion.mine_low.a), channel_id=1, source_target_pairs={{0,8},{1,5},{2,10},{3,7},{4,12},{5,1},{6,14},{7,3},{8,0},{9,13},{1... | collective-permute-start | bytes 3342344 | tf_op jit(solution)/shard_map/ppermute | solution.py:83
  38.2 18.1 %collective-permute-start.6 = (bf16[656,512]{1,0:T(8,128)(2,1)}, bf16[656,512]{1,0:T(8,128)(2,1)}, u32[]{:S(2)}, u32[]{:S(2)}) collective-permute-start(bf16[656,512]{1,0:T(8,128)(2,1)} %fusion.1.w_own), channel_id=1, source_target_pairs={{0,2},{1,3},{2,0},{3,1},{4,6},{5,7},{6,4},{7,5},{8,10},{9,11},{10,... | collective-permute-start | bytes 2015240 | tf_op jit(solution)/shard_map/ppermute | solution.py:122
  40.4 14.9 %collective-permute-start.5 = (bf16[2,512,256]{2,1,0:T(8,128)(2,1)S(1)}, bf16[2,512,256]{2,1,0:T(8,128)(2,1)S(1)}, u32[]{:S(2)}, u32[]{:S(2)}) collective-permute-start(bf16[2,512,256]{2,1,0:T(8,128)(2,1)S(1)} %pad_maximum_fusion.5), channel_id=1, source_target_pairs={{0,4},{1,17},{2,6},{3,19},{4,0},{5,21},{6,2},{7,23},{8,12},{9,25},... | collective-permute-start | bytes 1572872 | tf_op jit(solution)/shard_map/ppermute | solution.py:83
  41.9 19.6 %collective-permute-start.7 = (bf16[4,272,512]{2,1,0:T(8,128)(2,1)S(1)}, bf16[4,272,512]{2,1,0:T(8,128)(2,1)S(1)}, u32[]{:S(2)}, u32[]{:S(2)}) collective-permute-start(bf16[4,272,512]{2,1,0:T(8,128)(2,1)S(1)} %pad_maximum_fusion.mine_low.a), channel_id=1, source_target_pairs={{0,1},{1,0},{2,3},{3,2},{4,5},{5,4},{6,7},{7,6},{8,9},{9,8},{10,11... | collective-permute-start | bytes 3342344 | tf_op jit(solution)/shard_map/ppermute | solution.py:122
  58.9 4.4 %collective-permute-start.8 = (bf16[4,272,512]{2,1,0:T(8,128)(2,1)S(1)}, bf16[4,272,512]{2,1,0:T(8,128)(2,1)}, u32[]{:S(2)}, u32[]{:S(2)}) collective-permute-start(bf16[4,272,512]{2,1,0:T(8,128)(2,1)S(1)} %collective-permute-done.4.mine_high.c), channel_id=1, source_target_pairs={{0,1},{1,0},{2,3},{3,2},{4,5},{5,4},{6,7},{7,6},{8,9},{9,8},{10,11... | collective-permute-start | bytes 3342344 | tf_op jit(solution)/shard_map/ppermute | solution.py:122
  58.9 12.2 %collective-permute-start.10 = (bf16[4,512,256]{2,1,0:T(8,128)(2,1)}, bf16[4,512,256]{2,1,0:T(8,128)(2,1)}, u32[]{:S(2)}, u32[]{:S(2)}) collective-permute-start(bf16[4,512,256]{2,1,0:T(8,128)(2,1)} %pad_maximum_fusion.2.mine_low), channel_id=1, source_target_pairs={{0,1},{1,0},{2,3},{3,2},{4,5},{5,4},{6,7},{7,6},{8,9},{9,8},{10,11... | collective-permute-start | bytes 3145736 | tf_op jit(solution)/shard_map/ppermute | solution.py:122
  59.4 15.1 %collective-permute-start.9 = (bf16[4,512,256]{2,1,0:T(8,128)(2,1)}, bf16[4,512,256]{2,1,0:T(8,128)(2,1)}, u32[]{:S(2)}, u32[]{:S(2)}) collective-permute-start(bf16[4,512,256]{2,1,0:T(8,128)(2,1)} %pad_maximum_fusion.2.mine_low), channel_id=1, source_target_pairs={{0,8},{1,5},{2,10},{3,7},{4,12},{5,1},{6,14},{7,3},{8,0},{9,13},{1... | collective-permute-start | bytes 3145736 | tf_op jit(solution)/shard_map/ppermute | solution.py:83
  59.7 11.3 %collective-permute-start.11 = (bf16[656,512]{1,0:T(8,128)(2,1)}, bf16[656,512]{1,0:T(8,128)(2,1)}, u32[]{:S(2)}, u32[]{:S(2)}) collective-permute-start(bf16[656,512]{1,0:T(8,128)(2,1)} %fusion.1.w_own), channel_id=1, source_target_pairs={{0,1},{1,0},{2,3},{3,2},{4,5},{5,4},{6,7},{7,6},{8,9},{9,8},{10,11... | collective-permute-start | bytes 2015240 | tf_op jit(solution)/shard_map/ppermute | solution.py:122
  61.5 9.5 %collective-permute-start.12 = (bf16[656,512]{1,0:T(8,128)(2,1)}, bf16[656,512]{1,0:T(8,128)(2,1)}, u32[]{:S(2)}, u32[]{:S(2)}) collective-permute-start(bf16[656,512]{1,0:T(8,128)(2,1)} %collective-permute-done.6.w_along), channel_id=1, source_target_pairs={{0,1},{1,0},{2,3},{3,2},{4,5},{5,4},{6,7},{7,6},{8,9},{9,8},{10,11... | collective-permute-start | bytes 2015240 | tf_op jit(solution)/shard_map/ppermute | solution.py:122
  74.6 3.1 %collective-permute-start.13 = (bf16[4,512,256]{2,1,0:T(8,128)(2,1)}, bf16[4,512,256]{2,1,0:T(8,128)(2,1)}, u32[]{:S(2)}, u32[]{:S(2)}) collective-permute-start(bf16[4,512,256]{2,1,0:T(8,128)(2,1)} %collective-permute-done.9.mine_high), channel_id=1, source_target_pairs={{0,1},{1,0},{2,3},{3,2},{4,5},{5,4},{6,7},{7,6},{8,9},{9,8},{10,11... | collective-permute-start | bytes 3145736 | tf_op jit(solution)/shard_map/ppermute | solution.py:122
  91.0 8.6 %collective-permute-start.14 = (bf16[528,256]{1,0:T(8,128)(2,1)S(1)}, bf16[528,256]{1,0:T(8,128)(2,1)S(1)}, u32[]{:S(2)}, u32[]{:S(2)}) collective-permute-start(bf16[528,256]{1,0:T(8,128)(2,1)S(1)} %get-tuple-element.121), channel_id=1, source_target_pairs={{0,2},{1,3},{2,0},{3,1},{4,6},{5,7},{6,4},{7,5},{8,10},{9,11},{10,... | collective-permute-start | bytes 811016 | tf_op jit(solution)/shard_map/ppermute | solution.py:122
  110.5 6.5 %collective-permute-start.16 = (bf16[1,544,256]{2,1,0:T(8,128)(2,1)S(1)}, bf16[1,544,256]{2,1,0:T(8,128)(2,1)S(1)}, u32[]{:S(2)}, u32[]{:S(2)}) collective-permute-start(bf16[1,544,256]{2,1,0:T(8,128)(2,1)S(1)} %bitcast.39), channel_id=1, source_target_pairs={{0,4},{1,17},{2,6},{3,19},{4,0},{5,21},{6,2},{7,23},{8,12},{9,25},... | collective-permute-start | bytes 835592 | tf_op jit(solution)/shard_map/ppermute | solution.py:83
  110.6 9.6 %collective-permute-start.17 = (bf16[544,256]{1,0:T(8,128)(2,1)S(1)}, bf16[544,256]{1,0:T(8,128)(2,1)S(1)}, u32[]{:S(2)}, u32[]{:S(2)}) collective-permute-start(bf16[544,256]{1,0:T(8,128)(2,1)S(1)} %get-tuple-element.131.pack_own.do_ref), channel_id=1, source_target_pairs={{0,2},{1,3},{2,0},{3,1},{4,6},{5,7},{6,4},{7,5},{8,10},{9,11},{10,... | collective-permute-start | bytes 835592 | tf_op jit(solution)/shard_map/ppermute | solution.py:122
  112.4 34.4 %collective-permute-start.21 = (bf16[256,512]{1,0:T(8,128)(2,1)S(1)}, bf16[256,512]{1,0:T(8,128)(2,1)S(1)}, u32[]{:S(2)}, u32[]{:S(2)}) collective-permute-start(bf16[256,512]{1,0:T(8,128)(2,1)S(1)} %constant_dynamic-slice_fusion.1), channel_id=1, source_target_pairs={{0,2},{1,3},{2,0},{3,1},{4,6},{5,7},{6,4},{7,5},{8,10},{9,11},{10,... | collective-permute-start | bytes 786440 | tf_op jit(solution)/shard_map/ppermute | solution.py:122
  120.1 16.2 %collective-permute-start.18 = (bf16[2,544,256]{2,1,0:T(8,128)(2,1)S(1)}, bf16[2,544,256]{2,1,0:T(8,128)(2,1)S(1)}, u32[]{:S(2)}, u32[]{:S(2)}) collective-permute-start(bf16[2,544,256]{2,1,0:T(8,128)(2,1)S(1)} %pad_maximum_fusion.4), channel_id=1, source_target_pairs={{0,16},{1,9},{2,18},{3,11},{4,20},{5,13},{6,22},{7,15},{8,24},{9,1... | collective-permute-start | bytes 1671176 | tf_op jit(solution)/shard_map/ppermute | solution.py:83
  136.5 10.3 %collective-permute-start.20 = (bf16[512,256]{1,0:T(8,128)(2,1)S(1)}, bf16[512,256]{1,0:T(8,128)(2,1)S(1)}, u32[]{:S(2)}, u32[]{:S(2)}) collective-permute-start(bf16[512,256]{1,0:T(8,128)(2,1)S(1)} %get-tuple-element.143), channel_id=1, source_target_pairs={{0,2},{1,3},{2,0},{3,1},{4,6},{5,7},{6,4},{7,5},{8,10},{9,11},{10,... | collective-permute-start | bytes 786440 | tf_op jit(solution)/shard_map/ppermute | solution.py:122
  137.2 15.5 %collective-permute-start.19 = (bf16[4,544,256]{2,1,0:T(8,128)(2,1)S(1)}, bf16[4,544,256]{2,1,0:T(8,128)(2,1)S(1)}, u32[]{:S(2)}, u32[]{:S(2)}) collective-permute-start(bf16[4,544,256]{2,1,0:T(8,128)(2,1)S(1)} %pad_maximum_fusion.1.pack_ref.low_ref), channel_id=1, source_target_pairs={{0,8},{1,5},{2,10},{3,7},{4,12},{5,1},{6,14},{7,3},{8,0},{9,13},{1... | collective-permute-start | bytes 3342344 | tf_op jit(solution)/shard_map/ppermute | solution.py:83
  156.8 13.2 %collective-permute-start.31 = (bf16[256,512]{1,0:T(8,128)(2,1)S(1)}, bf16[256,512]{1,0:T(8,128)(2,1)}, u32[]{:S(2)}, u32[]{:S(2)}) collective-permute-start(bf16[256,512]{1,0:T(8,128)(2,1)S(1)} %collective-permute-done.21), channel_id=1, source_target_pairs={{0,1},{1,0},{2,3},{3,2},{4,5},{5,4},{6,7},{7,6},{8,9},{9,8},{10,11... | collective-permute-start | bytes 786440 | tf_op jit(solution)/shard_map/ppermute | solution.py:122
  160.2 14.7 %collective-permute-start.23 = (bf16[1000,256]{1,0:T(8,128)(2,1)S(1)}, bf16[1000,256]{1,0:T(8,128)(2,1)S(1)}, u32[]{:S(2)}, u32[]{:S(2)}) collective-permute-start(bf16[1000,256]{1,0:T(8,128)(2,1)S(1)} %reduce-precision_convert_fusion.1.a_ref), channel_id=1, source_target_pairs={{0,2},{1,3},{2,0},{3,1},{4,6},{5,7},{6,4},{7,5},{8,10},{9,11},{10,... | collective-permute-start | bytes 1536008 | tf_op jit(solution)/shard_map/ppermute | solution.py:122
  169.9 18.5 %collective-permute-start.27 = (bf16[512,512]{1,0:T(8,128)(2,1)}, bf16[512,512]{1,0:T(8,128)(2,1)S(1)}, u32[]{:S(2)}, u32[]{:S(2)}) collective-permute-start(bf16[512,512]{1,0:T(8,128)(2,1)} %get-tuple-element.165), channel_id=1, source_target_pairs={{0,1},{1,0},{2,3},{3,2},{4,5},{5,4},{6,7},{7,6},{8,9},{9,8},{10,11... | collective-permute-start | bytes 1572872 | tf_op jit(solution)/shard_map/ppermute | solution.py:122
  176.3 10.5 %collective-permute-start.26 = (f32[8,128]{1,0:T(8,128)S(1)}, f32[8,128]{1,0:T(8,128)S(1)}, u32[]{:S(2)}, u32[]{:S(2)}) collective-permute-start(f32[8,128]{1,0:T(8,128)S(1)} %get-tuple-element.163), channel_id=1, source_target_pairs={{0,5},{1,4},{2,7},{3,6},{4,1},{5,0},{6,3},{7,2},{8,13},{9,12},{10,... | collective-permute-start | bytes 12296 | tf_op jit(solution)/shard_map/ppermute | solution.py:101
  184.8 3.6 %collective-permute-start.25 = (f32[8,128]{1,0:T(8,128)S(1)}, f32[8,128]{1,0:T(8,128)S(1)}, u32[]{:S(2)}, u32[]{:S(2)}) collective-permute-start(f32[8,128]{1,0:T(8,128)S(1)} %get-tuple-element.163), channel_id=1, source_target_pairs={{0,4},{1,5},{2,6},{3,7},{4,0},{5,1},{6,2},{7,3},{8,12},{9,13},{10,... | collective-permute-start | bytes 12296 | tf_op jit(solution)/shard_map/ppermute | solution.py:101
  186.0 2.4 %collective-permute-start.24 = (f32[8,128]{1,0:T(8,128)S(1)}, f32[8,128]{1,0:T(8,128)S(1)}, u32[]{:S(2)}, u32[]{:S(2)}) collective-permute-start(f32[8,128]{1,0:T(8,128)S(1)} %get-tuple-element.163), channel_id=1, source_target_pairs={{0,1},{1,0},{2,3},{3,2},{4,5},{5,4},{6,7},{7,6},{8,9},{9,8},{10,11... | collective-permute-start | bytes 12296 | tf_op jit(solution)/shard_map/ppermute | solution.py:101
  186.2 11.2 %collective-permute-start.33 = (bf16[1000,256]{1,0:T(8,128)(2,1)S(1)}, bf16[1000,256]{1,0:T(8,128)(2,1)S(1)}, u32[]{:S(2)}, u32[]{:S(2)}) collective-permute-start(bf16[1000,256]{1,0:T(8,128)(2,1)S(1)} %get-tuple-element.170.mine), channel_id=1, source_target_pairs={{0,1},{1,0},{2,3},{3,2},{4,5},{5,4},{6,7},{7,6},{8,9},{9,8},{10,11... | collective-permute-start | bytes 1536008 | tf_op jit(solution)/shard_map/ppermute | solution.py:122
  188.7 8.1 %collective-permute-start.30 = (f32[8,128]{1,0:T(8,128)S(1)}, f32[8,128]{1,0:T(8,128)S(1)}, u32[]{:S(2)}, u32[]{:S(2)}) collective-permute-start(f32[8,128]{1,0:T(8,128)S(1)} %add_add_fusion.1), channel_id=1, source_target_pairs={{0,24},{1,25},{2,26},{3,27},{4,28},{5,29},{6,30},{7,31},{8,16},{9,... | collective-permute-start | bytes 12296 | tf_op jit(solution)/shard_map/ppermute | solution.py:101
  188.8 8.1 %collective-permute-start.29 = (f32[8,128]{1,0:T(8,128)S(1)}, f32[8,128]{1,0:T(8,128)S(1)}, u32[]{:S(2)}, u32[]{:S(2)}) collective-permute-start(f32[8,128]{1,0:T(8,128)S(1)} %add_add_fusion.1), channel_id=1, source_target_pairs={{0,16},{1,17},{2,18},{3,19},{4,20},{5,21},{6,22},{7,23},{8,24},{9,... | collective-permute-start | bytes 12296 | tf_op jit(solution)/shard_map/ppermute | solution.py:101
  193.8 3.6 %collective-permute-start.28 = (f32[8,128]{1,0:T(8,128)S(1)}, f32[8,128]{1,0:T(8,128)S(1)}, u32[]{:S(2)}, u32[]{:S(2)}) collective-permute-start(f32[8,128]{1,0:T(8,128)S(1)} %add_add_fusion.1), channel_id=1, source_target_pairs={{0,8},{1,9},{2,10},{3,11},{4,12},{5,13},{6,14},{7,15},{8,0},{9,1},... | collective-permute-start | bytes 12296 | tf_op jit(solution)/shard_map/ppermute | solution.py:101
  193.9 8.5 %collective-permute-start.32 = (bf16[256,512]{1,0:T(8,128)(2,1)S(1)}, bf16[256,512]{1,0:T(8,128)(2,1)S(1)}, u32[]{:S(2)}, u32[]{:S(2)}) collective-permute-start(bf16[256,512]{1,0:T(8,128)(2,1)S(1)} %constant_dynamic-slice_fusion), channel_id=1, source_target_pairs={{0,2},{1,3},{2,0},{3,1},{4,6},{5,7},{6,4},{7,5},{8,10},{9,11},{10,... | collective-permute-start | bytes 786440 | tf_op jit(solution)/shard_map/ppermute | solution.py:122
  (48 other events, 392.2 us)
